TPU v7x, 32 devices: a whole 2x2x4 slice. The times are simulated.
32 devices in a mesh: mom: 2 (over x), en: 16 (over z, y, core).
Axes of the slice: x: 2, y: 2, z: 4, core: 2. Of those that a mesh axis runs over, the one named last changes fastest.
Arguments:
- green0: bfloat16 [2, 64, 2, 512, 512], P('mom', 'en'), may hold values from -6 to 6
- phonon_me: bfloat16 [512, 512], replicated, may hold values from 0.25 to 4
- coupling: float32 [2, 2, 16], replicated, may hold values from 0.0015 to 0.045
- shift_table: int32 [2, 16], replicated, may hold values from 0 to 1
- offsets: int32 [16], replicated, may hold values from 1 to 8
Outputs:
- green: bfloat16 [2, 64, 2, 512, 512], P('mom', 'en')
All inputs are finite; a program needn't handle non-finite values.
Results may differ from a plain program's by a relative error of at most 0.02.
Values may be sent and summed in bfloat16 or wider, within the bound.
No kernel may reach another device: no remote copies, remote signals or barrier semaphores. Data moves between devices by JAX's collectives and lax.ppermute only.
A program may use at most 128 MiB of HBM per device.

v0:
```python
import jax
import jax.numpy as jnp
from jax import lax
from jax.sharding import PartitionSpec as P

NEUMANN = 3


def kernel_table(shift_table, coupling, offsets, mom_count, energies):
    energy = jnp.arange(energies, dtype=jnp.int32)
    offset_grid = energy[:, None] - energy[None, :]
    downward = (offset_grid[None, :, :] == offsets[:, None, None]).astype(jnp.float32)
    upward = (offset_grid[None, :, :] == -offsets[:, None, None]).astype(jnp.float32)
    moment = jnp.arange(mom_count, dtype=jnp.int32)
    select = (shift_table[:, :, None] == moment[None, None, :]).astype(jnp.float32)
    emission = jnp.einsum("awb,aw->abw", select, coupling[0])
    absorption = jnp.einsum("awb,aw->abw", select, coupling[1])
    kernel = jnp.einsum("abw,wef->abef", emission, downward) + jnp.einsum(
        "abw,wef->abef", absorption, upward
    )
    return kernel.astype(jnp.bfloat16)


def per_device(green0, phonon_me, coupling, shift_table, offsets):
    mom_count = lax.axis_size("mom")
    en_count = lax.axis_size("en")
    local_energies = green0.shape[1]
    orbitals = green0.shape[3]
    energies = local_energies * en_count
    local_green = green0[0]
    kernel = kernel_table(shift_table, coupling, offsets, mom_count, energies)
    tile_count = mom_count * en_count
    tile_rows = orbitals // tile_count
    spread = local_green.reshape(1, local_energies, 2, tile_count, tile_rows, orbitals)
    columns = lax.all_to_all(spread, ("mom", "en"), split_axis=3, concat_axis=0, tiled=True)
    column_count = columns.shape[-1]
    flattened = columns.reshape(mom_count, energies, 2 * tile_rows * column_count)
    summed = jnp.einsum("abef,bfx->aex", kernel, flattened, preferred_element_type=jnp.float32)
    smooth = summed.astype(jnp.bfloat16).reshape(
        tile_count, local_energies, 2, 1, tile_rows, column_count
    )
    returned = lax.all_to_all(smooth, ("mom", "en"), split_axis=0, concat_axis=3, tiled=True)
    smooth_all = returned.reshape(local_energies, 2, orbitals, column_count)
    scale = 1.0 / orbitals
    self_energy = (
        phonon_me.astype(jnp.float32)[None, None] * smooth_all.astype(jnp.float32)
    ).astype(jnp.bfloat16)
    left_factor = jnp.concatenate([local_green[:, 0], local_green[:, 1]], axis=2)
    right_real = jnp.concatenate([self_energy[:, 0], -self_energy[:, 1]], axis=1)
    right_imag = jnp.concatenate([self_energy[:, 1], self_energy[:, 0]], axis=1)
    prod_real = (
        jnp.einsum("eij,ejk->eik", left_factor, right_real, preferred_element_type=jnp.float32)
        * scale
    ).astype(jnp.bfloat16)
    prod_imag = (
        jnp.einsum("eij,ejk->eik", left_factor, right_imag, preferred_element_type=jnp.float32)
        * scale
    ).astype(jnp.bfloat16)
    transfer = jnp.concatenate([prod_real, prod_imag], axis=2)
    current_real = local_green[:, 0]
    current_imag = local_green[:, 1]
    for iteration in range(NEUMANN):
        stacked_real = jnp.concatenate([current_real, -current_imag], axis=1)
        stacked_imag = jnp.concatenate([current_imag, current_real], axis=1)
        new_real = local_green[:, 0].astype(jnp.float32) + jnp.einsum(
            "eij,ejk->eik", transfer, stacked_real, preferred_element_type=jnp.float32
        )
        new_imag = local_green[:, 1].astype(jnp.float32) + jnp.einsum(
            "eij,ejk->eik", transfer, stacked_imag, preferred_element_type=jnp.float32
        )
        current_real = new_real.astype(jnp.bfloat16)
        current_imag = new_imag.astype(jnp.bfloat16)
    return jnp.stack([current_real, current_imag], axis=1)[None]


def solution(mesh):
    in_specs = (P("mom", "en", None, None, None), P(), P(), P(), P())
    out_specs = P("mom", "en", None, None, None)
    return jax.shard_map(
        per_device, mesh=mesh, in_specs=in_specs, out_specs=out_specs, check_vma=False
    )
```

profile of v0, /device:TPU:0, one launch (start us, length us, event | category | flops | bytes accessed | tf_op | source)
XLA Modules:
  0.0 283.2 jit_solution(13912337403849061613)
XLA Ops:
  0.0 4.8 %copy.44 = bf16[1,4,2,32,16,512]{5,4,2,1,0,3:T(8,128)(2,1)} copy(bf16[1,4,2,32,16,512]{5,4,3,2,1,0:T(8,128)(2,1)} %bitcast.87) | data formatting | bytes 8388608 | tf_op jit(solution)/shard_map/reshape;squeeze | solution.py:34
  4.8 0.0 copy-start.5
  4.9 0.0 copy-start.6
  4.9 7.4 %all-to-all-start = ((bf16[1,4,2,32,16,512]{5,4,2,1,0,3:T(8,128)(2,1)}), bf16[1,4,2,32,16,512]{5,4,2,1,0,3:T(8,128)(2,1)}, u32[]{:S(2)}, u32[]{:S(2)}) async-start(bf16[1,4,2,32,16,512]{5,4,2,1,0,3:T(8,128)(2,1)} %copy.44), calls=%async_computation | async-start | bytes 8388608 | tf_op jit(solution)/shard_map/all_to_all | solution.py:35
  12.3 0.0 copy-done.7
  12.3 0.0 copy-done.5
  12.3 0.0 copy-done.6
  12.4 0.3 fusion.59
  12.6 0.3 fusion.57
  12.9 94.1 %all-to-all-done = bf16[1,4,2,32,16,512]{5,4,2,1,0,3:T(8,128)(2,1)} async-done(((bf16[1,4,2,32,16,512]{5,4,2,1,0,3:T(8,128)(2,1)}), bf16[1,4,2,32,16,512]{5,4,2,1,0,3:T(8,128)(2,1)}, u32[]{:S(2)}, u32[]{:S(2)}) %all-to-all-start) | async-done | bytes 4194336 | tf_op jit(solution)/shard_map/all_to_all | solution.py:35
  106.9 7.4 %reshape.38 = bf16[2,64,16384,1]{2,1,0,3:T(8,128)(2,1)} reshape(bf16[32,1,4,2,1,16,512]{6,5,3,2,0,4,1:T(8,128)(2,1)} %bitcast.15) | data formatting | bytes 8388608 | tf_op jit(solution)/shard_map/reshape | solution.py:37
  114.3 3.5 %fusion = bf16[2,64,16384]{2,1,0:T(8,128)(2,1)S(1)} fusion(bf16[2,64,16384,1]{2,1,0,3:T(8,128)(2,1)} %reshape.38, bf16[2,2,64,64]{3,1,2,0:T(2,128)(2,1)S(1)} %fusion.57), kind=kOutput, calls=%fused_computation.1 | convolution fusion | flops 538968064 | bytes 8421376 | tf_op jit(solution)/shard_map/abef,bfx->aex/dot_general | solution.py:38
  117.8 3.7 %copy.65 = bf16[16,8,32,512]{3,2,1,0:T(8,128)(2,1)} copy(bf16[16,8,32,512]{3,1,2,0:T(8,128)(2,1)S(1)} %bitcast.89) | data formatting | bytes 8388608
  121.5 3.8 %all-to-all-start.1 = ((bf16[32,4,2,1,16,512]{5,4,2,1,3,0:T(8,128)(2,1)}), bf16[32,4,2,1,16,512]{5,4,2,1,3,0:T(8,128)(2,1)}, u32[]{:S(2)}, u32[]{:S(2)}) async-start(bf16[32,4,2,1,16,512]{5,4,2,1,3,0:T(8,128)(2,1)} %bitcast.88), calls=%async_computation.1 | async-start | bytes 8388608 | tf_op jit(solution)/shard_map/all_to_all | solution.py:42
  125.2 0.0 copy-start.4
  125.2 4.5 %copy.70 = bf16[1,4,2,512,512]{4,3,1,2,0:T(8,128)(2,1)} copy(bf16[1,4,2,512,512]{4,3,2,1,0:T(8,128)(2,1)} %param.5) | data formatting | bytes 8388608 | tf_op args[0]
  129.8 0.0 copy-done.4
  129.8 0.2 copy.43
  130.0 0.0 copy-start
  130.0 1.9 fusion.89
  131.9 0.9 copy-done
  132.8 2.2 slice_bitcast_fusion.3
  135.0 84.7 %all-to-all-done.1 = bf16[32,4,2,1,16,512]{5,4,2,1,3,0:T(8,128)(2,1)} async-done(((bf16[32,4,2,1,16,512]{5,4,2,1,3,0:T(8,128)(2,1)}), bf16[32,4,2,1,16,512]{5,4,2,1,3,0:T(8,128)(2,1)}, u32[]{:S(2)}, u32[]{:S(2)}) %all-to-all-start.1) | async-done | bytes 4194336 | tf_op jit(solution)/shard_map/all_to_all | solution.py:42
  219.8 6.6 %bitcast_convert_fusion = f32[32,1,4,2,1,16,512]{6,5,0,3,2,4,1:T(8,128)} fusion(bf16[32,4,2,1,16,512]{5,4,2,1,3,0:T(8,128)(2,1)} %all-to-all-done.1), kind=kLoop, calls=%fused_computation.50 | loop fusion | flops 2097152 | bytes 12582912 | tf_op jit(solution)/shard_map/convert_element_type | solution.py:46
  226.4 9.9 %copy.48 = f32[4,2,512,512]{2,3,0,1:T(8,128)} copy(f32[4,2,512,512]{3,2,1,0:T(8,128)} %bitcast.80) | data formatting | bytes 16777216 | tf_op jit(solution)/shard_map/convert_element_type | solution.py:46
  236.3 4.7 %multiply_convert_fusion = bf16[4,2,512,512]{2,3,0,1:T(8,128)(2,1)S(1)} fusion(f32[4,2,512,512]{2,3,0,1:T(8,128)} %copy.48, f32[512,512]{0,1:T(8,128)S(1)} %copy.43), kind=kLoop, calls=%fused_computation.2 | loop fusion | flops 4194304 | bytes 13631488 | tf_op jit(solution)/shard_map/convert_element_type | solution.py:47
  241.0 0.1 fusion.88
  241.2 0.0 copy-start.2
  241.2 0.0 copy-start.3
  241.2 0.5 slice_bitcast_fusion
  241.6 1.1 copy-done.2
  242.8 0.6 copy-done.3
  243.4 3.5 %multiply_convert_fusion.1 = bf16[4,512,512]{1,2,0:T(8,128)(2,1)} fusion(bf16[4,512,512]{1,2,0:T(8,128)(2,1)S(1)} %get-tuple-element.6, bf16[4,512,512]{1,2,0:T(8,128)(2,1)S(1)} %get-tuple-element.5, bf16[4,512,512]{2,1,0:T(8,128)(2,1)S(1)} %copy-done.3, bf16[4,512,512]{2,1,0:T(8,128)(2,1)S(1)} %copy-done.2), kind=kOutput, calls=%fused_computation.52 | convolution fusion | flops 2166358016 | bytes 10485760 | tf_op jit(solution)/shard_map/eij,ejk->eik/dot_general | solution.py:56
  246.9 3.5 %multiply_convert_fusion.2 = bf16[4,512,512]{1,2,0:T(8,128)(2,1)} fusion(bf16[4,512,512]{1,2,0:T(8,128)(2,1)S(1)} %fusion.88, bf16[4,512,512]{1,2,0:T(8,128)(2,1)S(1)} %get-tuple-element.6, bf16[4,512,512]{2,1,0:T(8,128)(2,1)S(1)} %copy-done.3, bf16[4,512,512]{2,1,0:T(8,128)(2,1)S(1)} %copy-done.2), kind=kOutput, calls=%fused_computation.53 | convolution fusion | flops 2166358016 | bytes 10485760 | tf_op jit(solution)/shard_map/eij,ejk->eik/dot_general | solution.py:52
  250.5 0.0 copy-done.8
  250.5 6.3 %fusion.90 = (bf16[4,512,512]{2,1,0:T(8,128)(2,1)}, bf16[4,512,512]{2,1,0:T(8,128)(2,1)}) fusion(bf16[4,512,512]{2,1,0:T(8,128)(2,1)S(1)} %copy-done.2, bf16[4,512,512]{2,1,0:T(8,128)(2,1)S(1)} %copy-done.3, bf16[4,512,512]{1,2,0:T(8,128)(2,1)S(1)} %copy-done.8, bf16[4,512,512]{1,2,0:T(8,128)(2,1)} %multiply_convert_fusion.2), kind=kOutput, calls=%fused_computation.98 | convolution fusion | flops 2168455168 | bytes 12582912 | tf_op jit(solution)/shard_map/eij,ejk->eik/dot_general | solution.py:68
  256.8 0.0 copy-done.9
  256.8 3.7 %fusion.1 = bf16[4,512,512]{2,1,0:T(8,128)(2,1)} fusion(bf16[4,512,512]{2,1,0:T(8,128)(2,1)S(1)} %copy-done.2, bf16[4,512,512]{2,1,0:T(8,128)(2,1)S(1)} %fusion.89, bf16[4,512,512]{1,2,0:T(8,128)(2,1)S(1)} %copy-done.8, bf16[4,512,512]{1,2,0:T(8,128)(2,1)S(1)} %copy-done.9), kind=kOutput, calls=%fused_computation.9 | convolution fusion | flops 2167406592 | bytes 10485760 | tf_op jit(solution)/shard_map/eij,ejk->eik/dot_general | solution.py:65
  260.5 0.0 copy-done.1
  260.5 6.1 %fusion.2 = bf16[4,512,512]{2,1,0:T(8,128)(2,1)} fusion(bf16[4,512,512]{2,1,0:T(8,128)(2,1)} %get-tuple-element.11, bf16[4,512,512]{2,1,0:T(8,128)(2,1)} %fusion.1, bf16[4,2,512,512]{3,2,0,1:T(8,128)(2,1)S(1)} %bitcast.83, bf16[4,512,512]{1,2,0:T(8,128)(2,1)S(1)} %copy-done.8, bf16[4,512,512]{1,2,0:T(8,128)(2,1)S(1)} %copy-done.9), kind=kOutput, calls=%fused_computation.10 | convolution fusion | flops 2167406592 | bytes 12582912 | tf_op jit(solution)/shard_map/eij,ejk->eik/dot_general | solution.py:65
  266.6 0.0 copy-done.11
  266.6 0.0 copy-done.12
  266.6 4.3 %fusion.91 = (bf16[4,512,512]{2,1,0:T(8,128)(2,1)}, bf16[4,512,512]{2,1,0:T(8,128)(2,1)}) fusion(bf16[4,512,512]{2,1,0:T(8,128)(2,1)S(1)} %copy-done.12, bf16[4,512,512]{2,1,0:T(8,128)(2,1)S(1)} %copy-done.11, bf16[4,512,512]{1,2,0:T(8,128)(2,1)S(1)} %copy-done.8, bf16[4,512,512]{1,2,0:T(8,128)(2,1)S(1)} %copy-done.9, bf16[4,2,512,512]{3,2,0,1:T(8,128)(2,1)S(1)} %bitcast.84), kind=kOutput, calls=%fused_computation.99 | convolution fusion | flops 2168455168 | bytes 14680064 | tf_op jit(solution)/shard_map/eij,ejk->eik/dot_general | solution.py:68
  270.9 4.8 %fusion.40 = bf16[4,1,512,512]{3,2,0,1:T(8,128)(2,1)S(1)} fusion(bf16[4,512,512]{2,1,0:T(8,128)(2,1)} %get-tuple-element.13, bf16[4,512,512]{2,1,0:T(8,128)(2,1)} %fusion.2, bf16[4,2,512,512]{3,2,0,1:T(8,128)(2,1)S(1)} %bitcast.85, bf16[4,512,512]{1,2,0:T(8,128)(2,1)S(1)} %copy-done.8, bf16[4,512,512]{1,2,0:T(8,128)(2,1)S(1)} %copy-done.9), kind=kOutput, calls=%fused_computation.55 | convolution fusion | flops 2167406592 | bytes 12582912 | tf_op jit(solution)/shard_map/eij,ejk->eik/dot_general | solution.py:65
  275.7 0.0 copy-done.10
  275.7 4.7 %fusion.39 = bf16[4,1,512,512]{3,2,0,1:T(8,128)(2,1)S(1)} fusion(bf16[4,512,512]{2,1,0:T(8,128)(2,1)} %fusion.2, bf16[4,512,512]{2,1,0:T(8,128)(2,1)} %get-tuple-element.14, bf16[4,2,512,512]{3,2,0,1:T(8,128)(2,1)S(1)} %bitcast.86, bf16[4,512,512]{1,2,0:T(8,128)(2,1)S(1)} %copy-done.8, bf16[4,512,512]{1,2,0:T(8,128)(2,1)S(1)} %copy-done.10), kind=kOutput, calls=%fused_computation.54 | convolution fusion | flops 2167406592 | bytes 12582912 | tf_op jit(solution)/shard_map/eij,ejk->eik/dot_general | solution.py:68
  280.4 0.4 maximum_bitcast_fusion
  280.8 2.5 copy.55
  (10 shorter events, 0.0 us)
Async XLA Ops:
  4.8 7.4 %copy-start.7 = (s32[16]{0:T(128)S(1)}, s32[16]{0:T(128)}, u32[]{:S(2)}) copy-start(s32[16]{0:T(128)} %param.9) | copy-start | bytes 196
  4.8 7.5 %copy-start.5 = (f32[2,2,16]{2,1,0:T(2,128)S(1)}, f32[2,2,16]{2,1,0:T(2,128)}, u32[]{:S(2)}) copy-start(f32[2,2,16]{2,1,0:T(2,128)} %param.7) | copy-start | bytes 772
  4.9 7.5 %copy-start.6 = (s32[2,16]{1,0:T(2,128)S(1)}, s32[2,16]{1,0:T(2,128)}, u32[]{:S(2)}) copy-start(s32[2,16]{1,0:T(2,128)} %param.8) | copy-start | bytes 388
  4.9 102.1 %all-to-all-start = ((bf16[1,4,2,32,16,512]{5,4,2,1,0,3:T(8,128)(2,1)}), bf16[1,4,2,32,16,512]{5,4,2,1,0,3:T(8,128)(2,1)}, u32[]{:S(2)}, u32[]{:S(2)}) async-start(bf16[1,4,2,32,16,512]{5,4,2,1,0,3:T(8,128)(2,1)} %copy.44), calls=%async_computation | async-start | bytes 8388608 | tf_op jit(solution)/shard_map/all_to_all | solution.py:35
  121.5 98.3 %all-to-all-start.1 = ((bf16[32,4,2,1,16,512]{5,4,2,1,3,0:T(8,128)(2,1)}), bf16[32,4,2,1,16,512]{5,4,2,1,3,0:T(8,128)(2,1)}, u32[]{:S(2)}, u32[]{:S(2)}) async-start(bf16[32,4,2,1,16,512]{5,4,2,1,3,0:T(8,128)(2,1)} %bitcast.88), calls=%async_computation.1 | async-start | bytes 8388608 | tf_op jit(solution)/shard_map/all_to_all | solution.py:42
  125.2 4.5 %copy-start.4 = (bf16[512,512]{1,0:T(8,128)(2,1)S(1)}, bf16[512,512]{1,0:T(8,128)(2,1)}, u32[]{:S(2)}) copy-start(bf16[512,512]{1,0:T(8,128)(2,1)} %param.6) | copy-start | bytes 1572868
  130.0 2.8 copy-start
  241.2 1.6 copy-start.2
  241.2 2.2 copy-start.3
  246.9 3.6 %copy-start.8 = (bf16[4,512,512]{1,2,0:T(8,128)(2,1)S(1)}, bf16[4,512,512]{1,2,0:T(8,128)(2,1)}, u32[]{:S(2)}) copy-start(bf16[4,512,512]{1,2,0:T(8,128)(2,1)} %multiply_convert_fusion.1) | copy-start | bytes 6291460
  250.5 6.3 %copy-start.9 = (bf16[4,512,512]{1,2,0:T(8,128)(2,1)S(1)}, bf16[4,512,512]{1,2,0:T(8,128)(2,1)}, u32[]{:S(2)}) copy-start(bf16[4,512,512]{1,2,0:T(8,128)(2,1)} %multiply_convert_fusion.2) | copy-start | bytes 6291460
  256.8 3.7 %copy-start.1 = (bf16[1,4,2,512,512]{4,3,1,2,0:T(8,128)(2,1)S(1)}, bf16[1,4,2,512,512]{4,3,1,2,0:T(8,128)(2,1)}, u32[]{:S(2)}) copy-start(bf16[1,4,2,512,512]{4,3,1,2,0:T(8,128)(2,1)} %copy.70) | copy-start | bytes 12582916
  260.5 6.1 %copy-start.11 = (bf16[4,512,512]{2,1,0:T(8,128)(2,1)S(1)}, bf16[4,512,512]{2,1,0:T(8,128)(2,1)}, u32[]{:S(2)}) copy-start(bf16[4,512,512]{2,1,0:T(8,128)(2,1)} %get-tuple-element.12) | copy-start | bytes 6291460
  260.5 6.1 %copy-start.12 = (bf16[4,512,512]{2,1,0:T(8,128)(2,1)S(1)}, bf16[4,512,512]{2,1,0:T(8,128)(2,1)}, u32[]{:S(2)}) copy-start(bf16[4,512,512]{2,1,0:T(8,128)(2,1)} %fusion.1) | copy-start | bytes 6291460
  270.9 4.8 %copy-start.10 = (bf16[4,512,512]{1,2,0:T(8,128)(2,1)S(1)}, bf16[4,512,512]{1,2,0:T(8,128)(2,1)}, u32[]{:S(2)}) copy-start(bf16[4,512,512]{1,2,0:T(8,128)(2,1)} %multiply_convert_fusion.2) | copy-start | bytes 6291460
where the time goes:
time: 284 us; the launch traced here: 283 us
  waiting for transfers between devices  179 us (63%)
  matrix products  40.9 us (14%)
  local copies, waits for them, and re-layouts  38.4 us (14%)
  other arithmetic  13.8 us (5%)
  starting transfers between devices  11.2 us (4%)
    all_to_all x1, waiting for transfers between devices, per_device(): lax.all_to_all(spread, ('mom', 'en'), split_axis=3, concat_axis=0, tiled=...  94.1 us
    all_to_all x1, waiting for transfers between devices, per_device(): lax.all_to_all(smooth, ('mom', 'en'), split_axis=0, concat_axis=3, tiled=...  84.7 us
    dot_general x3, matrix products, per_device(): jnp.einsum('eij,ejk->eik', transfer, stacked_imag, preferred_element_type...  15.2 us
    dot_general x3, matrix products, per_device(): jnp.einsum('eij,ejk->eik', transfer, stacked_real, preferred_element_type...  14.6 us
    unnamed x28, local copies, waits for them, and re-layouts  10.9 us
    convert_element_type x1, local copies, waits for them, and re-layouts, per_device(): smooth_all.astype(jnp.float32)  9.89 us
    all_to_all x1, starting transfers between devices, per_device(): lax.all_to_all(spread, ('mom', 'en'), split_axis=3, concat_axis=0, tiled=...  7.43 us
    reshape x1, local copies, waits for them, and re-layouts, per_device(): columns.reshape(mom_count, energies, 2 * tile_rows * column_count)  7.37 us
  transfers between devices with their start and end apart: 2, of which 2 were waited for; matrix products, arithmetic and copies ran while one was open for 3% of the time, Pallas kernels for 0%

commit v1 on v0

v1 whole, which is shorter than its diff:
```python
import functools

import jax
import jax.numpy as jnp
from jax import lax
from jax.experimental import pallas as pl
from jax.experimental.pallas import tpu as pltpu
from jax.sharding import PartitionSpec as P

NEUMANN = 3
TILE = 16
AXES = ("mom", "en")
VMEM_LIMIT = 48 * 1024 * 1024


class Place:
    def __init__(self, local_energies, orbitals):
        self.moms = lax.axis_size("mom")
        self.ens = lax.axis_size("en")
        self.local = local_energies
        self.energies = local_energies * self.ens
        self.reach = -(-(self.energies // 8) // local_energies)
        self.planes = self.ens // (2 * self.reach)
        assert self.planes * 2 * self.reach == self.ens
        self.group = self.moms * 2 * self.reach
        self.rows = orbitals // self.group
        self.shifts = [
            (dm, dh, dq)
            for dh in range(2)
            for dm in range(self.moms)
            for dq in range(self.reach)
        ]

    def here(self):
        n = lax.axis_index("en")
        plane = 2 * self.reach
        return lax.axis_index("mom"), n // plane, (n // self.reach) % 2, n % self.reach

    def index(self, m, z, h, q):
        return m * self.ens + (z * 2 + h) * self.reach + q

    def everyone(self):
        return [
            (m, z, h, q)
            for m in range(self.moms)
            for z in range(self.planes)
            for h in range(2)
            for q in range(self.reach)
        ]

    def target(self, m, h, q, shift):
        dm, dh, dq = shift
        return (m + dm) % self.moms, (h + dh) % 2, (q + dq) % self.reach

    def source(self, m, h, q, shift):
        dm, dh, dq = shift
        return (m - dm) % self.moms, (h + dh) % 2, (q - dq) % self.reach

    def tile(self, m, h, q):
        return (m * 2 + h) * self.reach + q

    def shift_perm(self, shift):
        pairs = []
        for m, z, h, q in self.everyone():
            tm, th, tq = self.target(m, h, q, shift)
            pairs.append((self.index(m, z, h, q), self.index(tm, z, th, tq)))
        return pairs

    def plane_perm(self, other):
        pairs = []
        for m, z, h, q in self.everyone():
            to = z + (1 if (h + other) % 2 == 1 else -1)
            if 0 <= to < self.planes:
                pairs.append((self.index(m, z, h, q), self.index(m, to, h, q)))
        return pairs

    def first_energy(self, z, h, q):
        return ((z * 2 + h) * self.reach + q) * self.local


def mixing(place, coupling, shift_table, offsets):
    m, z, h, q = place.here()
    source_mom, source_energy, target_mom, target_energy = [], [], [], []
    span = jnp.arange(place.local, dtype=jnp.int32)

    def add(moms, energies, mom, first):
        moms.append(jnp.full((place.local,), mom, jnp.int32))
        energies.append(first + span)

    for shift in place.shifts:
        tm, th, tq = place.target(m, h, q, shift)
        add(target_mom, target_energy, tm, place.first_energy(z, th, tq))
        sm, sh, sq = place.source(m, h, q, shift)
        add(source_mom, source_energy, sm, place.first_energy(z, sh, sq))
    for other in range(2):
        from_plane = jnp.where((h + other) % 2 == 1, z - 1, z + 1)
        for shift in place.shifts:
            if shift[1] == other:
                sm, sh, sq = place.source(m, h, q, shift)
                add(source_mom, source_energy, sm, place.first_energy(from_plane, sh, sq))
    source_mom, source_energy = jnp.concatenate(source_mom), jnp.concatenate(source_energy)
    target_mom, target_energy = jnp.concatenate(target_mom), jnp.concatenate(target_energy)
    one_hot = (target_mom[:, None] == jnp.arange(place.moms, dtype=jnp.int32)[None]).astype(jnp.float32)
    pick = functools.partial(jnp.einsum, "tm,mw->tw", one_hot, precision=lax.Precision.HIGHEST)
    emission, absorption = pick(coupling[0]), pick(coupling[1])
    shifted = jnp.sum(
        jnp.where(target_mom[:, None, None] == jnp.arange(place.moms)[None, :, None], shift_table[None], 0), axis=1
    )
    apart = (target_energy[:, None] - source_energy[None])[:, :, None]
    chosen = shifted[:, None, :] == source_mom[None, :, None]
    real = ((source_energy >= 0) & (source_energy < place.energies))[None, :, None]
    terms = jnp.where(apart == offsets, emission[:, None, :], 0.0) + jnp.where(
        apart == -offsets, absorption[:, None, :], 0.0
    )
    table = jnp.sum(jnp.where(chosen & real, terms, 0.0), axis=2).astype(jnp.bfloat16)
    targets, sources = table.shape
    tall = (jnp.arange(targets * TILE)[:, None] // TILE == jnp.arange(targets)[None]).astype(jnp.bfloat16)
    wide = (jnp.arange(sources)[:, None] == jnp.arange(sources * TILE)[None] // TILE).astype(jnp.bfloat16)
    spread = jnp.dot(tall, table, preferred_element_type=jnp.float32).astype(jnp.bfloat16)
    spread = jnp.dot(spread, wide, preferred_element_type=jnp.float32)
    diagonal = jnp.arange(targets * TILE)[:, None] % TILE == jnp.arange(sources * TILE)[None] % TILE
    return jnp.where(diagonal, spread, 0.0).astype(jnp.bfloat16)


def smooth_kernel(local, splits, n_in, place_ref, mix_ref, own_ref, *refs):
    pieces, halos, outs = refs[: n_in - 2], refs[n_in - 2 : n_in], refs[n_in:]
    width = own_ref.shape[-1]
    parts = [own_ref[0, :, 0].reshape(local * TILE, width)]
    parts += [r[...].reshape(local * TILE, width) for r in pieces]
    parts += [r[...].reshape(-1, width) for r in halos]
    stacked = jnp.concatenate(parts, axis=0)
    mixed = jnp.dot(mix_ref[...], stacked, preferred_element_type=jnp.float32).astype(jnp.bfloat16)
    at = 0
    for i, out in enumerate(outs):
        first, last = splits[i % len(splits)]
        out[...] = mixed[at : at + (last - first) * TILE].reshape(last - first, TILE, width)
        at += (last - first) * TILE


def smooth_call(place, part, green0, mix, pieces, halos, splits):
    local, orbitals = place.local, green0.shape[-1]
    steps = place.rows // TILE
    m, z, h, q = place.here()
    where = jnp.asarray(place.tile(m, h, q) * steps, jnp.int32).reshape(1)
    block = pl.BlockSpec((local, TILE, orbitals), lambda j, w: (0, j, 0))
    halo = halos[0].shape[0]
    return pl.pallas_call(
        functools.partial(smooth_kernel, local, splits, len(pieces) + 2),
        out_shape=[
            jax.ShapeDtypeStruct((last - first, place.rows, orbitals), jnp.bfloat16)
            for _ in place.shifts
            for first, last in splits
        ],
        grid_spec=pltpu.PrefetchScalarGridSpec(
            num_scalar_prefetch=1,
            grid=(steps,),
            in_specs=[
                pl.BlockSpec(mix.shape, lambda j, w: (0, 0)),
                pl.BlockSpec((1, local, 1, TILE, orbitals), lambda j, w: (0, 0, part, w[0] + j, 0)),
            ]
            + [block] * len(pieces)
            + [pl.BlockSpec((halo, TILE, orbitals), lambda j, w: (0, j, 0))] * 2,
            out_specs=[
                pl.BlockSpec((last - first, TILE, orbitals), lambda j, w: (0, j, 0))
                for _ in place.shifts
                for first, last in splits
            ],
        ),
        compiler_params=pltpu.CompilerParams(vmem_limit_bytes=VMEM_LIMIT),
        cost_estimate=pl.CostEstimate(
            flops=2 * mix.shape[0] * mix.shape[1] * steps * orbitals,
            bytes_accessed=2 * (mix.size + (mix.shape[0] + mix.shape[1]) * steps * orbitals),
            transcendentals=0,
        ),
        name="smooth",
    )(where, mix, green0, *pieces, *halos)


def dyson_kernel(rows, n, tile_ref, green_ref, phonon_ref, *refs):
    reals, imags = refs[:n], refs[n : 2 * n]
    out_ref, energy, transfer, series = refs[-4:]
    size = phonon_ref.shape[0]
    low, high = pl.ds(0, size), pl.ds(size, size)

    def put(to, re, im, at=None):
        top = low if at is None else pl.ds(at, rows)
        bottom = high if at is None else pl.ds(size + at, rows)
        to[top, low] = re
        to[bottom, high] = re
        to[top, high] = im
        to[bottom, low] = -im

    for k in range(n):
        at = pl.multiple_of(tile_ref[k] * rows, rows)
        scale = phonon_ref[pl.ds(at, rows), :].astype(jnp.float32)
        re = (scale * reals[k][0].astype(jnp.float32)).astype(jnp.bfloat16)
        im = (scale * imags[k][0].astype(jnp.float32)).astype(jnp.bfloat16)
        put(energy, re, im, at)
    left = jnp.concatenate([green_ref[0, 0, 0], green_ref[0, 0, 1]], axis=1)
    product = jnp.dot(left, energy[...], preferred_element_type=jnp.float32)
    transfer[...] = (product * (1.0 / size)).astype(jnp.bfloat16)
    put(series, green_ref[0, 0, 0], green_ref[0, 0, 1])
    for step in range(NEUMANN):
        added = left.astype(jnp.float32) + jnp.dot(
            transfer[...], series[...], preferred_element_type=jnp.float32
        )
        added = added.astype(jnp.bfloat16)
        if step < NEUMANN - 1:
            put(series, added[:, :size], added[:, size:])
        else:
            out_ref[0, 0, 0] = added[:, :size]
            out_ref[0, 0, 1] = added[:, size:]


def dyson_call(place, green0, phonon_me, reals, imags, first, last, out):
    size, rows, n = green0.shape[-1], place.rows, len(reals)
    m, z, h, q = place.here()
    tiles = jnp.stack([place.tile(*place.source(m, h, q, s)) for s in place.shifts]).astype(jnp.int32)
    block = pl.BlockSpec((1, 1, 2, size, size), lambda e, t: (0, first + e, 0, 0, 0))
    piece = pl.BlockSpec((1, rows, size), lambda e, t: (first + e, 0, 0))
    late = pl.BlockSpec((1, rows, size), lambda e, t: (e, 0, 0))
    specs = [block, pl.BlockSpec((size, size), lambda e, t: (0, 0))] + [piece] * n + [late] * n
    args = [tiles, green0, phonon_me, *reals, *imags]
    aliases = {}
    if out is not None:
        aliases = {len(args): 0}
        args.append(out)
        specs.append(pl.BlockSpec(memory_space=pl.ANY))
    count = last - first
    return pl.pallas_call(
        functools.partial(dyson_kernel, rows, n),
        out_shape=jax.ShapeDtypeStruct(green0.shape, green0.dtype),
        grid_spec=pltpu.PrefetchScalarGridSpec(
            num_scalar_prefetch=1,
            grid=(count,),
            in_specs=specs,
            out_specs=block,
            scratch_shapes=[
                pltpu.VMEM((2 * size, 2 * size), jnp.bfloat16),
                pltpu.VMEM((size, 2 * size), jnp.bfloat16),
                pltpu.VMEM((2 * size, 2 * size), jnp.bfloat16),
            ],
        ),
        input_output_aliases=aliases,
        compiler_params=pltpu.CompilerParams(vmem_limit_bytes=VMEM_LIMIT),
        cost_estimate=pl.CostEstimate(
            flops=count * (NEUMANN + 1) * 8 * size**3,
            bytes_accessed=(6 * count + 1) * 2 * size * size,
            transcendentals=0,
        ),
        name="dyson",
    )(*args)


def per_device(green0, phonon_me, coupling, shift_table, offsets):
    local, orbitals = green0.shape[1], green0.shape[3]
    place = Place(local, orbitals)
    m, z, h, q = place.here()
    mix = mixing(place, coupling, shift_table, offsets)
    splits = ((0, local // 2), (local // 2, local))
    whole = ((0, local),)
    pieces = [[], []]
    for part in range(2):
        for shift in place.shifts:
            at = place.tile(*place.target(m, h, q, shift)) * place.rows
            piece = lax.dynamic_slice(
                green0, (0, 0, part, at, 0), (1, local, 1, place.rows, orbitals)
            ).reshape(local, place.rows, orbitals)
            if shift != (0, 0, 0):
                piece = lax.ppermute(piece, AXES, place.shift_perm(shift))
            pieces[part].append(piece)
    back = []
    half = place.group // 2
    for part in range(2):
        halos = [
            lax.ppermute(
                jnp.concatenate(pieces[part][other * half : (other + 1) * half], axis=0),
                AXES,
                place.plane_perm(other),
            )
            for other in range(2)
        ]
        cut = whole if part == 0 else splits
        mixed = smooth_call(place, part, green0, mix, pieces[part][1:], halos, cut)
        arrived = []
        for s in range(len(cut)):
            arrived.append(
                [
                    mixed[i * len(cut) + s]
                    if shift == (0, 0, 0)
                    else lax.ppermute(mixed[i * len(cut) + s], AXES, place.shift_perm(shift))
                    for i, shift in enumerate(place.shifts)
                ]
            )
        back.append(arrived)
    out = None
    for s, (first, last) in enumerate(splits):
        out = dyson_call(place, green0, phonon_me, back[0][0], back[1][s], first, last, out)
    return out


def solution(mesh):
    in_specs = (P("mom", "en", None, None, None), P(), P(), P(), P())
    out_specs = P("mom", "en", None, None, None)
    return jax.shard_map(
        per_device, mesh=mesh, in_specs=in_specs, out_specs=out_specs, check_vma=False
    )
```

time: 284 us -> 187 us (0.66)
  waiting for transfers between devices: 179 us -> 67.2 us
  starting transfers between devices: 11.2 us -> 53 us
  matrix products: 40.9 us -> 1 us
  Pallas kernels: 0 us -> 35 us
  local copies, waits for them, and re-layouts: 38.4 us -> 23 us
  other arithmetic: 13.8 us -> 6.11 us
    all_to_all x2 -> x0, waiting for transfers between devices: 179 us -> none  [the longest x1 94.1 us: per_device(): lax.all_to_all(spread, ('mom', 'en'), split_axis=3, concat_axis=0, tiled=...]
    ppermute x0 -> x39, waiting for transfers between devices: none -> 67.2 us  [the longest x14 23.6 us: per_device(): piece = lax.ppermute(piece, AXES, place.shift_perm(shift))]
    ppermute x0 -> x39, starting transfers between devices: none -> 53 us  [the longest x21 21.4 us: per_device(): lax.ppermute(mixed[i * len(cut) + s], AXES, place.shift_perm(shift))]
    dot_general x11 -> x3, matrix products: 40.9 us -> 1 us  [the longest x1 0.6 us: mixing(): spread = jnp.dot(spread, wide, preferred_element_type=jnp.float32)]
    pallas_call x0 -> x4, Pallas kernels: none -> 35 us  [the longest x2 24.9 us: dyson_call(): pl.pallas_call(functools.partial(dyson_kernel, rows, n), out_shape=jax.Sh...]
    convert_element_type x2 -> x0, other arithmetic: 11.3 us -> none  [the longest x1 6.63 us: per_device(): smooth_all.astype(jnp.float32)]
    all_to_all x2 -> x0, starting transfers between devices: 11.2 us -> none  [the longest x1 7.43 us: per_device(): lax.all_to_all(spread, ('mom', 'en'), split_axis=3, concat_axis=0, tiled=...]
    convert_element_type x2 -> x0, local copies, waits for them, and re-layouts: 10.1 us -> none  [the longest x1 9.89 us: per_device(): smooth_all.astype(jnp.float32)]
  transfers between devices with their start and end apart: 2 -> 39, of which waited for: 2 -> 16; matrix products, arithmetic and copies ran while one was open for 3% -> 4% of each run, Pallas kernels for 0% -> 12%
where the time goes in v1:
time: 187 us; the launch traced here: 186 us
  waiting for transfers between devices  67.2 us (36%)
  starting transfers between devices  53 us (28%)
  Pallas kernels  35 us (19%)
  local copies, waits for them, and re-layouts  23 us (12%)
  other arithmetic  6.11 us (3%)
    pallas_call x2, Pallas kernels, dyson_call(): pl.pallas_call(functools.partial(dyson_kernel, rows, n), out_shape=jax.Sh...  24.9 us
    ppermute x14, waiting for transfers between devices, per_device(): piece = lax.ppermute(piece, AXES, place.shift_perm(shift))  23.6 us
    ppermute x4, waiting for transfers between devices, per_device(): lax.ppermute(jnp.concatenate(pieces[part][other * half:(other + 1) * half...  22.1 us
    ppermute x21, waiting for transfers between devices, per_device(): lax.ppermute(mixed[i * len(cut) + s], AXES, place.shift_perm(shift))  21.5 us
    ppermute x21, starting transfers between devices, per_device(): lax.ppermute(mixed[i * len(cut) + s], AXES, place.shift_perm(shift))  21.4 us
    unnamed x98, local copies, waits for them, and re-layouts  18.9 us
    ppermute x14, starting transfers between devices, per_device(): piece = lax.ppermute(piece, AXES, place.shift_perm(shift))  17.8 us
    ppermute x4, starting transfers between devices, per_device(): lax.ppermute(jnp.concatenate(pieces[part][other * half:(other + 1) * half...  13.8 us
  transfers between devices with their start and end apart: 39, of which 16 were waited for; matrix products, arithmetic and copies ran while one was open for 4% of the time, Pallas kernels for 12%

profile of v1, /device:TPU:0, one launch (start us, length us, event | category | flops | bytes accessed | tf_op | source)
XLA Modules:
  0.0 185.7 jit_solution(17081014214455699504)
XLA Ops:
  0.0 3.6 %dynamic-slice_bitcast_fusion = (bf16[4,64,512]{2,1,0:T(8,128)(2,1)S(1)}, bf16[4,64,512]{2,1,0:T(8,128)(2,1)S(1)}, bf16[4,64,512]{2,1,0:T(8,128)(2,1)S(1)}, bf16...) fusion(bf16[1,4,2,512,512]{4,3,2,1,0:T(8,128)(2,1)} %green_ref., ...), kind=kLoop, calls=%fused_computation.6 | loop fusion | bytes 8388640 | tf_op jit(solution)/shard_map/reshape | solution.py:268
  3.6 3.3 %collective-permute-start.22 = (bf16[4,64,512]{2,1,0:T(8,128)(2,1)S(1)}, bf16[4,64,512]{2,1,0:T(8,128)(2,1)S(1)}, u32[]{:S(2)}, u32[]{:S(2)}) collective-permute-start(bf16[4,64,512]{2,1,0:T(8,128)(2,1)S(1)} %get-tuple-element.54), channel_id=1, source_target_pairs={{0,19},{1,18},{2,17},{3,16},{4,23},{5,22},{6,21},{7,20},{8,27},{9,... | collective-permute-start | bytes 786440 | tf_op jit(solution)/shard_map/ppermute | solution.py:270
  7.6 1.4 collective-permute-start.20
  9.3 1.1 collective-permute-start.18
  11.0 2.7 %collective-permute-done.22.refs_6_ = bf16[4,64,512]{2,1,0:T(8,128)(2,1)S(1)} collective-permute-done((bf16[4,64,512]{2,1,0:T(8,128)(2,1)S(1)}, bf16[4,64,512]{2,1,0:T(8,128)(2,1)S(1)}, u32[]{:S(2)}, u32[]{:S(2)}) %collective-permute-start.22) | collective-permute-done | bytes 262176 | tf_op jit(solution)/shard_map/ppermute | solution.py:270
  13.7 2.5 %collective-permute-start.17 = (bf16[4,64,512]{2,1,0:T(8,128)(2,1)S(1)}, bf16[4,64,512]{2,1,0:T(8,128)(2,1)S(1)}, u32[]{:S(2)}, u32[]{:S(2)}) collective-permute-start(bf16[4,64,512]{2,1,0:T(8,128)(2,1)S(1)} %get-tuple-element.59), channel_id=1, source_target_pairs={{0,16},{1,17},{2,18},{3,19},{4,20},{5,21},{6,22},{7,23},{8,24},{9,... | collective-permute-start | bytes 786440 | tf_op jit(solution)/shard_map/ppermute | solution.py:270
  16.2 4.2 %collective-permute-done.21.refs_5_ = bf16[4,64,512]{2,1,0:T(8,128)(2,1)S(1)} collective-permute-done((bf16[4,64,512]{2,1,0:T(8,128)(2,1)S(1)}, bf16[4,64,512]{2,1,0:T(8,128)(2,1)S(1)}, u32[]{:S(2)}, u32[]{:S(2)}) %collective-permute-start.21) | collective-permute-done | bytes 262176 | tf_op jit(solution)/shard_map/ppermute | solution.py:270
  20.3 4.7 %collective-permute-done.20.refs_4_ = bf16[4,64,512]{2,1,0:T(8,128)(2,1)S(1)} collective-permute-done((bf16[4,64,512]{2,1,0:T(8,128)(2,1)S(1)}, bf16[4,64,512]{2,1,0:T(8,128)(2,1)S(1)}, u32[]{:S(2)}, u32[]{:S(2)}) %collective-permute-start.20) | collective-permute-done | bytes 262176 | tf_op jit(solution)/shard_map/ppermute | solution.py:270
  25.0 3.0 %collective-permute-start.6 = (bf16[4,64,512]{2,1,0:T(8,128)(2,1)}, bf16[4,64,512]{2,1,0:T(8,128)(2,1)S(1)}, u32[]{:S(2)}, u32[]{:S(2)}) collective-permute-start(bf16[4,64,512]{2,1,0:T(8,128)(2,1)} %get-tuple-element.62), channel_id=1, source_target_pairs={{0,19},{1,18},{2,17},{3,16},{4,23},{5,22},{6,21},{7,20},{8,27},{9,... | collective-permute-start | bytes 786440 | tf_op jit(solution)/shard_map/ppermute | solution.py:270
  28.4 3.2 %collective-permute-done.17.refs_1_ = bf16[4,64,512]{2,1,0:T(8,128)(2,1)S(1)} collective-permute-done((bf16[4,64,512]{2,1,0:T(8,128)(2,1)S(1)}, bf16[4,64,512]{2,1,0:T(8,128)(2,1)S(1)}, u32[]{:S(2)}, u32[]{:S(2)}) %collective-permute-start.17) | collective-permute-done | bytes 262176 | tf_op jit(solution)/shard_map/ppermute | solution.py:270
  31.6 1.7 collective-permute-start.3
  33.3 1.1 pad_maximum_fusion.2
  34.4 1.3 collective-permute-start.2
  36.3 2.3 %collective-permute-start.1 = (bf16[4,64,512]{2,1,0:T(8,128)(2,1)}, bf16[4,64,512]{2,1,0:T(8,128)(2,1)}, u32[]{:S(2)}, u32[]{:S(2)}) collective-permute-start(bf16[4,64,512]{2,1,0:T(8,128)(2,1)} %get-tuple-element.67), channel_id=1, source_target_pairs={{0,16},{1,17},{2,18},{3,19},{4,20},{5,21},{6,22},{7,23},{8,24},{9,... | collective-permute-start | bytes 786440 | tf_op jit(solution)/shard_map/ppermute | solution.py:270
  38.7 4.2 %collective-permute-done.5.refs_5_ = bf16[4,64,512]{2,1,0:T(8,128)(2,1)S(1)} collective-permute-done((bf16[4,64,512]{2,1,0:T(8,128)(2,1)}, bf16[4,64,512]{2,1,0:T(8,128)(2,1)S(1)}, u32[]{:S(2)}, u32[]{:S(2)}) %collective-permute-start.5) | collective-permute-done | bytes 262176 | tf_op jit(solution)/shard_map/ppermute | solution.py:270
  42.8 1.1 pad_maximum_fusion.3
  44.0 3.6 %collective-permute-done.4.refs_4_ = bf16[4,64,512]{2,1,0:T(8,128)(2,1)S(1)} collective-permute-done((bf16[4,64,512]{2,1,0:T(8,128)(2,1)}, bf16[4,64,512]{2,1,0:T(8,128)(2,1)S(1)}, u32[]{:S(2)}, u32[]{:S(2)}) %collective-permute-start.4) | collective-permute-done | bytes 262176 | tf_op jit(solution)/shard_map/ppermute | solution.py:270
  47.6 5.2 %collective-permute-start.24 = (bf16[16,64,512]{2,1,0:T(8,128)(2,1)}, bf16[16,64,512]{2,1,0:T(8,128)(2,1)}, u32[]{:S(2)}, u32[]{:S(2)}) collective-permute-start(bf16[16,64,512]{2,1,0:T(8,128)(2,1)} %pad_maximum_fusion.3), channel_id=1, source_target_pairs={{0,4},{1,5},{4,8},{5,9},{6,2},{7,3},{8,12},{9,13},{10,6},{11,7},{1... | collective-permute-start | bytes 3145736 | tf_op jit(solution)/shard_map/ppermute | solution.py:276
  53.2 1.3 collective-permute-start.23
  54.7 1.1 pad_maximum_fusion.1
  55.8 5.8 %collective-permute-start.8 = (bf16[16,64,512]{2,1,0:T(8,128)(2,1)}, bf16[16,64,512]{2,1,0:T(8,128)(2,1)}, u32[]{:S(2)}, u32[]{:S(2)}) collective-permute-start(bf16[16,64,512]{2,1,0:T(8,128)(2,1)} %pad_maximum_fusion.1), channel_id=1, source_target_pairs={{0,4},{1,5},{4,8},{5,9},{6,2},{7,3},{8,12},{9,13},{10,6},{11,7},{1... | collective-permute-start | bytes 3145736 | tf_op jit(solution)/shard_map/ppermute | solution.py:276
  61.7 2.3 %pad_maximum_fusion = bf16[16,64,512]{2,1,0:T(8,128)(2,1)} fusion(bf16[4,64,512]{2,1,0:T(8,128)(2,1)} %collective-permute-done.2.refs_2_, bf16[4,64,512]{2,1,0:T(8,128)(2,1)} %collective-permute-done.1.refs_1_, bf16[4,64,512]{2,1,0:T(8,128)(2,1)} %collective-permute-done.refs_0_, bf16[4,64,512]{2,1,0:T(8,128)(2,1)} %get-tuple-element.61), kind=kLoop, calls=%fused_computation.2 | loop fusion | flops 1572864 | bytes 2097152 | tf_op jit(solution)/shard_map/concatenate | solution.py:277
  64.0 1.5 collective-permute-start.7
  66.6 9.0 %collective-permute-done.24.refs_8_ = bf16[16,64,512]{2,1,0:T(8,128)(2,1)} collective-permute-done((bf16[16,64,512]{2,1,0:T(8,128)(2,1)}, bf16[16,64,512]{2,1,0:T(8,128)(2,1)}, u32[]{:S(2)}, u32[]{:S(2)}) %collective-permute-start.24) | collective-permute-done | bytes 1048608 | tf_op jit(solution)/shard_map/ppermute | solution.py:276
  75.6 6.0 %collective-permute-done.23.refs_7_ = bf16[16,64,512]{2,1,0:T(8,128)(2,1)S(1)} collective-permute-done((bf16[16,64,512]{2,1,0:T(8,128)(2,1)}, bf16[16,64,512]{2,1,0:T(8,128)(2,1)S(1)}, u32[]{:S(2)}, u32[]{:S(2)}) %collective-permute-start.23) | collective-permute-done | bytes 1048608 | tf_op jit(solution)/shard_map/ppermute | solution.py:276
  81.6 0.9 copy-done.1
  82.5 0.9 copy-done.3
  87.3 4.8 %smooth.3 = (bf16[2,64,512]{2,1,0:T(8,128)(2,1)S(1)}, bf16[2,64,512]{2,1,0:T(8,128)(2,1)S(1)}, bf16[2,64,512]{2,1,0:T(8,128)(2,1)S(1)}, bf16[2,64,512]{2,1,0:T(8...) custom-call(s32[1]{0:T(128)} %bitcast.8.place_ref, ...), custom_call_target="tpu_custom_call" | custom-call | flops 2147483648 | bytes 7340032 | tf_op jit(solution)/shard_map/smooth/pallas_call | solution.py:147
  92.8 2.0 %collective-permute-start.26 = (bf16[2,64,512]{2,1,0:T(8,128)(2,1)S(1)}, bf16[2,64,512]{2,1,0:T(8,128)(2,1)S(1)}, u32[]{:S(2)}, u32[]{:S(2)}) collective-permute-start(bf16[2,64,512]{2,1,0:T(8,128)(2,1)S(1)} %get-tuple-element.39), channel_id=1, source_target_pairs={{0,16},{1,17},{2,18},{3,19},{4,20},{5,21},{6,22},{7,23},{8,24},{9,... | collective-permute-start | bytes 393224 | tf_op jit(solution)/shard_map/ppermute | solution.py:291
  95.0 2.3 %collective-permute-done.8.refs_8_ = bf16[16,64,512]{2,1,0:T(8,128)(2,1)} collective-permute-done((bf16[16,64,512]{2,1,0:T(8,128)(2,1)}, bf16[16,64,512]{2,1,0:T(8,128)(2,1)}, u32[]{:S(2)}, u32[]{:S(2)}) %collective-permute-start.8) | collective-permute-done | bytes 1048608 | tf_op jit(solution)/shard_map/ppermute | solution.py:276
  97.4 1.5 collective-permute-start.33
  98.9 4.7 %collective-permute-done.7.refs_7_ = bf16[16,64,512]{2,1,0:T(8,128)(2,1)S(1)} collective-permute-done((bf16[16,64,512]{2,1,0:T(8,128)(2,1)}, bf16[16,64,512]{2,1,0:T(8,128)(2,1)S(1)}, u32[]{:S(2)}, u32[]{:S(2)}) %collective-permute-start.7) | collective-permute-done | bytes 1048608 | tf_op jit(solution)/shard_map/ppermute | solution.py:276
  104.9 5.3 %smooth.2 = (bf16[4,64,512]{2,1,0:T(8,128)(2,1)S(1)}, bf16[4,64,512]{2,1,0:T(8,128)(2,1)S(1)}, bf16[4,64,512]{2,1,0:T(8,128)(2,1)S(1)}, bf16[4,64,512]{2,1,0:T(8...) custom-call(s32[1]{0:T(128)} %bitcast.8.place_ref, ...), custom_call_target="tpu_custom_call" | custom-call | flops 2147483648 | bytes 7340032 | tf_op jit(solution)/shard_map/smooth/pallas_call | solution.py:147
  110.8 1.0 collective-permute-start.9
  115.2 1.4 collective-permute-start.37
  117.3 1.3 collective-permute-start.38
  120.1 1.2 collective-permute-start.11
  121.2 4.1 %collective-permute-done.37.refs_14_ = bf16[2,64,512]{2,1,0:T(8,128)(2,1)S(1)} collective-permute-done((bf16[2,64,512]{2,1,0:T(8,128)(2,1)S(1)}, bf16[2,64,512]{2,1,0:T(8,128)(2,1)S(1)}, u32[]{:S(2)}, u32[]{:S(2)}) %collective-permute-start.37) | collective-permute-done | bytes 131104 | tf_op jit(solution)/shard_map/ppermute | solution.py:291
  127.2 1.6 collective-permute-start.13
  128.8 1.2 collective-permute-start.14
  130.0 1.0 collective-permute-start.15
  131.1 1.7 collective-permute-start.27
  132.8 13.8 %collective-permute-done.12.refs_4_ = bf16[4,64,512]{2,1,0:T(8,128)(2,1)S(1)} collective-permute-done((bf16[4,64,512]{2,1,0:T(8,128)(2,1)}, bf16[4,64,512]{2,1,0:T(8,128)(2,1)S(1)}, u32[]{:S(2)}, u32[]{:S(2)}) %collective-permute-start.12) | collective-permute-done | bytes 262176 | tf_op jit(solution)/shard_map/ppermute | solution.py:291
  146.9 2.8 %collective-permute-done.13.refs_5_ = bf16[4,64,512]{2,1,0:T(8,128)(2,1)S(1)} collective-permute-done((bf16[4,64,512]{2,1,0:T(8,128)(2,1)}, bf16[4,64,512]{2,1,0:T(8,128)(2,1)S(1)}, u32[]{:S(2)}, u32[]{:S(2)}) %collective-permute-start.13) | collective-permute-done | bytes 262176 | tf_op jit(solution)/shard_map/ppermute | solution.py:291
  149.6 1.8 collective-permute-start.29
  151.4 1.5 collective-permute-start.30
  160.7 12.4 %dyson.2.refs_16_ = bf16[1,4,2,512,512]{4,3,2,1,0:T(8,128)(2,1)} custom-call(s32[8]{0:T(128)S(1)} %stack.44.tile_ref, bf16[1,4,2,512,512]{4,3,2,1,0:T(8,128)(2,1)} %green_ref.3, bf16[512,512]{1,0:T(8,128)(2,1)S(1)} %copy-done.20, bf16[4,64,512]{2,1,0:T(8,128)(2,1)S(1)} %get-tuple-element.29.refs_0_, bf16[4,64,512]{2,1,0:T(8,128)(2,1)S(1)} %collective-permute-done.9.refs_1_, ...), custom_call_target="tpu_custom_call" | custom-call | flops 8589934592 | bytes 6815744 | tf_op jit(solution)/shard_map/dyson/pallas_call | solution.py:230
  173.2 12.5 %dyson.3 = bf16[1,4,2,512,512]{4,3,2,1,0:T(8,128)(2,1)} custom-call(s32[8]{0:T(128)S(1)} %stack.44.tile_ref, bf16[1,4,2,512,512]{4,3,2,1,0:T(8,128)(2,1)} %green_ref.3, bf16[512,512]{1,0:T(8,128)(2,1)S(1)} %copy-done.20, bf16[4,64,512]{2,1,0:T(8,128)(2,1)S(1)} %get-tuple-element.29.refs_0_, ...), custom_call_target="tpu_custom_call", output_to_operand_aliasing={{}: (19, {})} | custom-call | flops 8589934592 | bytes 6815744 | tf_op jit(solution)/shard_map/dyson/pallas_call | solution.py:230
  (162 shorter events, 26.3 us)
Async XLA Ops:
  0.0 28.3 %copy-start.47 = (s32[2,16]{1,0:T(2,128)S(1)}, s32[2,16]{1,0:T(2,128)}, u32[]{:S(2)}) copy-start(s32[2,16]{1,0:T(2,128)} %param.8) | copy-start | bytes 388
  3.6 10.1 %collective-permute-start.22 = (bf16[4,64,512]{2,1,0:T(8,128)(2,1)S(1)}, bf16[4,64,512]{2,1,0:T(8,128)(2,1)S(1)}, u32[]{:S(2)}, u32[]{:S(2)}) collective-permute-start(bf16[4,64,512]{2,1,0:T(8,128)(2,1)S(1)} %get-tuple-element.54), channel_id=1, source_target_pairs={{0,19},{1,18},{2,17},{3,16},{4,23},{5,22},{6,21},{7,20},{8,27},{9,... | collective-permute-start | bytes 786440 | tf_op jit(solution)/shard_map/ppermute | solution.py:270
  7.0 13.4 %collective-permute-start.21 = (bf16[4,64,512]{2,1,0:T(8,128)(2,1)S(1)}, bf16[4,64,512]{2,1,0:T(8,128)(2,1)S(1)}, u32[]{:S(2)}, u32[]{:S(2)}) collective-permute-start(bf16[4,64,512]{2,1,0:T(8,128)(2,1)S(1)} %get-tuple-element.55), channel_id=1, source_target_pairs={{0,18},{1,19},{2,16},{3,17},{4,22},{5,23},{6,20},{7,21},{8,26},{9,... | collective-permute-start | bytes 786440 | tf_op jit(solution)/shard_map/ppermute | solution.py:270
  7.6 17.4 %collective-permute-start.20 = (bf16[4,64,512]{2,1,0:T(8,128)(2,1)S(1)}, bf16[4,64,512]{2,1,0:T(8,128)(2,1)S(1)}, u32[]{:S(2)}, u32[]{:S(2)}) collective-permute-start(bf16[4,64,512]{2,1,0:T(8,128)(2,1)S(1)} %get-tuple-element.56), channel_id=1, source_target_pairs={{0,3},{1,2},{2,1},{3,0},{4,7},{5,6},{6,5},{7,4},{8,11},{9,10},{10,... | collective-permute-start | bytes 786440 | tf_op jit(solution)/shard_map/ppermute | solution.py:270
  9.0 25.4 %collective-permute-start.19 = (bf16[4,64,512]{2,1,0:T(8,128)(2,1)}, bf16[4,64,512]{2,1,0:T(8,128)(2,1)S(1)}, u32[]{:S(2)}, u32[]{:S(2)}) collective-permute-start(bf16[4,64,512]{2,1,0:T(8,128)(2,1)} %get-tuple-element.57), channel_id=1, source_target_pairs={{0,2},{1,3},{2,0},{3,1},{4,6},{5,7},{6,4},{7,5},{8,10},{9,11},{10,... | collective-permute-start | bytes 786440 | tf_op jit(solution)/shard_map/ppermute | solution.py:270
  9.3 18.8 %collective-permute-start.18 = (bf16[4,64,512]{2,1,0:T(8,128)(2,1)S(1)}, bf16[4,64,512]{2,1,0:T(8,128)(2,1)S(1)}, u32[]{:S(2)}, u32[]{:S(2)}) collective-permute-start(bf16[4,64,512]{2,1,0:T(8,128)(2,1)S(1)} %get-tuple-element.58), channel_id=1, source_target_pairs={{0,17},{1,16},{2,19},{3,18},{4,21},{5,20},{6,23},{7,22},{8,25},{9,... | collective-permute-start | bytes 786440 | tf_op jit(solution)/shard_map/ppermute | solution.py:270
  13.7 17.8 %collective-permute-start.17 = (bf16[4,64,512]{2,1,0:T(8,128)(2,1)S(1)}, bf16[4,64,512]{2,1,0:T(8,128)(2,1)S(1)}, u32[]{:S(2)}, u32[]{:S(2)}) collective-permute-start(bf16[4,64,512]{2,1,0:T(8,128)(2,1)S(1)} %get-tuple-element.59), channel_id=1, source_target_pairs={{0,16},{1,17},{2,18},{3,19},{4,20},{5,21},{6,22},{7,23},{8,24},{9,... | collective-permute-start | bytes 786440 | tf_op jit(solution)/shard_map/ppermute | solution.py:270
  20.3 23.6 %copy-start = (bf16[4,64,512]{2,1,0:T(8,128)(2,1)}, bf16[4,64,512]{2,1,0:T(8,128)(2,1)S(1)}, u32[]{:S(2)}) copy-start(bf16[4,64,512]{2,1,0:T(8,128)(2,1)S(1)} %collective-permute-done.21.refs_5_) | copy-start | bytes 786436
  20.3 11.2 %collective-permute-start.16 = (bf16[4,64,512]{2,1,0:T(8,128)(2,1)S(1)}, bf16[4,64,512]{2,1,0:T(8,128)(2,1)S(1)}, u32[]{:S(2)}, u32[]{:S(2)}) collective-permute-start(bf16[4,64,512]{2,1,0:T(8,128)(2,1)S(1)} %get-tuple-element.60), channel_id=1, source_target_pairs={{0,1},{1,0},{2,3},{3,2},{4,5},{5,4},{6,7},{7,6},{8,9},{9,8},{10,11... | collective-permute-start | bytes 786440 | tf_op jit(solution)/shard_map/ppermute | solution.py:270
  25.0 18.9 %copy-start.2 = (bf16[4,64,512]{2,1,0:T(8,128)(2,1)}, bf16[4,64,512]{2,1,0:T(8,128)(2,1)S(1)}, u32[]{:S(2)}) copy-start(bf16[4,64,512]{2,1,0:T(8,128)(2,1)S(1)} %collective-permute-done.20.refs_4_) | copy-start | bytes 786436
  25.0 11.3 %collective-permute-start.6 = (bf16[4,64,512]{2,1,0:T(8,128)(2,1)}, bf16[4,64,512]{2,1,0:T(8,128)(2,1)S(1)}, u32[]{:S(2)}, u32[]{:S(2)}) collective-permute-start(bf16[4,64,512]{2,1,0:T(8,128)(2,1)} %get-tuple-element.62), channel_id=1, source_target_pairs={{0,19},{1,18},{2,17},{3,16},{4,23},{5,22},{6,21},{7,20},{8,27},{9,... | collective-permute-start | bytes 786440 | tf_op jit(solution)/shard_map/ppermute | solution.py:270
  28.0 14.8 %collective-permute-start.5 = (bf16[4,64,512]{2,1,0:T(8,128)(2,1)}, bf16[4,64,512]{2,1,0:T(8,128)(2,1)S(1)}, u32[]{:S(2)}, u32[]{:S(2)}) collective-permute-start(bf16[4,64,512]{2,1,0:T(8,128)(2,1)} %get-tuple-element.63), channel_id=1, source_target_pairs={{0,18},{1,19},{2,16},{3,17},{4,22},{5,23},{6,20},{7,21},{8,26},{9,... | collective-permute-start | bytes 786440 | tf_op jit(solution)/shard_map/ppermute | solution.py:270
  31.5 16.0 %collective-permute-start.4 = (bf16[4,64,512]{2,1,0:T(8,128)(2,1)}, bf16[4,64,512]{2,1,0:T(8,128)(2,1)S(1)}, u32[]{:S(2)}, u32[]{:S(2)}) collective-permute-start(bf16[4,64,512]{2,1,0:T(8,128)(2,1)} %get-tuple-element.64), channel_id=1, source_target_pairs={{0,3},{1,2},{2,1},{3,0},{4,7},{5,6},{6,5},{7,4},{8,11},{9,10},{10,... | collective-permute-start | bytes 786440 | tf_op jit(solution)/shard_map/ppermute | solution.py:270
  31.6 21.6 %collective-permute-start.3 = (bf16[4,64,512]{2,1,0:T(8,128)(2,1)S(1)}, bf16[4,64,512]{2,1,0:T(8,128)(2,1)S(1)}, u32[]{:S(2)}, u32[]{:S(2)}) collective-permute-start(bf16[4,64,512]{2,1,0:T(8,128)(2,1)S(1)} %get-tuple-element.65), channel_id=1, source_target_pairs={{0,2},{1,3},{2,0},{3,1},{4,6},{5,7},{6,4},{7,5},{8,10},{9,11},{10,... | collective-permute-start | bytes 786440 | tf_op jit(solution)/shard_map/ppermute | solution.py:270
  33.3 21.4 %copy-start.48 = (s32[16]{0:T(128)S(1)}, s32[16]{0:T(128)}, u32[]{:S(2)}) copy-start(s32[16]{0:T(128)} %param.9) | copy-start | bytes 196
  34.4 21.4 %copy-start.4 = (bf16[4,64,512]{2,1,0:T(8,128)(2,1)}, bf16[4,64,512]{2,1,0:T(8,128)(2,1)S(1)}, u32[]{:S(2)}) copy-start(bf16[4,64,512]{2,1,0:T(8,128)(2,1)S(1)} %collective-permute-done.19.refs_3_) | copy-start | bytes 786436
  34.4 21.4 %collective-permute-start.2 = (bf16[4,64,512]{2,1,0:T(8,128)(2,1)}, bf16[4,64,512]{2,1,0:T(8,128)(2,1)}, u32[]{:S(2)}, u32[]{:S(2)}) collective-permute-start(bf16[4,64,512]{2,1,0:T(8,128)(2,1)} %get-tuple-element.66), channel_id=1, source_target_pairs={{0,17},{1,16},{2,19},{3,18},{4,21},{5,20},{6,23},{7,22},{8,25},{9,... | collective-permute-start | bytes 786440 | tf_op jit(solution)/shard_map/ppermute | solution.py:270
  36.3 19.5 %copy-start.8 = (bf16[4,64,512]{2,1,0:T(8,128)(2,1)}, bf16[4,64,512]{2,1,0:T(8,128)(2,1)S(1)}, u32[]{:S(2)}) copy-start(bf16[4,64,512]{2,1,0:T(8,128)(2,1)S(1)} %collective-permute-done.6.refs_6_) | copy-start | bytes 786436
  36.3 25.3 %collective-permute-start.1 = (bf16[4,64,512]{2,1,0:T(8,128)(2,1)}, bf16[4,64,512]{2,1,0:T(8,128)(2,1)}, u32[]{:S(2)}, u32[]{:S(2)}) collective-permute-start(bf16[4,64,512]{2,1,0:T(8,128)(2,1)} %get-tuple-element.67), channel_id=1, source_target_pairs={{0,16},{1,17},{2,18},{3,19},{4,20},{5,21},{6,22},{7,23},{8,24},{9,... | collective-permute-start | bytes 786440 | tf_op jit(solution)/shard_map/ppermute | solution.py:270
  42.8 18.8 %collective-permute-start = (bf16[4,64,512]{2,1,0:T(8,128)(2,1)}, bf16[4,64,512]{2,1,0:T(8,128)(2,1)}, u32[]{:S(2)}, u32[]{:S(2)}) collective-permute-start(bf16[4,64,512]{2,1,0:T(8,128)(2,1)} %get-tuple-element.68), channel_id=1, source_target_pairs={{0,1},{1,0},{2,3},{3,2},{4,5},{5,4},{6,7},{7,6},{8,9},{9,8},{10,11... | collective-permute-start | bytes 786440 | tf_op jit(solution)/shard_map/ppermute | solution.py:270
  47.6 28.0 %collective-permute-start.24 = (bf16[16,64,512]{2,1,0:T(8,128)(2,1)}, bf16[16,64,512]{2,1,0:T(8,128)(2,1)}, u32[]{:S(2)}, u32[]{:S(2)}) collective-permute-start(bf16[16,64,512]{2,1,0:T(8,128)(2,1)} %pad_maximum_fusion.3), channel_id=1, source_target_pairs={{0,4},{1,5},{4,8},{5,9},{6,2},{7,3},{8,12},{9,13},{10,6},{11,7},{1... | collective-permute-start | bytes 3145736 | tf_op jit(solution)/shard_map/ppermute | solution.py:276
  53.2 28.4 %collective-permute-start.23 = (bf16[16,64,512]{2,1,0:T(8,128)(2,1)}, bf16[16,64,512]{2,1,0:T(8,128)(2,1)S(1)}, u32[]{:S(2)}, u32[]{:S(2)}) collective-permute-start(bf16[16,64,512]{2,1,0:T(8,128)(2,1)} %pad_maximum_fusion.2), channel_id=1, source_target_pairs={{2,6},{3,7},{4,0},{5,1},{6,10},{7,11},{8,4},{9,5},{10,14},{11,15},... | collective-permute-start | bytes 3145736 | tf_op jit(solution)/shard_map/ppermute | solution.py:276
  55.8 41.6 %collective-permute-start.8 = (bf16[16,64,512]{2,1,0:T(8,128)(2,1)}, bf16[16,64,512]{2,1,0:T(8,128)(2,1)}, u32[]{:S(2)}, u32[]{:S(2)}) collective-permute-start(bf16[16,64,512]{2,1,0:T(8,128)(2,1)} %pad_maximum_fusion.1), channel_id=1, source_target_pairs={{0,4},{1,5},{4,8},{5,9},{6,2},{7,3},{8,12},{9,13},{10,6},{11,7},{1... | collective-permute-start | bytes 3145736 | tf_op jit(solution)/shard_map/ppermute | solution.py:276
  64.0 39.6 %collective-permute-start.7 = (bf16[16,64,512]{2,1,0:T(8,128)(2,1)}, bf16[16,64,512]{2,1,0:T(8,128)(2,1)S(1)}, u32[]{:S(2)}, u32[]{:S(2)}) collective-permute-start(bf16[16,64,512]{2,1,0:T(8,128)(2,1)} %pad_maximum_fusion), channel_id=1, source_target_pairs={{2,6},{3,7},{4,0},{5,1},{6,10},{7,11},{8,4},{9,5},{10,14},{11,15},... | collective-permute-start | bytes 3145736 | tf_op jit(solution)/shard_map/ppermute | solution.py:276
  87.3 17.6 %copy-start.13 = (bf16[4,64,512]{2,1,0:T(8,128)(2,1)S(1)}, bf16[4,64,512]{2,1,0:T(8,128)(2,1)}, u32[]{:S(2)}) copy-start(bf16[4,64,512]{2,1,0:T(8,128)(2,1)} %copy-done.12) | copy-start | bytes 786436
  87.3 17.6 %copy-start.15 = (bf16[4,64,512]{2,1,0:T(8,128)(2,1)S(1)}, bf16[4,64,512]{2,1,0:T(8,128)(2,1)}, u32[]{:S(2)}) copy-start(bf16[4,64,512]{2,1,0:T(8,128)(2,1)} %copy-done.14) | copy-start | bytes 786436
  92.8 11.5 %collective-permute-start.25 = (bf16[2,64,512]{2,1,0:T(8,128)(2,1)S(1)}, bf16[2,64,512]{2,1,0:T(8,128)(2,1)S(1)}, u32[]{:S(2)}, u32[]{:S(2)}) collective-permute-start(bf16[2,64,512]{2,1,0:T(8,128)(2,1)S(1)} %get-tuple-element.38), channel_id=1, source_target_pairs={{0,1},{1,0},{2,3},{3,2},{4,5},{5,4},{6,7},{7,6},{8,9},{9,8},{10,11... | collective-permute-start | bytes 393224 | tf_op jit(solution)/shard_map/ppermute | solution.py:291
  92.8 17.3 %collective-permute-start.26 = (bf16[2,64,512]{2,1,0:T(8,128)(2,1)S(1)}, bf16[2,64,512]{2,1,0:T(8,128)(2,1)S(1)}, u32[]{:S(2)}, u32[]{:S(2)}) collective-permute-start(bf16[2,64,512]{2,1,0:T(8,128)(2,1)S(1)} %get-tuple-element.39), channel_id=1, source_target_pairs={{0,16},{1,17},{2,18},{3,19},{4,20},{5,21},{6,22},{7,23},{8,24},{9,... | collective-permute-start | bytes 393224 | tf_op jit(solution)/shard_map/ppermute | solution.py:291
  94.9 16.9 %collective-permute-start.32 = (bf16[2,64,512]{2,1,0:T(8,128)(2,1)S(1)}, bf16[2,64,512]{2,1,0:T(8,128)(2,1)S(1)}, u32[]{:S(2)}, u32[]{:S(2)}) collective-permute-start(bf16[2,64,512]{2,1,0:T(8,128)(2,1)S(1)} %get-tuple-element.46), channel_id=1, source_target_pairs={{0,1},{1,0},{2,3},{3,2},{4,5},{5,4},{6,7},{7,6},{8,9},{9,8},{10,11... | collective-permute-start | bytes 393224 | tf_op jit(solution)/shard_map/ppermute | solution.py:291
  97.4 15.6 %collective-permute-start.33 = (bf16[2,64,512]{2,1,0:T(8,128)(2,1)S(1)}, bf16[2,64,512]{2,1,0:T(8,128)(2,1)S(1)}, u32[]{:S(2)}, u32[]{:S(2)}) collective-permute-start(bf16[2,64,512]{2,1,0:T(8,128)(2,1)S(1)} %get-tuple-element.47), channel_id=1, source_target_pairs={{0,16},{1,17},{2,18},{3,19},{4,20},{5,21},{6,22},{7,23},{8,24},{9,... | collective-permute-start | bytes 393224 | tf_op jit(solution)/shard_map/ppermute | solution.py:291
  103.6 10.9 %collective-permute-start.34 = (bf16[2,64,512]{2,1,0:T(8,128)(2,1)S(1)}, bf16[2,64,512]{2,1,0:T(8,128)(2,1)S(1)}, u32[]{:S(2)}, u32[]{:S(2)}) collective-permute-start(bf16[2,64,512]{2,1,0:T(8,128)(2,1)S(1)} %get-tuple-element.48), channel_id=1, source_target_pairs={{0,17},{1,16},{2,19},{3,18},{4,21},{5,20},{6,23},{7,22},{8,25},{9,... | collective-permute-start | bytes 393224 | tf_op jit(solution)/shard_map/ppermute | solution.py:291
  104.3 49.2 %copy-start.20 = (bf16[512,512]{1,0:T(8,128)(2,1)S(1)}, bf16[512,512]{1,0:T(8,128)(2,1)}, u32[]{:S(2)}) copy-start(bf16[512,512]{1,0:T(8,128)(2,1)} %phonon_ref.3) | copy-start | bytes 1572868
  104.3 12.4 %collective-permute-start.35 = (bf16[2,64,512]{2,1,0:T(8,128)(2,1)S(1)}, bf16[2,64,512]{2,1,0:T(8,128)(2,1)S(1)}, u32[]{:S(2)}, u32[]{:S(2)}) collective-permute-start(bf16[2,64,512]{2,1,0:T(8,128)(2,1)S(1)} %get-tuple-element.49), channel_id=1, source_target_pairs={{0,2},{1,3},{2,0},{3,1},{4,6},{5,7},{6,4},{7,5},{8,10},{9,11},{10,... | collective-permute-start | bytes 393224 | tf_op jit(solution)/shard_map/ppermute | solution.py:291
  110.8 18.0 %collective-permute-start.9 = (bf16[4,64,512]{2,1,0:T(8,128)(2,1)S(1)}, bf16[4,64,512]{2,1,0:T(8,128)(2,1)S(1)}, u32[]{:S(2)}, u32[]{:S(2)}) collective-permute-start(bf16[4,64,512]{2,1,0:T(8,128)(2,1)S(1)} %get-tuple-element.30), channel_id=1, source_target_pairs={{0,1},{1,0},{2,3},{3,2},{4,5},{5,4},{6,7},{7,6},{8,9},{9,8},{10,11... | collective-permute-start | bytes 786440 | tf_op jit(solution)/shard_map/ppermute | solution.py:291
  112.5 17.5 %collective-permute-start.10 = (bf16[4,64,512]{2,1,0:T(8,128)(2,1)S(1)}, bf16[4,64,512]{2,1,0:T(8,128)(2,1)S(1)}, u32[]{:S(2)}, u32[]{:S(2)}) collective-permute-start(bf16[4,64,512]{2,1,0:T(8,128)(2,1)S(1)} %get-tuple-element.31), channel_id=1, source_target_pairs={{0,16},{1,17},{2,18},{3,19},{4,20},{5,21},{6,22},{7,23},{8,24},{9,... | collective-permute-start | bytes 786440 | tf_op jit(solution)/shard_map/ppermute | solution.py:291
  113.7 5.8 %collective-permute-start.36 = (bf16[2,64,512]{2,1,0:T(8,128)(2,1)S(1)}, bf16[2,64,512]{2,1,0:T(8,128)(2,1)S(1)}, u32[]{:S(2)}, u32[]{:S(2)}) collective-permute-start(bf16[2,64,512]{2,1,0:T(8,128)(2,1)S(1)} %get-tuple-element.50), channel_id=1, source_target_pairs={{0,3},{1,2},{2,1},{3,0},{4,7},{5,6},{6,5},{7,4},{8,11},{9,10},{10,... | collective-permute-start | bytes 393224 | tf_op jit(solution)/shard_map/ppermute | solution.py:291
  115.2 10.1 %collective-permute-start.37 = (bf16[2,64,512]{2,1,0:T(8,128)(2,1)S(1)}, bf16[2,64,512]{2,1,0:T(8,128)(2,1)S(1)}, u32[]{:S(2)}, u32[]{:S(2)}) collective-permute-start(bf16[2,64,512]{2,1,0:T(8,128)(2,1)S(1)} %get-tuple-element.51), channel_id=1, source_target_pairs={{0,18},{1,19},{2,16},{3,17},{4,22},{5,23},{6,20},{7,21},{8,26},{9,... | collective-permute-start | bytes 393224 | tf_op jit(solution)/shard_map/ppermute | solution.py:291
  117.3 9.2 %collective-permute-start.38 = (bf16[2,64,512]{2,1,0:T(8,128)(2,1)S(1)}, bf16[2,64,512]{2,1,0:T(8,128)(2,1)S(1)}, u32[]{:S(2)}, u32[]{:S(2)}) collective-permute-start(bf16[2,64,512]{2,1,0:T(8,128)(2,1)S(1)} %get-tuple-element.52), channel_id=1, source_target_pairs={{0,19},{1,18},{2,17},{3,16},{4,23},{5,22},{6,21},{7,20},{8,27},{9,... | collective-permute-start | bytes 393224 | tf_op jit(solution)/shard_map/ppermute | solution.py:291
  120.1 11.0 %collective-permute-start.11 = (bf16[4,64,512]{2,1,0:T(8,128)(2,1)}, bf16[4,64,512]{2,1,0:T(8,128)(2,1)S(1)}, u32[]{:S(2)}, u32[]{:S(2)}) collective-permute-start(bf16[4,64,512]{2,1,0:T(8,128)(2,1)} %get-tuple-element.32), channel_id=1, source_target_pairs={{0,17},{1,16},{2,19},{3,18},{4,21},{5,20},{6,23},{7,22},{8,25},{9,... | collective-permute-start | bytes 786440 | tf_op jit(solution)/shard_map/ppermute | solution.py:291
  125.9 20.7 %collective-permute-start.12 = (bf16[4,64,512]{2,1,0:T(8,128)(2,1)}, bf16[4,64,512]{2,1,0:T(8,128)(2,1)S(1)}, u32[]{:S(2)}, u32[]{:S(2)}) collective-permute-start(bf16[4,64,512]{2,1,0:T(8,128)(2,1)} %get-tuple-element.33), channel_id=1, source_target_pairs={{0,2},{1,3},{2,0},{3,1},{4,6},{5,7},{6,4},{7,5},{8,10},{9,11},{10,... | collective-permute-start | bytes 786440 | tf_op jit(solution)/shard_map/ppermute | solution.py:291
  127.2 22.4 %collective-permute-start.13 = (bf16[4,64,512]{2,1,0:T(8,128)(2,1)}, bf16[4,64,512]{2,1,0:T(8,128)(2,1)S(1)}, u32[]{:S(2)}, u32[]{:S(2)}) collective-permute-start(bf16[4,64,512]{2,1,0:T(8,128)(2,1)} %get-tuple-element.34), channel_id=1, source_target_pairs={{0,3},{1,2},{2,1},{3,0},{4,7},{5,6},{6,5},{7,4},{8,11},{9,10},{10,... | collective-permute-start | bytes 786440 | tf_op jit(solution)/shard_map/ppermute | solution.py:291
  128.8 22.6 %collective-permute-start.14 = (bf16[4,64,512]{2,1,0:T(8,128)(2,1)S(1)}, bf16[4,64,512]{2,1,0:T(8,128)(2,1)S(1)}, u32[]{:S(2)}, u32[]{:S(2)}) collective-permute-start(bf16[4,64,512]{2,1,0:T(8,128)(2,1)S(1)} %get-tuple-element.35), channel_id=1, source_target_pairs={{0,18},{1,19},{2,16},{3,17},{4,22},{5,23},{6,20},{7,21},{8,26},{9,... | collective-permute-start | bytes 786440 | tf_op jit(solution)/shard_map/ppermute | solution.py:291
  130.0 23.0 %collective-permute-start.15 = (bf16[4,64,512]{2,1,0:T(8,128)(2,1)S(1)}, bf16[4,64,512]{2,1,0:T(8,128)(2,1)S(1)}, u32[]{:S(2)}, u32[]{:S(2)}) collective-permute-start(bf16[4,64,512]{2,1,0:T(8,128)(2,1)S(1)} %get-tuple-element.36), channel_id=1, source_target_pairs={{0,19},{1,18},{2,17},{3,16},{4,23},{5,22},{6,21},{7,20},{8,27},{9,... | collective-permute-start | bytes 786440 | tf_op jit(solution)/shard_map/ppermute | solution.py:291
  131.1 42.1 %collective-permute-start.27 = (bf16[2,64,512]{2,1,0:T(8,128)(2,1)}, bf16[2,64,512]{2,1,0:T(8,128)(2,1)S(1)}, u32[]{:S(2)}, u32[]{:S(2)}) collective-permute-start(bf16[2,64,512]{2,1,0:T(8,128)(2,1)} %copy-done.29), channel_id=1, source_target_pairs={{0,17},{1,16},{2,19},{3,18},{4,21},{5,20},{6,23},{7,22},{8,25},{9,... | collective-permute-start | bytes 393224 | tf_op jit(solution)/shard_map/ppermute | solution.py:291
  146.6 26.5 %collective-permute-start.28 = (bf16[2,64,512]{2,1,0:T(8,128)(2,1)}, bf16[2,64,512]{2,1,0:T(8,128)(2,1)S(1)}, u32[]{:S(2)}, u32[]{:S(2)}) collective-permute-start(bf16[2,64,512]{2,1,0:T(8,128)(2,1)} %copy-done.26), channel_id=1, source_target_pairs={{0,2},{1,3},{2,0},{3,1},{4,6},{5,7},{6,4},{7,5},{8,10},{9,11},{10,... | collective-permute-start | bytes 393224 | tf_op jit(solution)/shard_map/ppermute | solution.py:291
  149.6 23.5 %collective-permute-start.29 = (bf16[2,64,512]{2,1,0:T(8,128)(2,1)}, bf16[2,64,512]{2,1,0:T(8,128)(2,1)S(1)}, u32[]{:S(2)}, u32[]{:S(2)}) collective-permute-start(bf16[2,64,512]{2,1,0:T(8,128)(2,1)} %copy-done.23), channel_id=1, source_target_pairs={{0,3},{1,2},{2,1},{3,0},{4,7},{5,6},{6,5},{7,4},{8,11},{9,10},{10,... | collective-permute-start | bytes 393224 | tf_op jit(solution)/shard_map/ppermute | solution.py:291
  151.4 21.7 %collective-permute-start.30 = (bf16[2,64,512]{2,1,0:T(8,128)(2,1)}, bf16[2,64,512]{2,1,0:T(8,128)(2,1)S(1)}, u32[]{:S(2)}, u32[]{:S(2)}) collective-permute-start(bf16[2,64,512]{2,1,0:T(8,128)(2,1)} %copy-done.22), channel_id=1, source_target_pairs={{0,18},{1,19},{2,16},{3,17},{4,22},{5,23},{6,20},{7,21},{8,26},{9,... | collective-permute-start | bytes 393224 | tf_op jit(solution)/shard_map/ppermute | solution.py:291
  153.0 20.2 %collective-permute-start.31 = (bf16[2,64,512]{2,1,0:T(8,128)(2,1)}, bf16[2,64,512]{2,1,0:T(8,128)(2,1)S(1)}, u32[]{:S(2)}, u32[]{:S(2)}) collective-permute-start(bf16[2,64,512]{2,1,0:T(8,128)(2,1)} %copy-done.21), channel_id=1, source_target_pairs={{0,19},{1,18},{2,17},{3,16},{4,23},{5,22},{6,21},{7,20},{8,27},{9,... | collective-permute-start | bytes 393224 | tf_op jit(solution)/shard_map/ppermute | solution.py:291
  (40 other events, 241.3 us)

commit v2 on v0

v2 whole, which is shorter than its diff:
```python
import functools

import jax
import jax.numpy as jnp
from jax import lax
from jax.experimental import pallas as pl
from jax.experimental.pallas import tpu as pltpu
from jax.sharding import PartitionSpec as P

NEUMANN = 3
TILE = 16
STEP = 32
CUTS = 2
AXES = ("mom", "en")
SMALL_VMEM = 12 * 1024 * 1024
VMEM_LIMIT = 20 * 1024 * 1024


class Place:
    def __init__(self, local_energies, orbitals):
        self.moms = lax.axis_size("mom")
        self.ens = lax.axis_size("en")
        self.local = local_energies
        self.energies = local_energies * self.ens
        self.reach = -(-(self.energies // 8) // local_energies)
        self.planes = self.ens // (2 * self.reach)
        assert self.planes * 2 * self.reach == self.ens
        self.block = 2 * orbitals // (2 * self.moms)
        units = self.block // STEP
        assert units * STEP == self.block
        sizes = [STEP * (units // CUTS + (i < units % CUTS)) for i in range(CUTS)]
        self.parts = [(sum(sizes[:i]), size) for i, size in enumerate(sizes) if size]
        self.shifts = [(dm, dh) for dh in range(2) for dm in range(self.moms)]

    def here(self):
        n = lax.axis_index("en")
        plane = 2 * self.reach
        return lax.axis_index("mom"), n // plane, (n // self.reach) % 2, n % self.reach

    def index(self, m, z, h, q):
        return m * self.ens + (z * 2 + h) * self.reach + q

    def everyone(self):
        return [
            (m, z, h, q)
            for m in range(self.moms)
            for z in range(self.planes)
            for h in range(2)
            for q in range(self.reach)
        ]

    def target(self, m, h, shift):
        return (m + shift[0]) % self.moms, (h + shift[1]) % 2

    def source(self, m, h, shift):
        return (m - shift[0]) % self.moms, (h + shift[1]) % 2

    def row(self, m, h, part):
        return (m * 2 + h) * self.block + part[0]

    def shift_perm(self, shift):
        pairs = []
        for m, z, h, q in self.everyone():
            tm, th = self.target(m, h, shift)
            pairs.append((self.index(m, z, h, q), self.index(tm, z, th, q)))
        return pairs

    def goes_up(self, z, odd):
        return z % 2 == odd

    def plane_perm(self, odd):
        pairs = []
        for m, z, h, q in self.everyone():
            to = z + 1 if self.goes_up(z, odd) else z - 1
            if 0 <= to < self.planes:
                pairs.append((self.index(m, z, h, q), self.index(m, to, h, q)))
        return pairs

    def swap_perm(self, dq):
        return [
            (self.index(m, z, h, q), self.index(m, z, h, (q + dq) % self.reach))
            for m, z, h, q in self.everyone()
        ]

    def first_energy(self, z, h, q):
        return ((z * 2 + h) * self.reach + q) * self.local


def mix_kernel(place, coupling_ref, shift_ref, offset_ref, here_ref, *outs):
    m, z, h, q = here_ref[0], here_ref[1], here_ref[2], here_ref[3]
    count = len(place.shifts) * place.local
    shape = (place.reach * count, 2 * count)
    row = lax.broadcasted_iota(jnp.int32, shape, 0)
    column = lax.broadcasted_iota(jnp.int32, shape, 1)

    def energy(plane, half, at, of):
        return ((plane * 2 + half) * place.reach + at) * place.local + of % place.local

    shift = (row // place.local) % len(place.shifts)
    target_mom = (m + shift % place.moms) % place.moms
    target_energy = energy(z, (h + shift // place.moms) % 2, (q + row // count) % place.reach, row)
    shift = (column // place.local) % len(place.shifts)
    second = shift // place.moms
    up = (z + second) % 2 == 0
    near = column < count
    plane = jnp.where(near, z, jnp.where(up, z + 1, z - 1))
    half = jnp.where(near, (h + second) % 2, jnp.where(up, 0, 1))
    source_mom = (m + place.moms - shift % place.moms) % place.moms
    source_energy = energy(plane, half, q, column)
    real = (source_energy >= 0) & (source_energy < place.energies)
    apart = jnp.where(real, target_energy - source_energy, 2 * place.energies)
    table = jnp.zeros(shape, jnp.float32)
    for k in range(place.moms):
        here = target_mom == k
        for w in range(offset_ref.shape[0]):
            chosen = here & (source_mom == shift_ref[k, w])
            table += jnp.where(chosen & (apart == offset_ref[w]), coupling_ref[0, k, w], 0.0)
            table += jnp.where(chosen & (apart == -offset_ref[w]), coupling_ref[1, k, w], 0.0)
    table = table.astype(jnp.bfloat16)
    wide = (2 * count, 2 * count * TILE)
    spread = (
        lax.broadcasted_iota(jnp.int32, wide, 0) == lax.broadcasted_iota(jnp.int32, wide, 1) // TILE
    ).astype(jnp.bfloat16)
    tall = (count * TILE, count)
    repeat = (
        lax.broadcasted_iota(jnp.int32, tall, 0) // TILE == lax.broadcasted_iota(jnp.int32, tall, 1)
    ).astype(jnp.bfloat16)
    full = (count * TILE, 2 * count * TILE)
    diagonal = lax.broadcasted_iota(jnp.int32, full, 0) % TILE == lax.broadcasted_iota(jnp.int32, full, 1) % TILE
    for dq, out in enumerate(outs):
        part = table[dq * count : (dq + 1) * count]
        part = jnp.dot(part, spread, preferred_element_type=jnp.float32).astype(jnp.bfloat16)
        part = jnp.dot(repeat, part, preferred_element_type=jnp.float32)
        out[...] = jnp.where(diagonal, part, 0.0).astype(jnp.bfloat16)


def mixing(place, coupling, shift_table, offsets, after):
    count = len(place.shifts) * place.local
    shape = (count * TILE, 2 * count * TILE)
    smem = pl.BlockSpec(memory_space=pltpu.SMEM)

    def kernel(coupling_ref, shift_ref, offset_ref, here_ref, *refs):
        mix_kernel(place, coupling_ref, shift_ref, offset_ref, here_ref, *refs[len(after) :])

    return pl.pallas_call(
        kernel,
        out_shape=[jax.ShapeDtypeStruct(shape, jnp.bfloat16)] * place.reach,
        in_specs=[smem] * 4 + anywhere(after),
        out_specs=[in_vmem()] * place.reach,
        compiler_params=pltpu.CompilerParams(vmem_limit_bytes=2 * SMALL_VMEM),
        cost_estimate=pl.CostEstimate(flops=0, bytes_accessed=0, transcendentals=0),
        name="mixing",
    )(coupling, shift_table, offsets, jnp.stack(place.here()).astype(jnp.int32), *after)


def in_vmem():
    return pl.BlockSpec(memory_space=pltpu.VMEM)


def in_hbm(x):
    return pltpu.with_memory_space_constraint(x, pltpu.HBM)


def anywhere(arrays):
    return [pl.BlockSpec(memory_space=pl.ANY)] * len(arrays)


def cut_kernel(n, sizes, at_ref, green_ref, *refs):
    outs, sems = refs[-n - 1 : -1], refs[-1]
    copies = []
    for k, out in enumerate(outs):
        rows = pl.ds(pl.multiple_of(at_ref[k], STEP), sizes)
        copies.append(pltpu.make_async_copy(green_ref.at[0, :, rows, :], out, sems.at[k]))
    for copy in copies:
        copy.start()
    for copy in copies:
        copy.wait()


def cut_call(place, part, green0, after):
    local, orbitals = place.local, green0.shape[-1]
    m, z, h, q = place.here()
    at = jnp.stack([place.row(*place.target(m, h, shift), part) for shift in place.shifts]).astype(jnp.int32)
    shape = (local, part[1], orbitals)
    n = len(place.shifts)
    return pl.pallas_call(
        functools.partial(cut_kernel, n, part[1]),
        out_shape=[jax.ShapeDtypeStruct(shape, jnp.bfloat16)] * n,
        in_specs=[pl.BlockSpec(memory_space=pltpu.SMEM)] + anywhere([green0, *after]),
        out_specs=[in_vmem()] * n,
        scratch_shapes=[pltpu.SemaphoreType.DMA((n,))],
        compiler_params=pltpu.CompilerParams(vmem_limit_bytes=SMALL_VMEM),
        cost_estimate=pl.CostEstimate(flops=0, bytes_accessed=0, transcendentals=0),
        name="cut",
    )(at, in_hbm(green0), *after)


def halo_kernel(moms, local, which_ref, *refs):
    pieces, out = refs[: 2 * moms], refs[-1]
    for dh in range(2):

        @pl.when(which_ref[0] == dh)
        def _(dh=dh):
            for dm in range(moms):
                out[dm * local : (dm + 1) * local] = pieces[dh * moms + dm][...]


def halo_call(place, odd, pieces, after):
    local, rows, orbitals = pieces[0].shape
    _, z, h, _ = place.here()
    which = (place.goes_up(z, odd) != (h == 1)).astype(jnp.int32).reshape(1)
    return pl.pallas_call(
        functools.partial(halo_kernel, place.moms, local),
        out_shape=jax.ShapeDtypeStruct((place.moms * local, rows, orbitals), jnp.bfloat16),
        in_specs=[pl.BlockSpec(memory_space=pltpu.SMEM)] + [in_vmem()] * len(pieces) + anywhere(after),
        out_specs=in_vmem(),
        compiler_params=pltpu.CompilerParams(vmem_limit_bytes=SMALL_VMEM),
        cost_estimate=pl.CostEstimate(flops=0, bytes_accessed=0, transcendentals=0),
        name="halo",
    )(which, *pieces, *after)


def smooth_kernel(n_in, n_add, splits, mix_ref, *refs):
    inputs, addends, outs = refs[:n_in], refs[n_in : n_in + n_add], refs[-len(splits) :]
    size, width = inputs[0].shape[-2:]
    for at in range(0, size, TILE):
        rows = slice(at, at + TILE)
        stacked = jnp.concatenate([r[:, rows].reshape(-1, width) for r in inputs], axis=0)
        mixed = jnp.dot(mix_ref[...], stacked, preferred_element_type=jnp.float32)
        for r in addends:
            mixed += r[:, rows].reshape(-1, width).astype(jnp.float32)
        mixed = mixed.astype(jnp.bfloat16).reshape(-1, TILE, width)
        for out, (first, last) in zip(outs, splits, strict=True):
            out[:, rows] = mixed[first:last]


def smooth_call(part, mix, inputs, addends, splits, after):
    size, orbitals = inputs[0].shape[1:]
    counts = [last - first for first, last in splits]
    return pl.pallas_call(
        functools.partial(smooth_kernel, len(inputs), len(addends), splits),
        out_shape=[jax.ShapeDtypeStruct((count, size, orbitals), jnp.bfloat16) for count in counts],
        in_specs=[in_vmem()] * (1 + len(inputs) + len(addends)) + anywhere(after),
        out_specs=[in_vmem()] * len(counts),
        compiler_params=pltpu.CompilerParams(vmem_limit_bytes=SMALL_VMEM),
        cost_estimate=pl.CostEstimate(flops=0, bytes_accessed=0, transcendentals=0),
        name="smooth",
    )(mix, *inputs, *addends, *after)


def dyson_kernel(pieces, row_ref, green_ref, phonon_ref, *refs):
    out_ref, energy, left, series = refs[-4:]
    size = phonon_ref.shape[0]
    low, high = slice(0, size), slice(size, 2 * size)

    def as_left(re, im):
        left[low, low] = re
        left[high, high] = re
        left[low, high] = -im
        left[high, low] = im

    for k, rows in enumerate(pieces):
        at = pl.multiple_of(row_ref[k], STEP)
        scale = phonon_ref[pl.ds(pl.multiple_of(row_ref[len(pieces) + k], STEP), rows), :].astype(jnp.float32)
        value = refs[k][0].astype(jnp.float32)
        energy[pl.ds(at, rows), :] = (scale * value).astype(jnp.bfloat16)
    as_left(green_ref[0, 0, 0], green_ref[0, 0, 1])
    product = jnp.dot(left[...], energy[...], preferred_element_type=jnp.float32)
    product = (product * (1.0 / size)).astype(jnp.bfloat16)
    as_left(product[low], product[high])
    green = green_ref[0, 0].reshape(2 * size, size)
    last = green
    for step in range(NEUMANN):
        added = green.astype(jnp.float32) + jnp.dot(left[...], last, preferred_element_type=jnp.float32)
        if step < NEUMANN - 1:
            series[...] = added.astype(jnp.bfloat16)
            last = series[...]
        else:
            out_ref[0, 0] = added.astype(jnp.bfloat16).reshape(2, size, size)


def dyson_call(place, green0, phonon_me, pieces, first, last, out):
    size = green0.shape[-1]
    m, z, h, q = place.here()
    at = jnp.stack([place.row(*place.source(m, h, shift), part) for part, shift, _, _ in pieces]).astype(jnp.int32)
    block = pl.BlockSpec((1, 1, 2, size, size), lambda e, t: (0, first + e, 0, 0, 0))
    specs = [block, pl.BlockSpec((size, size), lambda e, t: (0, 0))]
    for part, _, _, whole in pieces:
        start = first if whole else 0
        specs.append(pl.BlockSpec((1, part[1], size), lambda e, t, start=start: (start + e, 0, 0)))
    args = [jnp.concatenate([at, at % size]), in_hbm(green0), phonon_me] + [x for _, _, x, _ in pieces]
    aliases = {}
    if out is not None:
        aliases = {len(args): 0}
        args.append(out)
        specs.append(pl.BlockSpec(memory_space=pl.ANY))
    count = last - first
    return pl.pallas_call(
        functools.partial(dyson_kernel, [part[1] for part, _, _, _ in pieces]),
        out_shape=jax.ShapeDtypeStruct(green0.shape, green0.dtype),
        grid_spec=pltpu.PrefetchScalarGridSpec(
            num_scalar_prefetch=1,
            grid=(count,),
            in_specs=specs,
            out_specs=block,
            scratch_shapes=[
                pltpu.VMEM((2 * size, size), jnp.bfloat16),
                pltpu.VMEM((2 * size, 2 * size), jnp.bfloat16),
                pltpu.VMEM((2 * size, size), jnp.bfloat16),
            ],
        ),
        input_output_aliases=aliases,
        compiler_params=pltpu.CompilerParams(vmem_limit_bytes=VMEM_LIMIT),
        cost_estimate=pl.CostEstimate(flops=0, bytes_accessed=0, transcendentals=0),
        name="dyson",
    )(*args)


def per_device(green0, phonon_me, coupling, shift_table, offsets):
    local, orbitals = green0.shape[1], green0.shape[3]
    place = Place(local, orbitals)
    m, z, h, q = place.here()
    flat = green0.reshape(1, local, 2 * orbitals, orbitals)
    groups = ((0, local // 2), (local // 2, local))
    stay = place.shifts[0]
    last_made = []

    def cut_and_send(part):
        mine = cut_call(place, part, flat, last_made)
        last_made[:] = [mine[0]]
        return [
            piece if shift == stay else lax.ppermute(piece, AXES, place.shift_perm(shift))
            for shift, piece in zip(place.shifts, mine, strict=True)
        ]

    def send_halos(mine):
        halos = []
        for odd in range(2):
            halo = halo_call(place, odd, mine, last_made)
            last_made[:] = [halo]
            halos.append(lax.ppermute(halo, AXES, place.plane_perm(odd)))
        return list(mine) + halos

    count = len(place.shifts) * local
    back = [[] for _ in groups]

    def partial_sums(part, inputs):
        addends = []
        for dq in range(1, place.reach):
            (sums,) = smooth_call(part, mix[dq], inputs, [], [(0, count)], last_made)
            last_made[:] = [sums]
            addends.append(lax.ppermute(sums, AXES, place.swap_perm(dq)))
        return addends

    def send_back(part, inputs, addends):
        apart = part == place.parts[-1]
        cut = groups if apart else ((0, local),)
        splits = [(i * local + first, i * local + last) for first, last in cut for i in range(len(place.shifts))]
        mixed = smooth_call(part, mix[0], inputs, addends, splits, last_made)
        last_made[:] = [mixed[0]]
        for s in range(len(cut)):
            for i, shift in enumerate(place.shifts):
                piece = mixed[s * len(place.shifts) + i]
                if shift != stay:
                    piece = lax.ppermute(piece, AXES, place.shift_perm(shift))
                for g in range(len(groups)):
                    if g == s or not apart:
                        back[g].append((part, shift, piece, not apart))
        return [back[0][k - len(place.shifts)][2] for k in range(1, len(place.shifts))]

    parts = place.parts
    pieces = [cut_and_send(part) for part in parts]
    mix = mixing(place, coupling, shift_table, offsets, last_made)
    last_made[:] = [mix[0]]
    inputs = [send_halos(mine) for mine in pieces]
    sent = []
    for part, mine in zip(parts, inputs, strict=True):
        last_made += sent
        addends = partial_sums(part, mine)
        sent = send_back(part, mine, addends)
    out = None
    for (first, last), arrived in zip(groups, back, strict=True):
        out = dyson_call(place, green0, phonon_me, arrived, first, last, out)
    return out


def solution(mesh):
    in_specs = (P("mom", "en", None, None, None), P(), P(), P(), P())
    out_specs = P("mom", "en", None, None, None)
    return jax.shard_map(
        per_device, mesh=mesh, in_specs=in_specs, out_specs=out_specs, check_vma=False
    )
```

time: 284 us -> 145 us (0.51)
  waiting for transfers between devices: 179 us -> 76.6 us
  matrix products: 40.9 us -> 0 us
  Pallas kernels: 0 us -> 37.6 us
  local copies, waits for them, and re-layouts: 38.4 us -> 3.51 us
  starting transfers between devices: 11.2 us -> 26.9 us
  other arithmetic: 13.8 us -> 0.24 us
    all_to_all x2 -> x0, waiting for transfers between devices: 179 us -> none  [the longest x1 94.1 us: per_device(): lax.all_to_all(spread, ('mom', 'en'), split_axis=3, concat_axis=0, tiled=...]
    ppermute x0 -> x21, waiting for transfers between devices: none -> 76.6 us  [the longest x6 40.6 us: cut_and_send(): lax.ppermute(piece, AXES, place.shift_perm(shift))]
    dot_general x11 -> x0, matrix products: 40.9 us -> none  [the longest x3 15.2 us: per_device(): jnp.einsum('eij,ejk->eik', transfer, stacked_imag, preferred_element_type...]
    pallas_call x0 -> x13, Pallas kernels: none -> 37.6 us  [the longest x2 25 us: dyson_call(): pl.pallas_call(functools.partial(dyson_kernel, [part[1] for part, _, _, _...]
    ppermute x0 -> x21, starting transfers between devices: none -> 26.9 us  [the longest x9 10.6 us: send_back(): piece = lax.ppermute(piece, AXES, place.shift_perm(shift))]
    convert_element_type x2 -> x0, other arithmetic: 11.3 us -> none  [the longest x1 6.63 us: per_device(): smooth_all.astype(jnp.float32)]
    all_to_all x2 -> x0, starting transfers between devices: 11.2 us -> none  [the longest x1 7.43 us: per_device(): lax.all_to_all(spread, ('mom', 'en'), split_axis=3, concat_axis=0, tiled=...]
    convert_element_type x2 -> x0, local copies, waits for them, and re-layouts: 10.1 us -> none  [the longest x1 9.89 us: per_device(): smooth_all.astype(jnp.float32)]
  transfers between devices with their start and end apart: 2 -> 21, of which waited for: 2 -> 11; matrix products, arithmetic and copies ran while one was open for 3% -> 0% of each run, Pallas kernels for 0% -> 12%
where the time goes in v2:
time: 145 us
  waiting for transfers between devices  76.6 us (53%)
  Pallas kernels  37.6 us (26%)
  starting transfers between devices  26.9 us (19%)
  local copies, waits for them, and re-layouts  3.51 us (2%)
    ppermute x6, waiting for transfers between devices, cut_and_send(): lax.ppermute(piece, AXES, place.shift_perm(shift))  40.6 us
    pallas_call x2, Pallas kernels, dyson_call(): pl.pallas_call(functools.partial(dyson_kernel, [part[1] for part, _, _, _...  25 us
    ppermute x4, waiting for transfers between devices, send_halos(): halos.append(lax.ppermute(halo, AXES, place.plane_perm(odd)))  17.6 us
    ppermute x9, waiting for transfers between devices, send_back(): piece = lax.ppermute(piece, AXES, place.shift_perm(shift))  13.1 us
    ppermute x9, starting transfers between devices, send_back(): piece = lax.ppermute(piece, AXES, place.shift_perm(shift))  10.6 us
    ppermute x4, starting transfers between devices, send_halos(): halos.append(lax.ppermute(halo, AXES, place.plane_perm(odd)))  8.1 us
    ppermute x6, starting transfers between devices, cut_and_send(): lax.ppermute(piece, AXES, place.shift_perm(shift))  8.03 us
    pallas_call x4, Pallas kernels, smooth_call(): pl.pallas_call(functools.partial(smooth_kernel, len(inputs), len(addends)...  6.05 us
  transfers between devices with their start and end apart: 21, of which 11 were waited for; matrix products, arithmetic and copies ran while one was open for 0% of the time, Pallas kernels for 12%

profile of v2, /device:TPU:0, one launch (start us, length us, event | category | flops | bytes accessed | tf_op | source)
XLA Modules:
  0.0 145.0 jit_solution(10816012589002157459)
XLA Ops:
  0.0 0.1 pad_add_fusion.2.at_ref
  0.1 2.9 %cut.2 = (bf16[4,128,512]{2,1,0:T(8,128)(2,1)S(1)}, bf16[4,128,512]{2,1,0:T(8,128)(2,1)}, bf16[4,128,512]{2,1,0:T(8,128)(2,1)S(1)}, bf16[4,128,512]{2,1,0:T(8,128)(2,1)S(1)}) custom-call(s32[4]{0:T(128)S(1)} %pad_add_fusion.2.at_ref, bf16[1,4,1024,512]{3,2,1,0:T(8,128)(2,1)} %bitcast.19), custom_call_target="tpu_custom_call" | custom-call | tf_op jit(solution)/shard_map/cut/pallas_call | solution.py:186
  3.0 3.0 %collective-permute-start = (bf16[4,128,512]{2,1,0:T(8,128)(2,1)}, bf16[4,128,512]{2,1,0:T(8,128)(2,1)S(1)}, u32[]{:S(2)}, u32[]{:S(2)}) collective-permute-start(bf16[4,128,512]{2,1,0:T(8,128)(2,1)} %get-tuple-element.30), channel_id=1, source_target_pairs={{0,16},{1,17},{2,18},{3,19},{4,20},{5,21},{6,22},{7,23},{8,24},{9,... | collective-permute-start | bytes 1572872 | tf_op jit(solution)/shard_map/ppermute | solution.py:332
  6.0 1.5 %collective-permute-start.1 = (bf16[4,128,512]{2,1,0:T(8,128)(2,1)S(1)}, bf16[4,128,512]{2,1,0:T(8,128)(2,1)S(1)}, u32[]{:S(2)}, u32[]{:S(2)}) collective-permute-start(bf16[4,128,512]{2,1,0:T(8,128)(2,1)S(1)} %get-tuple-element.31), channel_id=1, source_target_pairs={{0,2},{1,3},{2,0},{3,1},{4,6},{5,7},{6,4},{7,5},{8,10},{9,11},{10,... | collective-permute-start | bytes 1572872 | tf_op jit(solution)/shard_map/ppermute | solution.py:332
  7.6 2.1 %cut.3 = (bf16[4,128,512]{2,1,0:T(8,128)(2,1)S(1)}, bf16[4,128,512]{2,1,0:T(8,128)(2,1)S(1)}, bf16[4,128,512]{2,1,0:T(8,128)(2,1)S(1)}, bf16[4,128,512]{2,1,0:T(8,128)(2,1)S(1)}) custom-call(s32[4]{0:T(128)S(1)} %pad_add_fusion.1.at_ref, bf16[1,4,1024,512]{3,2,1,0:T(8,128)(2,1)} %bitcast.20, bf16[4,128,512]{2,1,0:T(8,128)(2,1)S(1)} %get-tuple-element.27.refs_0_), custom_call_target="tpu_custom_call" | custom-call | tf_op jit(solution)/shard_map/cut/pallas_call | solution.py:186
  9.7 0.1 pad_add_fusion.here_ref
  9.8 1.3 mixing.1
  11.1 7.8 %collective-permute-done.refs_1_ = bf16[4,128,512]{2,1,0:T(8,128)(2,1)S(1)} collective-permute-done((bf16[4,128,512]{2,1,0:T(8,128)(2,1)}, bf16[4,128,512]{2,1,0:T(8,128)(2,1)S(1)}, u32[]{:S(2)}, u32[]{:S(2)}) %collective-permute-start) | collective-permute-done | bytes 524320 | tf_op jit(solution)/shard_map/ppermute | solution.py:332
  18.9 10.7 %collective-permute-done.1.refs_2_ = bf16[4,128,512]{2,1,0:T(8,128)(2,1)S(1)} collective-permute-done((bf16[4,128,512]{2,1,0:T(8,128)(2,1)S(1)}, bf16[4,128,512]{2,1,0:T(8,128)(2,1)S(1)}, u32[]{:S(2)}, u32[]{:S(2)}) %collective-permute-start.1) | collective-permute-done | bytes 524320 | tf_op jit(solution)/shard_map/ppermute | solution.py:332
  29.6 1.0 collective-permute-done.2.refs_3_
  30.7 0.1 halo.5.refs_4_
  30.8 0.7 collective-permute-start.4
  31.5 4.4 %collective-permute-start.3 = (bf16[8,128,512]{2,1,0:T(8,128)(2,1)S(1)}, bf16[8,128,512]{2,1,0:T(8,128)(2,1)S(1)}, u32[]{:S(2)}, u32[]{:S(2)}) collective-permute-start(bf16[8,128,512]{2,1,0:T(8,128)(2,1)S(1)} %halo.4.refs_4_), channel_id=1, source_target_pairs={{0,4},{1,5},{2,6},{3,7},{4,0},{5,1},{6,2},{7,3},{8,12},{9,13},{10,... | collective-permute-start | bytes 3145736 | tf_op jit(solution)/shard_map/ppermute | solution.py:341
  35.9 1.4 collective-permute-start.5
  37.3 0.6 collective-permute-start.6
  38.0 1.4 collective-permute-start.7
  39.4 11.4 %collective-permute-done.5.refs_1_ = bf16[4,128,512]{2,1,0:T(8,128)(2,1)S(1)} collective-permute-done((bf16[4,128,512]{2,1,0:T(8,128)(2,1)S(1)}, bf16[4,128,512]{2,1,0:T(8,128)(2,1)S(1)}, u32[]{:S(2)}, u32[]{:S(2)}) %collective-permute-start.5) | collective-permute-done | bytes 524320 | tf_op jit(solution)/shard_map/ppermute | solution.py:332
  50.8 9.8 %collective-permute-done.6.refs_2_ = bf16[4,128,512]{2,1,0:T(8,128)(2,1)S(1)} collective-permute-done((bf16[4,128,512]{2,1,0:T(8,128)(2,1)S(1)}, bf16[4,128,512]{2,1,0:T(8,128)(2,1)S(1)}, u32[]{:S(2)}, u32[]{:S(2)}) %collective-permute-start.6) | collective-permute-done | bytes 524320 | tf_op jit(solution)/shard_map/ppermute | solution.py:332
  60.6 0.1 halo.7.refs_6_
  60.7 1.3 smooth.4.refs_7_
  62.1 0.9 collective-permute-start.13
  63.0 2.1 %collective-permute-start.12 = (bf16[8,128,512]{2,1,0:T(8,128)(2,1)S(1)}, bf16[8,128,512]{2,1,0:T(8,128)(2,1)S(1)}, u32[]{:S(2)}, u32[]{:S(2)}) collective-permute-start(bf16[8,128,512]{2,1,0:T(8,128)(2,1)S(1)} %halo.6.refs_4_), channel_id=1, source_target_pairs={{0,4},{1,5},{2,6},{3,7},{4,0},{5,1},{6,2},{7,3},{8,12},{9,13},{10,... | collective-permute-start | bytes 3145736 | tf_op jit(solution)/shard_map/ppermute | solution.py:341
  65.0 1.2 collective-permute-done.8.refs_6_
  66.2 1.3 smooth.5
  67.5 0.6 collective-permute-start.9
  68.1 1.2 collective-permute-start.10
  69.3 1.7 %collective-permute-start.11 = (bf16[4,128,512]{2,1,0:T(8,128)(2,1)S(1)}, bf16[4,128,512]{2,1,0:T(8,128)(2,1)S(1)}, u32[]{:S(2)}, u32[]{:S(2)}) collective-permute-start(bf16[4,128,512]{2,1,0:T(8,128)(2,1)S(1)} %get-tuple-element.40), channel_id=1, source_target_pairs={{0,18},{1,19},{2,16},{3,17},{4,22},{5,23},{6,20},{7,21},{8,26},{9,... | collective-permute-start | bytes 1572872 | tf_op jit(solution)/shard_map/ppermute | solution.py:365
  71.0 17.6 %collective-permute-done.12.refs_4_ = bf16[8,128,512]{2,1,0:T(8,128)(2,1)S(1)} collective-permute-done((bf16[8,128,512]{2,1,0:T(8,128)(2,1)S(1)}, bf16[8,128,512]{2,1,0:T(8,128)(2,1)S(1)}, u32[]{:S(2)}, u32[]{:S(2)}) %collective-permute-start.12) | collective-permute-done | bytes 1048608 | tf_op jit(solution)/shard_map/ppermute | solution.py:341
  88.6 4.4 %collective-permute-done.10.refs_8_.refs_2_ = bf16[4,128,512]{2,1,0:T(8,128)(2,1)S(1)} collective-permute-done((bf16[4,128,512]{2,1,0:T(8,128)(2,1)S(1)}, bf16[4,128,512]{2,1,0:T(8,128)(2,1)S(1)}, u32[]{:S(2)}, u32[]{:S(2)}) %collective-permute-start.10) | collective-permute-done | bytes 524320 | tf_op jit(solution)/shard_map/ppermute | solution.py:365
  93.0 1.3 smooth.6.refs_7_
  94.3 4.1 %collective-permute-done.14.refs_6_ = bf16[16,128,512]{2,1,0:T(8,128)(2,1)S(1)} collective-permute-done((bf16[16,128,512]{2,1,0:T(8,128)(2,1)S(1)}, bf16[16,128,512]{2,1,0:T(8,128)(2,1)S(1)}, u32[]{:S(2)}, u32[]{:S(2)}) %collective-permute-start.14) | collective-permute-done | bytes 2097184 | tf_op jit(solution)/shard_map/ppermute | solution.py:352
  98.5 2.3 %smooth.7 = (bf16[2,128,512]{2,1,0:T(8,128)(2,1)S(1)}, bf16[2,128,512]{2,1,0:T(8,128)(2,1)S(1)}, bf16[2,128,512]{2,1,0:T(8,128)(2,1)}, bf16[2,128,512]{2,1,0:T(8...) custom-call(bf16[256,512]{1,0:T(8,128)(2,1)S(1)} %get-tuple-element., ...), custom_call_target="tpu_custom_call" | custom-call | tf_op jit(solution)/shard_map/smooth/pallas_call | solution.py:240
  100.8 0.7 copy-done.1
  101.5 1.5 %collective-permute-start.18 = (bf16[2,128,512]{2,1,0:T(8,128)(2,1)S(1)}, bf16[2,128,512]{2,1,0:T(8,128)(2,1)S(1)}, u32[]{:S(2)}, u32[]{:S(2)}) collective-permute-start(bf16[2,128,512]{2,1,0:T(8,128)(2,1)S(1)} %get-tuple-element.46), channel_id=1, source_target_pairs={{0,16},{1,17},{2,18},{3,19},{4,20},{5,21},{6,22},{7,23},{8,24},{9,... | collective-permute-start | bytes 786440 | tf_op jit(solution)/shard_map/ppermute | solution.py:365
  103.0 0.6 collective-permute-start.19
  103.6 1.4 collective-permute-start.20
  105.0 1.5 %collective-permute-start.15 = (bf16[2,128,512]{2,1,0:T(8,128)(2,1)}, bf16[2,128,512]{2,1,0:T(8,128)(2,1)S(1)}, u32[]{:S(2)}, u32[]{:S(2)}) collective-permute-start(bf16[2,128,512]{2,1,0:T(8,128)(2,1)} %get-tuple-element.42), channel_id=1, source_target_pairs={{0,16},{1,17},{2,18},{3,19},{4,20},{5,21},{6,22},{7,23},{8,24},{9,... | collective-permute-start | bytes 786440 | tf_op jit(solution)/shard_map/ppermute | solution.py:365
  106.5 0.6 collective-permute-start.16
  107.0 3.6 %collective-permute-done.18.refs_5_ = bf16[2,128,512]{2,1,0:T(8,128)(2,1)S(1)} collective-permute-done((bf16[2,128,512]{2,1,0:T(8,128)(2,1)S(1)}, bf16[2,128,512]{2,1,0:T(8,128)(2,1)S(1)}, u32[]{:S(2)}, u32[]{:S(2)}) %collective-permute-start.18) | collective-permute-done | bytes 262176 | tf_op jit(solution)/shard_map/ppermute | solution.py:365
  110.6 0.7 copy-done.3
  111.3 1.5 %collective-permute-start.17 = (bf16[2,128,512]{2,1,0:T(8,128)(2,1)}, bf16[2,128,512]{2,1,0:T(8,128)(2,1)}, u32[]{:S(2)}, u32[]{:S(2)}) collective-permute-start(bf16[2,128,512]{2,1,0:T(8,128)(2,1)} %get-tuple-element.44), channel_id=1, source_target_pairs={{0,18},{1,19},{2,16},{3,17},{4,22},{5,23},{6,20},{7,21},{8,26},{9,... | collective-permute-start | bytes 786440 | tf_op jit(solution)/shard_map/ppermute | solution.py:365
  112.8 0.1 stack.81
  112.9 0.1 concatenate.6.row_ref
  113.0 5.1 %collective-permute-done.19.refs_6_ = bf16[2,128,512]{2,1,0:T(8,128)(2,1)} collective-permute-done((bf16[2,128,512]{2,1,0:T(8,128)(2,1)}, bf16[2,128,512]{2,1,0:T(8,128)(2,1)}, u32[]{:S(2)}, u32[]{:S(2)}) %collective-permute-start.19) | collective-permute-done | bytes 262176 | tf_op jit(solution)/shard_map/ppermute | solution.py:365
  118.1 0.9 copy-done.2
  119.1 0.9 copy-done.4
  120.0 12.5 %dyson.2.refs_8_ = bf16[1,4,2,512,512]{4,3,2,1,0:T(8,128)(2,1)} custom-call(s32[16]{0:T(128)S(1)} %concatenate.6.row_ref, bf16[1,4,2,512,512]{4,3,2,1,0:T(8,128)(2,1)} %green_ref.3, bf16[512,512]{1,0:T(8,128)(2,1)S(1)} %copy-done, bf16[4,128,512]{2,1,0:T(8,128)(2,1)S(1)} %get-tuple-element.37.refs_6_.refs_0_, ...), custom_call_target="tpu_custom_call" | custom-call | tf_op jit(solution)/shard_map/dyson/pallas_call | solution.py:298
  132.5 12.5 %dyson.3 = bf16[1,4,2,512,512]{4,3,2,1,0:T(8,128)(2,1)} custom-call(s32[16]{0:T(128)S(1)} %concatenate.6.row_ref, bf16[1,4,2,512,512]{4,3,2,1,0:T(8,128)(2,1)} %green_ref.3, bf16[512,512]{1,0:T(8,128)(2,1)S(1)} %copy-done, bf16[4,128,512]{2,1,0:T(8,128)(2,1)S(1)} %get-tuple-element.37.refs_6_.refs_0_, ...), custom_call_target="tpu_custom_call", output_to_operand_aliasing={{}: (11, {})} | custom-call | tf_op jit(solution)/shard_map/dyson/pallas_call | solution.py:298
  (29 shorter events, 0.4 us)
Async XLA Ops:
  3.0 16.0 %collective-permute-start = (bf16[4,128,512]{2,1,0:T(8,128)(2,1)}, bf16[4,128,512]{2,1,0:T(8,128)(2,1)S(1)}, u32[]{:S(2)}, u32[]{:S(2)}) collective-permute-start(bf16[4,128,512]{2,1,0:T(8,128)(2,1)} %get-tuple-element.30), channel_id=1, source_target_pairs={{0,16},{1,17},{2,18},{3,19},{4,20},{5,21},{6,22},{7,23},{8,24},{9,... | collective-permute-start | bytes 1572872 | tf_op jit(solution)/shard_map/ppermute | solution.py:332
  6.0 23.7 %collective-permute-start.1 = (bf16[4,128,512]{2,1,0:T(8,128)(2,1)S(1)}, bf16[4,128,512]{2,1,0:T(8,128)(2,1)S(1)}, u32[]{:S(2)}, u32[]{:S(2)}) collective-permute-start(bf16[4,128,512]{2,1,0:T(8,128)(2,1)S(1)} %get-tuple-element.31), channel_id=1, source_target_pairs={{0,2},{1,3},{2,0},{3,1},{4,6},{5,7},{6,4},{7,5},{8,10},{9,11},{10,... | collective-permute-start | bytes 1572872 | tf_op jit(solution)/shard_map/ppermute | solution.py:332
  7.5 23.1 %collective-permute-start.2 = (bf16[4,128,512]{2,1,0:T(8,128)(2,1)S(1)}, bf16[4,128,512]{2,1,0:T(8,128)(2,1)S(1)}, u32[]{:S(2)}, u32[]{:S(2)}) collective-permute-start(bf16[4,128,512]{2,1,0:T(8,128)(2,1)S(1)} %get-tuple-element.32), channel_id=1, source_target_pairs={{0,18},{1,19},{2,16},{3,17},{4,22},{5,23},{6,20},{7,21},{8,26},{9,... | collective-permute-start | bytes 1572872 | tf_op jit(solution)/shard_map/ppermute | solution.py:332
  7.6 2.2 %copy-start.5 = (f32[2,2,16]{2,1,0:T(2,128)S(1)}, f32[2,2,16]{2,1,0:T(2,128)}, u32[]{:S(2)}) copy-start(f32[2,2,16]{2,1,0:T(2,128)} %coupling_ref.1) | copy-start | bytes 772
  7.6 2.2 %copy-start.6 = (s32[2,16]{1,0:T(2,128)S(1)}, s32[2,16]{1,0:T(2,128)}, u32[]{:S(2)}) copy-start(s32[2,16]{1,0:T(2,128)} %shift_ref.1) | copy-start | bytes 388
  7.6 2.2 %copy-start.7 = (s32[16]{0:T(128)S(1)}, s32[16]{0:T(128)}, u32[]{:S(2)}) copy-start(s32[16]{0:T(128)} %offset_ref.1) | copy-start | bytes 196
  30.8 29.9 %collective-permute-start.4 = (bf16[8,128,512]{2,1,0:T(8,128)(2,1)S(1)}, bf16[8,128,512]{2,1,0:T(8,128)(2,1)S(1)}, u32[]{:S(2)}, u32[]{:S(2)}) collective-permute-start(bf16[8,128,512]{2,1,0:T(8,128)(2,1)S(1)} %halo.5.refs_4_), channel_id=1, source_target_pairs={{4,8},{5,9},{6,10},{7,11},{8,4},{9,5},{10,6},{11,7},{20,24},{21,25... | collective-permute-start | bytes 3145736 | tf_op jit(solution)/shard_map/ppermute | solution.py:341
  31.5 29.2 %collective-permute-start.3 = (bf16[8,128,512]{2,1,0:T(8,128)(2,1)S(1)}, bf16[8,128,512]{2,1,0:T(8,128)(2,1)S(1)}, u32[]{:S(2)}, u32[]{:S(2)}) collective-permute-start(bf16[8,128,512]{2,1,0:T(8,128)(2,1)S(1)} %halo.4.refs_4_), channel_id=1, source_target_pairs={{0,4},{1,5},{2,6},{3,7},{4,0},{5,1},{6,2},{7,3},{8,12},{9,13},{10,... | collective-permute-start | bytes 3145736 | tf_op jit(solution)/shard_map/ppermute | solution.py:341
  35.9 14.9 %collective-permute-start.5 = (bf16[4,128,512]{2,1,0:T(8,128)(2,1)S(1)}, bf16[4,128,512]{2,1,0:T(8,128)(2,1)S(1)}, u32[]{:S(2)}, u32[]{:S(2)}) collective-permute-start(bf16[4,128,512]{2,1,0:T(8,128)(2,1)S(1)} %get-tuple-element.34), channel_id=1, source_target_pairs={{0,16},{1,17},{2,18},{3,19},{4,20},{5,21},{6,22},{7,23},{8,24},{9,... | collective-permute-start | bytes 1572872 | tf_op jit(solution)/shard_map/ppermute | solution.py:332
  37.3 23.2 %collective-permute-start.6 = (bf16[4,128,512]{2,1,0:T(8,128)(2,1)S(1)}, bf16[4,128,512]{2,1,0:T(8,128)(2,1)S(1)}, u32[]{:S(2)}, u32[]{:S(2)}) collective-permute-start(bf16[4,128,512]{2,1,0:T(8,128)(2,1)S(1)} %get-tuple-element.35), channel_id=1, source_target_pairs={{0,2},{1,3},{2,0},{3,1},{4,6},{5,7},{6,4},{7,5},{8,10},{9,11},{10,... | collective-permute-start | bytes 1572872 | tf_op jit(solution)/shard_map/ppermute | solution.py:332
  38.0 22.6 %collective-permute-start.7 = (bf16[4,128,512]{2,1,0:T(8,128)(2,1)S(1)}, bf16[4,128,512]{2,1,0:T(8,128)(2,1)S(1)}, u32[]{:S(2)}, u32[]{:S(2)}) collective-permute-start(bf16[4,128,512]{2,1,0:T(8,128)(2,1)S(1)} %get-tuple-element.36), channel_id=1, source_target_pairs={{0,18},{1,19},{2,16},{3,17},{4,22},{5,23},{6,20},{7,21},{8,26},{9,... | collective-permute-start | bytes 1572872 | tf_op jit(solution)/shard_map/ppermute | solution.py:332
  62.0 4.2 %collective-permute-start.8 = (bf16[16,128,512]{2,1,0:T(8,128)(2,1)S(1)}, bf16[16,128,512]{2,1,0:T(8,128)(2,1)S(1)}, u32[]{:S(2)}, u32[]{:S(2)}) collective-permute-start(bf16[16,128,512]{2,1,0:T(8,128)(2,1)S(1)} %smooth.4.refs_7_), channel_id=1, source_target_pairs={{0,1},{1,0},{2,3},{3,2},{4,5},{5,4},{6,7},{7,6},{8,9},{9,8},{10,11... | collective-permute-start | bytes 6291464 | tf_op jit(solution)/shard_map/ppermute | solution.py:352
  62.1 9.0 %collective-permute-start.13 = (bf16[8,128,512]{2,1,0:T(8,128)(2,1)S(1)}, bf16[8,128,512]{2,1,0:T(8,128)(2,1)S(1)}, u32[]{:S(2)}, u32[]{:S(2)}) collective-permute-start(bf16[8,128,512]{2,1,0:T(8,128)(2,1)S(1)} %halo.7.refs_6_), channel_id=1, source_target_pairs={{4,8},{5,9},{6,10},{7,11},{8,4},{9,5},{10,6},{11,7},{20,24},{21,25... | collective-permute-start | bytes 3145736 | tf_op jit(solution)/shard_map/ppermute | solution.py:341
  63.0 25.6 %collective-permute-start.12 = (bf16[8,128,512]{2,1,0:T(8,128)(2,1)S(1)}, bf16[8,128,512]{2,1,0:T(8,128)(2,1)S(1)}, u32[]{:S(2)}, u32[]{:S(2)}) collective-permute-start(bf16[8,128,512]{2,1,0:T(8,128)(2,1)S(1)} %halo.6.refs_4_), channel_id=1, source_target_pairs={{0,4},{1,5},{2,6},{3,7},{4,0},{5,1},{6,2},{7,3},{8,12},{9,13},{10,... | collective-permute-start | bytes 3145736 | tf_op jit(solution)/shard_map/ppermute | solution.py:341
  67.5 21.1 %collective-permute-start.9 = (bf16[4,128,512]{2,1,0:T(8,128)(2,1)S(1)}, bf16[4,128,512]{2,1,0:T(8,128)(2,1)S(1)}, u32[]{:S(2)}, u32[]{:S(2)}) collective-permute-start(bf16[4,128,512]{2,1,0:T(8,128)(2,1)S(1)} %get-tuple-element.38), channel_id=1, source_target_pairs={{0,16},{1,17},{2,18},{3,19},{4,20},{5,21},{6,22},{7,23},{8,24},{9,... | collective-permute-start | bytes 1572872 | tf_op jit(solution)/shard_map/ppermute | solution.py:365
  68.1 24.9 %collective-permute-start.10 = (bf16[4,128,512]{2,1,0:T(8,128)(2,1)S(1)}, bf16[4,128,512]{2,1,0:T(8,128)(2,1)S(1)}, u32[]{:S(2)}, u32[]{:S(2)}) collective-permute-start(bf16[4,128,512]{2,1,0:T(8,128)(2,1)S(1)} %get-tuple-element.39), channel_id=1, source_target_pairs={{0,2},{1,3},{2,0},{3,1},{4,6},{5,7},{6,4},{7,5},{8,10},{9,11},{10,... | collective-permute-start | bytes 1572872 | tf_op jit(solution)/shard_map/ppermute | solution.py:365
  69.3 23.7 %collective-permute-start.11 = (bf16[4,128,512]{2,1,0:T(8,128)(2,1)S(1)}, bf16[4,128,512]{2,1,0:T(8,128)(2,1)S(1)}, u32[]{:S(2)}, u32[]{:S(2)}) collective-permute-start(bf16[4,128,512]{2,1,0:T(8,128)(2,1)S(1)} %get-tuple-element.40), channel_id=1, source_target_pairs={{0,18},{1,19},{2,16},{3,17},{4,22},{5,23},{6,20},{7,21},{8,26},{9,... | collective-permute-start | bytes 1572872 | tf_op jit(solution)/shard_map/ppermute | solution.py:365
  94.2 23.9 %copy-start = (bf16[512,512]{1,0:T(8,128)(2,1)S(1)}, bf16[512,512]{1,0:T(8,128)(2,1)}, u32[]{:S(2)}) copy-start(bf16[512,512]{1,0:T(8,128)(2,1)} %phonon_ref.3) | copy-start | bytes 1572868
  94.3 4.2 %collective-permute-start.14 = (bf16[16,128,512]{2,1,0:T(8,128)(2,1)S(1)}, bf16[16,128,512]{2,1,0:T(8,128)(2,1)S(1)}, u32[]{:S(2)}, u32[]{:S(2)}) collective-permute-start(bf16[16,128,512]{2,1,0:T(8,128)(2,1)S(1)} %smooth.6.refs_7_), channel_id=1, source_target_pairs={{0,1},{1,0},{2,3},{3,2},{4,5},{5,4},{6,7},{7,6},{8,9},{9,8},{10,11... | collective-permute-start | bytes 6291464 | tf_op jit(solution)/shard_map/ppermute | solution.py:352
  100.8 0.7 copy-start.1
  101.5 9.1 %collective-permute-start.18 = (bf16[2,128,512]{2,1,0:T(8,128)(2,1)S(1)}, bf16[2,128,512]{2,1,0:T(8,128)(2,1)S(1)}, u32[]{:S(2)}, u32[]{:S(2)}) collective-permute-start(bf16[2,128,512]{2,1,0:T(8,128)(2,1)S(1)} %get-tuple-element.46), channel_id=1, source_target_pairs={{0,16},{1,17},{2,18},{3,19},{4,20},{5,21},{6,22},{7,23},{8,24},{9,... | collective-permute-start | bytes 786440 | tf_op jit(solution)/shard_map/ppermute | solution.py:365
  103.0 15.1 %collective-permute-start.19 = (bf16[2,128,512]{2,1,0:T(8,128)(2,1)}, bf16[2,128,512]{2,1,0:T(8,128)(2,1)}, u32[]{:S(2)}, u32[]{:S(2)}) collective-permute-start(bf16[2,128,512]{2,1,0:T(8,128)(2,1)} %get-tuple-element.47), channel_id=1, source_target_pairs={{0,2},{1,3},{2,0},{3,1},{4,6},{5,7},{6,4},{7,5},{8,10},{9,11},{10,... | collective-permute-start | bytes 786440 | tf_op jit(solution)/shard_map/ppermute | solution.py:365
  103.6 14.6 %collective-permute-start.20 = (bf16[2,128,512]{2,1,0:T(8,128)(2,1)}, bf16[2,128,512]{2,1,0:T(8,128)(2,1)}, u32[]{:S(2)}, u32[]{:S(2)}) collective-permute-start(bf16[2,128,512]{2,1,0:T(8,128)(2,1)} %get-tuple-element.48), channel_id=1, source_target_pairs={{0,18},{1,19},{2,16},{3,17},{4,22},{5,23},{6,20},{7,21},{8,26},{9,... | collective-permute-start | bytes 786440 | tf_op jit(solution)/shard_map/ppermute | solution.py:365
  105.0 27.5 %collective-permute-start.15 = (bf16[2,128,512]{2,1,0:T(8,128)(2,1)}, bf16[2,128,512]{2,1,0:T(8,128)(2,1)S(1)}, u32[]{:S(2)}, u32[]{:S(2)}) collective-permute-start(bf16[2,128,512]{2,1,0:T(8,128)(2,1)} %get-tuple-element.42), channel_id=1, source_target_pairs={{0,16},{1,17},{2,18},{3,19},{4,20},{5,21},{6,22},{7,23},{8,24},{9,... | collective-permute-start | bytes 786440 | tf_op jit(solution)/shard_map/ppermute | solution.py:365
  106.5 26.1 %collective-permute-start.16 = (bf16[2,128,512]{2,1,0:T(8,128)(2,1)}, bf16[2,128,512]{2,1,0:T(8,128)(2,1)S(1)}, u32[]{:S(2)}, u32[]{:S(2)}) collective-permute-start(bf16[2,128,512]{2,1,0:T(8,128)(2,1)} %get-tuple-element.43), channel_id=1, source_target_pairs={{0,2},{1,3},{2,0},{3,1},{4,6},{5,7},{6,4},{7,5},{8,10},{9,11},{10,... | collective-permute-start | bytes 786440 | tf_op jit(solution)/shard_map/ppermute | solution.py:365
  110.6 0.7 copy-start.3
  111.3 21.2 %collective-permute-start.17 = (bf16[2,128,512]{2,1,0:T(8,128)(2,1)}, bf16[2,128,512]{2,1,0:T(8,128)(2,1)}, u32[]{:S(2)}, u32[]{:S(2)}) collective-permute-start(bf16[2,128,512]{2,1,0:T(8,128)(2,1)} %get-tuple-element.44), channel_id=1, source_target_pairs={{0,18},{1,19},{2,16},{3,17},{4,22},{5,23},{6,20},{7,21},{8,26},{9,... | collective-permute-start | bytes 786440 | tf_op jit(solution)/shard_map/ppermute | solution.py:365
  118.1 1.0 copy-start.2
  119.1 0.9 copy-start.4

commit v3 on v2

--- a/solution.py
+++ b/solution.py
@@ -12,8 +12,11 @@
 STEP = 32
 CUTS = 2
 AXES = ("mom", "en")
+HALO = 6_000_000_000
+GATE = 60_000_000_000
 SMALL_VMEM = 12 * 1024 * 1024
 VMEM_LIMIT = 20 * 1024 * 1024
+WIDTH = 256
 
 
 class Place:
@@ -196,32 +199,57 @@
 
 
 def halo_kernel(moms, local, which_ref, *refs):
-    pieces, out = refs[: 2 * moms], refs[-1]
-    for dh in range(2):
-
-        @pl.when(which_ref[0] == dh)
-        def _(dh=dh):
-            for dm in range(moms):
-                out[dm * local : (dm + 1) * local] = pieces[dh * moms + dm][...]
-
-
-def halo_call(place, odd, pieces, after):
+    pieces, outs, sems = refs[: 2 * moms], refs[-3:-1], refs[-1]
+    for first in range(2):
+
+        @pl.when(which_ref[0] == first)
+        def _(first=first):
+            copies = []
+            for dh, out in zip((first, 1 - first), outs, strict=True):
+                for dm in range(moms):
+                    k = dh * moms + dm
+                    rows = out.at[pl.ds(dm * local, local)]
+                    copies.append(pltpu.make_async_copy(pieces[k], rows, sems.at[k]))
+            for copy in copies:
+                copy.start()
+            for copy in copies:
+                copy.wait()
+
+
+def halo_call(place, pieces, after):
     local, rows, orbitals = pieces[0].shape
     _, z, h, _ = place.here()
-    which = (place.goes_up(z, odd) != (h == 1)).astype(jnp.int32).reshape(1)
+    which = (place.goes_up(z, 0) != (h == 1)).astype(jnp.int32).reshape(1)
     return pl.pallas_call(
         functools.partial(halo_kernel, place.moms, local),
-        out_shape=jax.ShapeDtypeStruct((place.moms * local, rows, orbitals), jnp.bfloat16),
-        in_specs=[pl.BlockSpec(memory_space=pltpu.SMEM)] + [in_vmem()] * len(pieces) + anywhere(after),
-        out_specs=in_vmem(),
+        out_shape=[jax.ShapeDtypeStruct((place.moms * local, rows, orbitals), jnp.bfloat16)] * 2,
+        in_specs=[pl.BlockSpec(memory_space=pltpu.SMEM)] + anywhere([*pieces, *after]),
+        out_specs=[in_vmem()] * 2,
+        scratch_shapes=[pltpu.SemaphoreType.DMA((len(pieces),))],
         compiler_params=pltpu.CompilerParams(vmem_limit_bytes=SMALL_VMEM),
         cost_estimate=pl.CostEstimate(flops=0, bytes_accessed=0, transcendentals=0),
         name="halo",
     )(which, *pieces, *after)
 
 
-def smooth_kernel(n_in, n_add, splits, mix_ref, *refs):
-    inputs, addends, outs = refs[:n_in], refs[n_in : n_in + n_add], refs[-len(splits) :]
+def gate_kernel(*refs):
+    refs[-1][...] = jnp.zeros_like(refs[-1])
+
+
+def gate_call(weight, after):
+    return pl.pallas_call(
+        gate_kernel,
+        out_shape=jax.ShapeDtypeStruct((8, 128), jnp.float32),
+        in_specs=anywhere(after),
+        out_specs=in_vmem(),
+        compiler_params=pltpu.CompilerParams(vmem_limit_bytes=SMALL_VMEM),
+        cost_estimate=pl.CostEstimate(flops=weight, bytes_accessed=0, transcendentals=0),
+        name="gate",
+    )(*after)
+
+
+def smooth_kernel(n_in, n_add, n_out, mix_ref, *refs):
+    inputs, addends, outs = refs[:n_in], refs[n_in : n_in + n_add], refs[-n_out:]
     size, width = inputs[0].shape[-2:]
     for at in range(0, size, TILE):
         rows = slice(at, at + TILE)
@@ -230,53 +258,98 @@
         for r in addends:
             mixed += r[:, rows].reshape(-1, width).astype(jnp.float32)
         mixed = mixed.astype(jnp.bfloat16).reshape(-1, TILE, width)
-        for out, (first, last) in zip(outs, splits, strict=True):
-            out[:, rows] = mixed[first:last]
-
-
-def smooth_call(part, mix, inputs, addends, splits, after):
+        count = mixed.shape[0] // n_out
+        for k, out in enumerate(outs):
+            out[:, rows] = mixed[k * count : (k + 1) * count]
+
+
+def smooth_call(mix, inputs, addends, outs, after):
     size, orbitals = inputs[0].shape[1:]
-    counts = [last - first for first, last in splits]
-    return pl.pallas_call(
-        functools.partial(smooth_kernel, len(inputs), len(addends), splits),
-        out_shape=[jax.ShapeDtypeStruct((count, size, orbitals), jnp.bfloat16) for count in counts],
+    count = mix.shape[0] // TILE // outs
+    return pl.pallas_call(
+        functools.partial(smooth_kernel, len(inputs), len(addends), outs),
+        out_shape=[jax.ShapeDtypeStruct((count, size, orbitals), jnp.bfloat16)] * outs,
         in_specs=[in_vmem()] * (1 + len(inputs) + len(addends)) + anywhere(after),
-        out_specs=[in_vmem()] * len(counts),
+        out_specs=[in_vmem()] * outs,
         compiler_params=pltpu.CompilerParams(vmem_limit_bytes=SMALL_VMEM),
         cost_estimate=pl.CostEstimate(flops=0, bytes_accessed=0, transcendentals=0),
         name="smooth",
     )(mix, *inputs, *addends, *after)
 
 
+def part_kernel(local, group, sums_ref, *refs):
+    outs, sems = refs[-1 - sums_ref.shape[0] // local : -1], refs[-1]
+    first, last = group
+    copies = [
+        pltpu.make_async_copy(sums_ref.at[pl.ds(k * local + first, last - first)], out, sems.at[k])
+        for k, out in enumerate(outs)
+    ]
+    for copy in copies:
+        copy.start()
+    for copy in copies:
+        copy.wait()
+
+
+def part_call(place, sums, group, after):
+    slots = len(place.shifts)
+    return pl.pallas_call(
+        functools.partial(part_kernel, place.local, group),
+        out_shape=[pltpu.HBM((group[1] - group[0],) + sums.shape[1:], jnp.bfloat16)] * slots,
+        in_specs=[in_vmem()] + anywhere(after),
+        out_specs=anywhere(place.shifts),
+        scratch_shapes=[pltpu.SemaphoreType.DMA((slots,))],
+        compiler_params=pltpu.CompilerParams(vmem_limit_bytes=SMALL_VMEM),
+        cost_estimate=pl.CostEstimate(flops=0, bytes_accessed=0, transcendentals=0),
+        name="part",
+    )(sums, *after)
+
+
 def dyson_kernel(pieces, row_ref, green_ref, phonon_ref, *refs):
-    out_ref, energy, left, series = refs[-4:]
+    out_ref, left, even, odd = refs[-4:]
     size = phonon_ref.shape[0]
-    low, high = slice(0, size), slice(size, 2 * size)
-
-    def as_left(re, im):
-        left[low, low] = re
-        left[high, high] = re
-        left[low, high] = -im
-        left[high, low] = im
-
     for k, rows in enumerate(pieces):
         at = pl.multiple_of(row_ref[k], STEP)
-        scale = phonon_ref[pl.ds(pl.multiple_of(row_ref[len(pieces) + k], STEP), rows), :].astype(jnp.float32)
+        scale = phonon_ref[pl.ds(at, rows), :].astype(jnp.float32)
         value = refs[k][0].astype(jnp.float32)
-        energy[pl.ds(at, rows), :] = (scale * value).astype(jnp.bfloat16)
-    as_left(green_ref[0, 0, 0], green_ref[0, 0, 1])
-    product = jnp.dot(left[...], energy[...], preferred_element_type=jnp.float32)
-    product = (product * (1.0 / size)).astype(jnp.bfloat16)
-    as_left(product[low], product[high])
-    green = green_ref[0, 0].reshape(2 * size, size)
-    last = green
+        odd[row_ref[len(pieces) + k], pl.ds(at, rows), :] = (scale * value).astype(jnp.bfloat16)
+    odd[2] = odd[0] + odd[1]
+
+    def hold(to, ref):
+        to[0] = ref[0, 0, 0]
+        to[1] = ref[0, 0, 1]
+        to[2] = ref[0, 0, 0] + ref[0, 0, 1]
+
+    def product(right, put):
+        for at in range(0, size, WIDTH):
+            columns = slice(at, at + WIDTH)
+            p, q, t = (
+                jnp.dot(left[c], right[c, :, columns], preferred_element_type=jnp.float32) for c in range(3)
+            )
+            put(columns, p - q, t - (p + q))
+
+    def put_transfer(columns, re, im):
+        out_ref[0, 0, 0, :, columns] = (re * (1.0 / size)).astype(jnp.bfloat16)
+        out_ref[0, 0, 1, :, columns] = (im * (1.0 / size)).astype(jnp.bfloat16)
+
+    hold(left, green_ref)
+    hold(even, green_ref)
+    product(odd, put_transfer)
+    hold(left, out_ref)
     for step in range(NEUMANN):
-        added = green.astype(jnp.float32) + jnp.dot(left[...], last, preferred_element_type=jnp.float32)
-        if step < NEUMANN - 1:
-            series[...] = added.astype(jnp.bfloat16)
-            last = series[...]
-        else:
-            out_ref[0, 0] = added.astype(jnp.bfloat16).reshape(2, size, size)
+        right, to = (even, odd) if step % 2 == 0 else (odd, even)
+
+        def put(columns, re, im, to=to, final=step == NEUMANN - 1):
+            re = (re + green_ref[0, 0, 0, :, columns].astype(jnp.float32)).astype(jnp.bfloat16)
+            im = (im + green_ref[0, 0, 1, :, columns].astype(jnp.float32)).astype(jnp.bfloat16)
+            if final:
+                out_ref[0, 0, 0, :, columns] = re
+                out_ref[0, 0, 1, :, columns] = im
+            else:
+                to[0, :, columns] = re
+                to[1, :, columns] = im
+                to[2, :, columns] = re + im
+
+        product(right, put)
 
 
 def dyson_call(place, green0, phonon_me, pieces, first, last, out):
@@ -288,7 +361,7 @@
     for part, _, _, whole in pieces:
         start = first if whole else 0
         specs.append(pl.BlockSpec((1, part[1], size), lambda e, t, start=start: (start + e, 0, 0)))
-    args = [jnp.concatenate([at, at % size]), in_hbm(green0), phonon_me] + [x for _, _, x, _ in pieces]
+    args = [jnp.concatenate([at % size, at // size]), in_hbm(green0), phonon_me] + [x for _, _, x, _ in pieces]
     aliases = {}
     if out is not None:
         aliases = {len(args): 0}
@@ -303,15 +376,13 @@
             grid=(count,),
             in_specs=specs,
             out_specs=block,
-            scratch_shapes=[
-                pltpu.VMEM((2 * size, size), jnp.bfloat16),
-                pltpu.VMEM((2 * size, 2 * size), jnp.bfloat16),
-                pltpu.VMEM((2 * size, size), jnp.bfloat16),
-            ],
+            scratch_shapes=[pltpu.VMEM((3, size, size), jnp.bfloat16)] * 3,
         ),
         input_output_aliases=aliases,
         compiler_params=pltpu.CompilerParams(vmem_limit_bytes=VMEM_LIMIT),
-        cost_estimate=pl.CostEstimate(flops=0, bytes_accessed=0, transcendentals=0),
+        cost_estimate=pl.CostEstimate(
+            flops=count * (NEUMANN + 1) * 8 * size**3, bytes_accessed=(6 * count + 1) * 2 * size * size, transcendentals=0
+        ),
         name="dyson",
     )(*args)
 
@@ -334,50 +405,50 @@
         ]
 
     def send_halos(mine):
-        halos = []
-        for odd in range(2):
-            halo = halo_call(place, odd, mine, last_made)
-            last_made[:] = [halo]
-            halos.append(lax.ppermute(halo, AXES, place.plane_perm(odd)))
-        return list(mine) + halos
-
-    count = len(place.shifts) * local
+        halos = halo_call(place, mine, last_made)
+        last_made[:] = [halos[0]]
+        return list(mine) + [lax.ppermute(x, AXES, place.plane_perm(odd)) for odd, x in enumerate(halos)]
+
     back = [[] for _ in groups]
 
-    def partial_sums(part, inputs):
+    def partial_sums(inputs):
         addends = []
         for dq in range(1, place.reach):
-            (sums,) = smooth_call(part, mix[dq], inputs, [], [(0, count)], last_made)
+            (sums,) = smooth_call(mix[dq], inputs, [], 1, last_made)
             last_made[:] = [sums]
             addends.append(lax.ppermute(sums, AXES, place.swap_perm(dq)))
         return addends
 
-    def send_back(part, inputs, addends):
-        apart = part == place.parts[-1]
-        cut = groups if apart else ((0, local),)
-        splits = [(i * local + first, i * local + last) for first, last in cut for i in range(len(place.shifts))]
-        mixed = smooth_call(part, mix[0], inputs, addends, splits, last_made)
+    def send_back(part, mixed, group):
         last_made[:] = [mixed[0]]
-        for s in range(len(cut)):
-            for i, shift in enumerate(place.shifts):
-                piece = mixed[s * len(place.shifts) + i]
-                if shift != stay:
-                    piece = lax.ppermute(piece, AXES, place.shift_perm(shift))
-                for g in range(len(groups)):
-                    if g == s or not apart:
-                        back[g].append((part, shift, piece, not apart))
-        return [back[0][k - len(place.shifts)][2] for k in range(1, len(place.shifts))]
+        arrived = []
+        for shift, piece in zip(place.shifts, mixed, strict=True):
+            if shift != stay:
+                piece = lax.ppermute(piece, AXES, place.shift_perm(shift))
+            arrived.append(piece)
+            for g in range(len(groups)):
+                if group in (g, None):
+                    back[g].append((part, shift, piece, group is None))
+        return arrived[1:]
 
     parts = place.parts
     pieces = [cut_and_send(part) for part in parts]
     mix = mixing(place, coupling, shift_table, offsets, last_made)
     last_made[:] = [mix[0]]
     inputs = [send_halos(mine) for mine in pieces]
+    last_made[:] = [gate_call(HALO, last_made)]
     sent = []
     for part, mine in zip(parts, inputs, strict=True):
-        last_made += sent
-        addends = partial_sums(part, mine)
-        sent = send_back(part, mine, addends)
+        addends = partial_sums(mine)
+        if sent:
+            last_made[:] = [gate_call(GATE, last_made + sent)]
+        if part != parts[-1]:
+            sent = send_back(part, smooth_call(mix[0], mine, addends, len(place.shifts), last_made), None)
+            continue
+        (sums,) = smooth_call(mix[0], mine, addends, 1, last_made)
+        last_made[:] = [sums]
+        for g, group in enumerate(groups):
+            send_back(part, part_call(place, sums, group, last_made), g)
     out = None
     for (first, last), arrived in zip(groups, back, strict=True):
         out = dyson_call(place, green0, phonon_me, arrived, first, last, out)

time: 145 us -> 139 us (0.959)
  waiting for transfers between devices: 76.6 us -> 59.3 us
  Pallas kernels: 37.6 us -> 43.1 us
  starting transfers between devices: 26.9 us -> 31.2 us
    ppermute x6, waiting for transfers between devices: 40.6 us -> 28.7 us  [cut_and_send(): lax.ppermute(piece, AXES, place.shift_perm(shift))]
    ppermute x9, waiting for transfers between devices: 13.1 us -> 8.05 us  [send_back(): piece = lax.ppermute(piece, AXES, place.shift_perm(shift))]
    pallas_call x2, Pallas kernels: 25 us -> 20.8 us  [dyson_call(): pl.pallas_call(functools.partial(dyson_kernel, [part[1] for part, _, _, _...]
    pallas_call x4, Pallas kernels: 6.05 us -> 9.9 us  [smooth_call(): pl.pallas_call(functools.partial(smooth_kernel, len(inputs), len(addends)...]
    ppermute x6, starting transfers between devices: 8.03 us -> 11 us  [cut_and_send(): lax.ppermute(piece, AXES, place.shift_perm(shift))]
    pallas_call x4 -> x2, Pallas kernels: 0.3 us -> 2.77 us  [halo_call(): pl.pallas_call(functools.partial(halo_kernel, place.moms, local), out_sha...]
    pallas_call x0 -> x4, Pallas kernels: none -> 2.03 us  [the longest x2 2.02 us: part_call(): pl.pallas_call(functools.partial(part_kernel, place.local, group), out_sh...]
    ppermute x2, waiting for transfers between devices: 5.31 us -> 3.55 us  [partial_sums(): addends.append(lax.ppermute(sums, AXES, place.swap_perm(dq)))]
  transfers between devices with their start and end apart: 21 -> 21, of which waited for: 11 -> 10; matrix products, arithmetic and copies ran while one was open for 0% -> 0% of each run, Pallas kernels for 12% -> 17%
where the time goes in v3:
time: 139 us
  waiting for transfers between devices  59.3 us (43%)
  Pallas kernels  43.1 us (31%)
  starting transfers between devices  31.2 us (22%)
  local copies, waits for them, and re-layouts  4.64 us (3%)
    ppermute x6, waiting for transfers between devices, cut_and_send(): lax.ppermute(piece, AXES, place.shift_perm(shift))  28.7 us
    pallas_call x2, Pallas kernels, dyson_call(): pl.pallas_call(functools.partial(dyson_kernel, [part[1] for part, _, _, _...  20.8 us
    ppermute x4, waiting for transfers between devices, send_halos(): lax.ppermute(x, AXES, place.plane_perm(odd))  19 us
    ppermute x6, starting transfers between devices, cut_and_send(): lax.ppermute(piece, AXES, place.shift_perm(shift))  11 us
    ppermute x9, starting transfers between devices, send_back(): piece = lax.ppermute(piece, AXES, place.shift_perm(shift))  10.5 us
    pallas_call x4, Pallas kernels, smooth_call(): pl.pallas_call(functools.partial(smooth_kernel, len(inputs), len(addends)...  9.9 us
    ppermute x4, starting transfers between devices, send_halos(): lax.ppermute(x, AXES, place.plane_perm(odd))  9.48 us
    ppermute x9, waiting for transfers between devices, send_back(): piece = lax.ppermute(piece, AXES, place.shift_perm(shift))  8.05 us
  transfers between devices with their start and end apart: 21, of which 10 were waited for; matrix products, arithmetic and copies ran while one was open for 0% of the time, Pallas kernels for 17%

profile of v3, /device:TPU:0, one launch (start us, length us, event | category | flops | bytes accessed | tf_op | source)
XLA Modules:
  0.0 138.7 jit_solution(2995107160494191377)
XLA Ops:
  0.1 3.3 %cut.2 = (bf16[4,128,512]{2,1,0:T(8,128)(2,1)S(1)}, bf16[4,128,512]{2,1,0:T(8,128)(2,1)}, bf16[4,128,512]{2,1,0:T(8,128)(2,1)}, bf16[4,128,512]{2,1,0:T(8,128)(2,1)}) custom-call(s32[4]{0:T(128)S(1)} %pad_add_fusion.3.at_ref, bf16[1,4,1024,512]{3,2,1,0:T(8,128)(2,1)} %bitcast.18), custom_call_target="tpu_custom_call" | custom-call | tf_op jit(solution)/shard_map/cut/pallas_call | solution.py:189
  3.4 3.0 %collective-permute-start = (bf16[4,128,512]{2,1,0:T(8,128)(2,1)}, bf16[4,128,512]{2,1,0:T(8,128)(2,1)S(1)}, u32[]{:S(2)}, u32[]{:S(2)}) collective-permute-start(bf16[4,128,512]{2,1,0:T(8,128)(2,1)} %get-tuple-element.34), channel_id=1, source_target_pairs={{0,16},{1,17},{2,18},{3,19},{4,20},{5,21},{6,22},{7,23},{8,24},{9,... | collective-permute-start | bytes 1572872 | tf_op jit(solution)/shard_map/ppermute | solution.py:403
  6.4 1.5 %collective-permute-start.1 = (bf16[4,128,512]{2,1,0:T(8,128)(2,1)}, bf16[4,128,512]{2,1,0:T(8,128)(2,1)S(1)}, u32[]{:S(2)}, u32[]{:S(2)}) collective-permute-start(bf16[4,128,512]{2,1,0:T(8,128)(2,1)} %get-tuple-element.35), channel_id=1, source_target_pairs={{0,2},{1,3},{2,0},{3,1},{4,6},{5,7},{6,4},{7,5},{8,10},{9,11},{10,... | collective-permute-start | bytes 1572872 | tf_op jit(solution)/shard_map/ppermute | solution.py:403
  8.0 3.1 %cut.3 = (bf16[4,128,512]{2,1,0:T(8,128)(2,1)S(1)}, bf16[4,128,512]{2,1,0:T(8,128)(2,1)}, bf16[4,128,512]{2,1,0:T(8,128)(2,1)}, bf16[4,128,512]{2,1,0:T(8,128)(2,1)S(1)}) custom-call(s32[4]{0:T(128)S(1)} %pad_add_fusion.2.at_ref, bf16[1,4,1024,512]{3,2,1,0:T(8,128)(2,1)} %bitcast.19, bf16[4,128,512]{2,1,0:T(8,128)(2,1)S(1)} %get-tuple-element.31.refs_0_), custom_call_target="tpu_custom_call" | custom-call | tf_op jit(solution)/shard_map/cut/pallas_call | solution.py:189
  11.1 0.8 copy-done.11
  11.9 1.9 %collective-permute-start.5 = (bf16[4,128,512]{2,1,0:T(8,128)(2,1)}, bf16[4,128,512]{2,1,0:T(8,128)(2,1)S(1)}, u32[]{:S(2)}, u32[]{:S(2)}) collective-permute-start(bf16[4,128,512]{2,1,0:T(8,128)(2,1)} %get-tuple-element.40), channel_id=1, source_target_pairs={{0,16},{1,17},{2,18},{3,19},{4,20},{5,21},{6,22},{7,23},{8,24},{9,... | collective-permute-start | bytes 1572872 | tf_op jit(solution)/shard_map/ppermute | solution.py:403
  13.8 1.5 %collective-permute-start.6 = (bf16[4,128,512]{2,1,0:T(8,128)(2,1)}, bf16[4,128,512]{2,1,0:T(8,128)(2,1)}, u32[]{:S(2)}, u32[]{:S(2)}) collective-permute-start(bf16[4,128,512]{2,1,0:T(8,128)(2,1)} %get-tuple-element.41), channel_id=1, source_target_pairs={{0,2},{1,3},{2,0},{3,1},{4,6},{5,7},{6,4},{7,5},{8,10},{9,11},{10,... | collective-permute-start | bytes 1572872 | tf_op jit(solution)/shard_map/ppermute | solution.py:403
  15.3 4.0 %collective-permute-done.refs_1_ = bf16[4,128,512]{2,1,0:T(8,128)(2,1)S(1)} collective-permute-done((bf16[4,128,512]{2,1,0:T(8,128)(2,1)}, bf16[4,128,512]{2,1,0:T(8,128)(2,1)S(1)}, u32[]{:S(2)}, u32[]{:S(2)}) %collective-permute-start) | collective-permute-done | bytes 524320 | tf_op jit(solution)/shard_map/ppermute | solution.py:403
  19.3 3.0 %collective-permute-start.7 = (bf16[4,128,512]{2,1,0:T(8,128)(2,1)}, bf16[4,128,512]{2,1,0:T(8,128)(2,1)}, u32[]{:S(2)}, u32[]{:S(2)}) collective-permute-start(bf16[4,128,512]{2,1,0:T(8,128)(2,1)} %copy-done.11), channel_id=1, source_target_pairs={{0,18},{1,19},{2,16},{3,17},{4,22},{5,23},{6,20},{7,21},{8,26},{9,... | collective-permute-start | bytes 1572872 | tf_op jit(solution)/shard_map/ppermute | solution.py:403
  22.4 1.3 mixing.1
  23.8 8.9 %collective-permute-done.1.refs_2_ = bf16[4,128,512]{2,1,0:T(8,128)(2,1)S(1)} collective-permute-done((bf16[4,128,512]{2,1,0:T(8,128)(2,1)}, bf16[4,128,512]{2,1,0:T(8,128)(2,1)S(1)}, u32[]{:S(2)}, u32[]{:S(2)}) %collective-permute-start.1) | collective-permute-done | bytes 524320 | tf_op jit(solution)/shard_map/ppermute | solution.py:403
  32.7 0.2 halo.2
  32.9 0.7 collective-permute-start.4
  33.6 4.4 %collective-permute-start.3 = (bf16[8,128,512]{2,1,0:T(8,128)(2,1)S(1)}, bf16[8,128,512]{2,1,0:T(8,128)(2,1)S(1)}, u32[]{:S(2)}, u32[]{:S(2)}) collective-permute-start(bf16[8,128,512]{2,1,0:T(8,128)(2,1)S(1)} %get-tuple-element.37.refs_4_), channel_id=1, source_target_pairs={{0,4},{1,5},{2,6},{3,7},{4,0},{5,1},{6,2},{7,3},{8,12},{9,13},{10,... | collective-permute-start | bytes 3145736 | tf_op jit(solution)/shard_map/ppermute | solution.py:410
  38.0 3.9 %collective-permute-done.5.refs_1_ = bf16[4,128,512]{2,1,0:T(8,128)(2,1)S(1)} collective-permute-done((bf16[4,128,512]{2,1,0:T(8,128)(2,1)}, bf16[4,128,512]{2,1,0:T(8,128)(2,1)S(1)}, u32[]{:S(2)}, u32[]{:S(2)}) %collective-permute-start.5) | collective-permute-done | bytes 524320 | tf_op jit(solution)/shard_map/ppermute | solution.py:403
  41.8 11.9 %collective-permute-done.6.refs_2_ = bf16[4,128,512]{2,1,0:T(8,128)(2,1)} collective-permute-done((bf16[4,128,512]{2,1,0:T(8,128)(2,1)}, bf16[4,128,512]{2,1,0:T(8,128)(2,1)}, u32[]{:S(2)}, u32[]{:S(2)}) %collective-permute-start.6) | collective-permute-done | bytes 524320 | tf_op jit(solution)/shard_map/ppermute | solution.py:403
  53.8 2.6 %halo.3 = (bf16[8,128,512]{2,1,0:T(8,128)(2,1)}, bf16[8,128,512]{2,1,0:T(8,128)(2,1)}) custom-call(s32[1]{0:T(128)} %bitcast.17.which_ref, bf16[4,128,512]{2,1,0:T(8,128)(2,1)S(1)} %get-tuple-element.32.refs_0_, bf16[4,128,512]{2,1,0:T(8,128)(2,1)S(1)} %collective-permute-done.5.refs_1_, bf16[4,128,512]{2,1,0:T(8,128)(2,1)} %collective-permute-done.6.refs_2_, ...), custom_call_target="tpu_custom_call" | custom-call | tf_op jit(solution)/shard_map/halo/pallas_call | solution.py:223
  56.4 1.9 %collective-permute-done.3.refs_4_ = bf16[8,128,512]{2,1,0:T(8,128)(2,1)S(1)} collective-permute-done((bf16[8,128,512]{2,1,0:T(8,128)(2,1)S(1)}, bf16[8,128,512]{2,1,0:T(8,128)(2,1)S(1)}, u32[]{:S(2)}, u32[]{:S(2)}) %collective-permute-start.3) | collective-permute-done | bytes 1048608 | tf_op jit(solution)/shard_map/ppermute | solution.py:410
  58.3 1.3 smooth.4.refs_7_
  59.7 1.6 %collective-permute-start.13 = (bf16[8,128,512]{2,1,0:T(8,128)(2,1)}, bf16[8,128,512]{2,1,0:T(8,128)(2,1)}, u32[]{:S(2)}, u32[]{:S(2)}) collective-permute-start(bf16[8,128,512]{2,1,0:T(8,128)(2,1)} %get-tuple-element.48), channel_id=1, source_target_pairs={{4,8},{5,9},{6,10},{7,11},{8,4},{9,5},{10,6},{11,7},{20,24},{21,25... | collective-permute-start | bytes 3145736 | tf_op jit(solution)/shard_map/ppermute | solution.py:410
  61.3 2.7 %collective-permute-start.12 = (bf16[8,128,512]{2,1,0:T(8,128)(2,1)}, bf16[8,128,512]{2,1,0:T(8,128)(2,1)}, u32[]{:S(2)}, u32[]{:S(2)}) collective-permute-start(bf16[8,128,512]{2,1,0:T(8,128)(2,1)} %get-tuple-element.43.refs_0_), channel_id=1, source_target_pairs={{0,4},{1,5},{2,6},{3,7},{4,0},{5,1},{6,2},{7,3},{8,12},{9,13},{10,... | collective-permute-start | bytes 3145736 | tf_op jit(solution)/shard_map/ppermute | solution.py:410
  64.0 2.4 %smooth.5 = (bf16[4,128,512]{2,1,0:T(8,128)(2,1)S(1)}, bf16[4,128,512]{2,1,0:T(8,128)(2,1)}, bf16[4,128,512]{2,1,0:T(8,128)(2,1)}, bf16[4,128,512]{2,1,0:T(8,128)(2,1)}) custom-call(bf16[256,512]{1,0:T(8,128)(2,1)S(1)} %get-tuple-element.33.refs_4_.mix_ref, bf16[4,128,512]{2,1,0:T(8,128)(2,1)S(1)} %get-tuple-element.31.refs_0_, ...), custom_call_target="tpu_custom_call" | custom-call | tf_op jit(solution)/shard_map/smooth/pallas_call | solution.py:269
  66.4 0.8 copy-done.2
  67.2 1.5 %collective-permute-start.9 = (bf16[4,128,512]{2,1,0:T(8,128)(2,1)}, bf16[4,128,512]{2,1,0:T(8,128)(2,1)S(1)}, u32[]{:S(2)}, u32[]{:S(2)}) collective-permute-start(bf16[4,128,512]{2,1,0:T(8,128)(2,1)} %get-tuple-element.45), channel_id=1, source_target_pairs={{0,16},{1,17},{2,18},{3,19},{4,20},{5,21},{6,22},{7,23},{8,24},{9,... | collective-permute-start | bytes 1572872 | tf_op jit(solution)/shard_map/ppermute | solution.py:427
  68.7 0.5 collective-permute-start.10
  69.2 1.5 %collective-permute-start.11 = (bf16[4,128,512]{2,1,0:T(8,128)(2,1)}, bf16[4,128,512]{2,1,0:T(8,128)(2,1)S(1)}, u32[]{:S(2)}, u32[]{:S(2)}) collective-permute-start(bf16[4,128,512]{2,1,0:T(8,128)(2,1)} %get-tuple-element.47), channel_id=1, source_target_pairs={{0,18},{1,19},{2,16},{3,17},{4,22},{5,23},{6,20},{7,21},{8,26},{9,... | collective-permute-start | bytes 1572872 | tf_op jit(solution)/shard_map/ppermute | solution.py:427
  70.7 0.1 stack.81
  70.8 17.0 %collective-permute-done.12.refs_4_ = bf16[8,128,512]{2,1,0:T(8,128)(2,1)} collective-permute-done((bf16[8,128,512]{2,1,0:T(8,128)(2,1)}, bf16[8,128,512]{2,1,0:T(8,128)(2,1)}, u32[]{:S(2)}, u32[]{:S(2)}) %collective-permute-start.12) | collective-permute-done | bytes 1048608 | tf_op jit(solution)/shard_map/ppermute | solution.py:410
  87.9 0.9 copy-done.1
  88.8 1.0 copy-done.3
  89.9 3.1 %smooth.6.refs_0_ = bf16[16,128,512]{2,1,0:T(8,128)(2,1)S(1)} custom-call(bf16[256,512]{1,0:T(8,128)(2,1)S(1)} %copy-done.1, bf16[4,128,512]{2,1,0:T(8,128)(2,1)S(1)} %get-tuple-element.32.refs_0_, bf16[4,128,512]{2,1,0:T(8,128)(2,1)S(1)} %collective-permute-done.5.refs_1_, bf16[4,128,512]{2,1,0:T(8,128)(2,1)} %collective-permute-done.6.refs_2_, ...), custom_call_target="tpu_custom_call" | custom-call | tf_op jit(solution)/shard_map/smooth/pallas_call | solution.py:269
  93.1 0.6 collective-permute-done.10.refs_2_
  93.7 3.6 %collective-permute-done.14.refs_6_ = bf16[16,128,512]{2,1,0:T(8,128)(2,1)S(1)} collective-permute-done((bf16[16,128,512]{2,1,0:T(8,128)(2,1)S(1)}, bf16[16,128,512]{2,1,0:T(8,128)(2,1)S(1)}, u32[]{:S(2)}, u32[]{:S(2)}) %collective-permute-start.14) | collective-permute-done | bytes 2097184 | tf_op jit(solution)/shard_map/ppermute | solution.py:419
  97.2 3.1 %smooth.7.sums_ref.refs_0_ = bf16[16,128,512]{2,1,0:T(8,128)(2,1)S(1)} custom-call(bf16[256,512]{1,0:T(8,128)(2,1)S(1)} %get-tuple-element.33.refs_4_.mix_ref, bf16[4,128,512]{2,1,0:T(8,128)(2,1)S(1)} %get-tuple-element.32.refs_0_, bf16[4,128,512]{2,1,0:T(8,128)(2,1)S(1)} %collective-permute-done.5.refs_1_, ...), custom_call_target="tpu_custom_call" | custom-call | tf_op jit(solution)/shard_map/smooth/pallas_call | solution.py:269
  100.3 1.0 part.2
  101.3 1.6 %collective-permute-start.18 = (bf16[2,128,512]{2,1,0:T(8,128)(2,1)}, bf16[2,128,512]{2,1,0:T(8,128)(2,1)S(1)}, u32[]{:S(2)}, u32[]{:S(2)}) collective-permute-start(bf16[2,128,512]{2,1,0:T(8,128)(2,1)} %get-tuple-element.54), channel_id=1, source_target_pairs={{0,16},{1,17},{2,18},{3,19},{4,20},{5,21},{6,22},{7,23},{8,24},{9,... | collective-permute-start | bytes 786440 | tf_op jit(solution)/shard_map/ppermute | solution.py:427
  102.9 0.5 collective-permute-start.19
  103.4 1.5 %collective-permute-start.20 = (bf16[2,128,512]{2,1,0:T(8,128)(2,1)}, bf16[2,128,512]{2,1,0:T(8,128)(2,1)S(1)}, u32[]{:S(2)}, u32[]{:S(2)}) collective-permute-start(bf16[2,128,512]{2,1,0:T(8,128)(2,1)} %get-tuple-element.56), channel_id=1, source_target_pairs={{0,18},{1,19},{2,16},{3,17},{4,22},{5,23},{6,20},{7,21},{8,26},{9,... | collective-permute-start | bytes 786440 | tf_op jit(solution)/shard_map/ppermute | solution.py:427
  104.9 0.1 pad_add_fusion.row_ref
  105.0 0.9 copy-done.5
  105.9 1.0 part.3
  107.0 1.6 %collective-permute-start.15 = (bf16[2,128,512]{2,1,0:T(8,128)(2,1)}, bf16[2,128,512]{2,1,0:T(8,128)(2,1)S(1)}, u32[]{:S(2)}, u32[]{:S(2)}) collective-permute-start(bf16[2,128,512]{2,1,0:T(8,128)(2,1)} %get-tuple-element.51), channel_id=1, source_target_pairs={{0,16},{1,17},{2,18},{3,19},{4,20},{5,21},{6,22},{7,23},{8,24},{9,... | collective-permute-start | bytes 786440 | tf_op jit(solution)/shard_map/ppermute | solution.py:427
  108.5 0.5 collective-permute-start.16
  109.0 1.7 %collective-permute-done.18.refs_5_ = bf16[2,128,512]{2,1,0:T(8,128)(2,1)S(1)} collective-permute-done((bf16[2,128,512]{2,1,0:T(8,128)(2,1)}, bf16[2,128,512]{2,1,0:T(8,128)(2,1)S(1)}, u32[]{:S(2)}, u32[]{:S(2)}) %collective-permute-start.18) | collective-permute-done | bytes 262176 | tf_op jit(solution)/shard_map/ppermute | solution.py:427
  110.8 1.4 %collective-permute-start.17 = (bf16[2,128,512]{2,1,0:T(8,128)(2,1)}, bf16[2,128,512]{2,1,0:T(8,128)(2,1)S(1)}, u32[]{:S(2)}, u32[]{:S(2)}) collective-permute-start(bf16[2,128,512]{2,1,0:T(8,128)(2,1)} %get-tuple-element.53), channel_id=1, source_target_pairs={{0,18},{1,19},{2,16},{3,17},{4,22},{5,23},{6,20},{7,21},{8,26},{9,... | collective-permute-start | bytes 786440 | tf_op jit(solution)/shard_map/ppermute | solution.py:427
  112.2 5.7 %collective-permute-done.19.refs_6_ = bf16[2,128,512]{2,1,0:T(8,128)(2,1)S(1)} collective-permute-done((bf16[2,128,512]{2,1,0:T(8,128)(2,1)}, bf16[2,128,512]{2,1,0:T(8,128)(2,1)S(1)}, u32[]{:S(2)}, u32[]{:S(2)}) %collective-permute-start.19) | collective-permute-done | bytes 262176 | tf_op jit(solution)/shard_map/ppermute | solution.py:427
  117.9 10.4 %dyson.2.refs_8_ = bf16[1,4,2,512,512]{4,3,2,1,0:T(8,128)(2,1)} custom-call(s32[16]{0:T(128)S(1)} %pad_add_fusion.row_ref, bf16[1,4,2,512,512]{4,3,2,1,0:T(8,128)(2,1)} %green_ref.3, bf16[512,512]{1,0:T(8,128)(2,1)S(1)} %copy-done.10, bf16[4,128,512]{2,1,0:T(8,128)(2,1)S(1)} %copy-done.4, bf16[4,128,512]{2,1,0:T(8,128)(2,1)S(1)} %collective-permute-done.9.refs_1_, ...), custom_call_target="tpu_custom_call" | custom-call | flops 8589934592 | bytes 6815744 | tf_op jit(solution)/shard_map/dyson/pallas_call | solution.py:371
  128.4 10.4 %dyson.3 = bf16[1,4,2,512,512]{4,3,2,1,0:T(8,128)(2,1)} custom-call(s32[16]{0:T(128)S(1)} %pad_add_fusion.row_ref, bf16[1,4,2,512,512]{4,3,2,1,0:T(8,128)(2,1)} %green_ref.3, bf16[512,512]{1,0:T(8,128)(2,1)S(1)} %copy-done.10, bf16[4,128,512]{2,1,0:T(8,128)(2,1)S(1)} %copy-done.4, ...), custom_call_target="tpu_custom_call", output_to_operand_aliasing={{}: (11, {})} | custom-call | flops 8589934592 | bytes 6815744 | tf_op jit(solution)/shard_map/dyson/pallas_call | solution.py:371
  (41 shorter events, 0.5 us)
Async XLA Ops:
  3.4 16.0 %collective-permute-start = (bf16[4,128,512]{2,1,0:T(8,128)(2,1)}, bf16[4,128,512]{2,1,0:T(8,128)(2,1)S(1)}, u32[]{:S(2)}, u32[]{:S(2)}) collective-permute-start(bf16[4,128,512]{2,1,0:T(8,128)(2,1)} %get-tuple-element.34), channel_id=1, source_target_pairs={{0,16},{1,17},{2,18},{3,19},{4,20},{5,21},{6,22},{7,23},{8,24},{9,... | collective-permute-start | bytes 1572872 | tf_op jit(solution)/shard_map/ppermute | solution.py:403
  6.4 26.3 %collective-permute-start.1 = (bf16[4,128,512]{2,1,0:T(8,128)(2,1)}, bf16[4,128,512]{2,1,0:T(8,128)(2,1)S(1)}, u32[]{:S(2)}, u32[]{:S(2)}) collective-permute-start(bf16[4,128,512]{2,1,0:T(8,128)(2,1)} %get-tuple-element.35), channel_id=1, source_target_pairs={{0,2},{1,3},{2,0},{3,1},{4,6},{5,7},{6,4},{7,5},{8,10},{9,11},{10,... | collective-permute-start | bytes 1572872 | tf_op jit(solution)/shard_map/ppermute | solution.py:403
  7.9 24.8 %collective-permute-start.2 = (bf16[4,128,512]{2,1,0:T(8,128)(2,1)}, bf16[4,128,512]{2,1,0:T(8,128)(2,1)S(1)}, u32[]{:S(2)}, u32[]{:S(2)}) collective-permute-start(bf16[4,128,512]{2,1,0:T(8,128)(2,1)} %get-tuple-element.36), channel_id=1, source_target_pairs={{0,18},{1,19},{2,16},{3,17},{4,22},{5,23},{6,20},{7,21},{8,26},{9,... | collective-permute-start | bytes 1572872 | tf_op jit(solution)/shard_map/ppermute | solution.py:403
  8.0 14.4 %copy-start.7 = (f32[2,2,16]{2,1,0:T(2,128)S(1)}, f32[2,2,16]{2,1,0:T(2,128)}, u32[]{:S(2)}) copy-start(f32[2,2,16]{2,1,0:T(2,128)} %coupling_ref.1) | copy-start | bytes 772
  8.0 14.4 %copy-start.8 = (s32[2,16]{1,0:T(2,128)S(1)}, s32[2,16]{1,0:T(2,128)}, u32[]{:S(2)}) copy-start(s32[2,16]{1,0:T(2,128)} %shift_ref.1) | copy-start | bytes 388
  8.0 14.4 %copy-start.9 = (s32[16]{0:T(128)S(1)}, s32[16]{0:T(128)}, u32[]{:S(2)}) copy-start(s32[16]{0:T(128)} %offset_ref.1) | copy-start | bytes 196
  11.1 0.8 copy-start.11
  11.9 30.0 %collective-permute-start.5 = (bf16[4,128,512]{2,1,0:T(8,128)(2,1)}, bf16[4,128,512]{2,1,0:T(8,128)(2,1)S(1)}, u32[]{:S(2)}, u32[]{:S(2)}) collective-permute-start(bf16[4,128,512]{2,1,0:T(8,128)(2,1)} %get-tuple-element.40), channel_id=1, source_target_pairs={{0,16},{1,17},{2,18},{3,19},{4,20},{5,21},{6,22},{7,23},{8,24},{9,... | collective-permute-start | bytes 1572872 | tf_op jit(solution)/shard_map/ppermute | solution.py:403
  13.8 39.9 %collective-permute-start.6 = (bf16[4,128,512]{2,1,0:T(8,128)(2,1)}, bf16[4,128,512]{2,1,0:T(8,128)(2,1)}, u32[]{:S(2)}, u32[]{:S(2)}) collective-permute-start(bf16[4,128,512]{2,1,0:T(8,128)(2,1)} %get-tuple-element.41), channel_id=1, source_target_pairs={{0,2},{1,3},{2,0},{3,1},{4,6},{5,7},{6,4},{7,5},{8,10},{9,11},{10,... | collective-permute-start | bytes 1572872 | tf_op jit(solution)/shard_map/ppermute | solution.py:403
  19.3 34.4 %collective-permute-start.7 = (bf16[4,128,512]{2,1,0:T(8,128)(2,1)}, bf16[4,128,512]{2,1,0:T(8,128)(2,1)}, u32[]{:S(2)}, u32[]{:S(2)}) collective-permute-start(bf16[4,128,512]{2,1,0:T(8,128)(2,1)} %copy-done.11), channel_id=1, source_target_pairs={{0,18},{1,19},{2,16},{3,17},{4,22},{5,23},{6,20},{7,21},{8,26},{9,... | collective-permute-start | bytes 1572872 | tf_op jit(solution)/shard_map/ppermute | solution.py:403
  23.8 34.6 %copy-start = (bf16[256,512]{1,0:T(8,128)(2,1)}, bf16[256,512]{1,0:T(8,128)(2,1)S(1)}, u32[]{:S(2)}) copy-start(bf16[256,512]{1,0:T(8,128)(2,1)S(1)} %get-tuple-element.39.mix_ref) | copy-start | bytes 786436
  32.9 23.5 %collective-permute-start.4 = (bf16[8,128,512]{2,1,0:T(8,128)(2,1)S(1)}, bf16[8,128,512]{2,1,0:T(8,128)(2,1)S(1)}, u32[]{:S(2)}, u32[]{:S(2)}) collective-permute-start(bf16[8,128,512]{2,1,0:T(8,128)(2,1)S(1)} %get-tuple-element.38), channel_id=1, source_target_pairs={{4,8},{5,9},{6,10},{7,11},{8,4},{9,5},{10,6},{11,7},{20,24},{21,25... | collective-permute-start | bytes 3145736 | tf_op jit(solution)/shard_map/ppermute | solution.py:410
  33.6 24.7 %collective-permute-start.3 = (bf16[8,128,512]{2,1,0:T(8,128)(2,1)S(1)}, bf16[8,128,512]{2,1,0:T(8,128)(2,1)S(1)}, u32[]{:S(2)}, u32[]{:S(2)}) collective-permute-start(bf16[8,128,512]{2,1,0:T(8,128)(2,1)S(1)} %get-tuple-element.37.refs_4_), channel_id=1, source_target_pairs={{0,4},{1,5},{2,6},{3,7},{4,0},{5,1},{6,2},{7,3},{8,12},{9,13},{10,... | collective-permute-start | bytes 3145736 | tf_op jit(solution)/shard_map/ppermute | solution.py:410
  59.6 4.4 %collective-permute-start.8 = (bf16[16,128,512]{2,1,0:T(8,128)(2,1)S(1)}, bf16[16,128,512]{2,1,0:T(8,128)(2,1)S(1)}, u32[]{:S(2)}, u32[]{:S(2)}) collective-permute-start(bf16[16,128,512]{2,1,0:T(8,128)(2,1)S(1)} %smooth.4.refs_7_), channel_id=1, source_target_pairs={{0,1},{1,0},{2,3},{3,2},{4,5},{5,4},{6,7},{7,6},{8,9},{9,8},{10,11... | collective-permute-start | bytes 6291464 | tf_op jit(solution)/shard_map/ppermute | solution.py:419
  59.7 11.2 %collective-permute-start.13 = (bf16[8,128,512]{2,1,0:T(8,128)(2,1)}, bf16[8,128,512]{2,1,0:T(8,128)(2,1)}, u32[]{:S(2)}, u32[]{:S(2)}) collective-permute-start(bf16[8,128,512]{2,1,0:T(8,128)(2,1)} %get-tuple-element.48), channel_id=1, source_target_pairs={{4,8},{5,9},{6,10},{7,11},{8,4},{9,5},{10,6},{11,7},{20,24},{21,25... | collective-permute-start | bytes 3145736 | tf_op jit(solution)/shard_map/ppermute | solution.py:410
  61.3 26.6 %collective-permute-start.12 = (bf16[8,128,512]{2,1,0:T(8,128)(2,1)}, bf16[8,128,512]{2,1,0:T(8,128)(2,1)}, u32[]{:S(2)}, u32[]{:S(2)}) collective-permute-start(bf16[8,128,512]{2,1,0:T(8,128)(2,1)} %get-tuple-element.43.refs_0_), channel_id=1, source_target_pairs={{0,4},{1,5},{2,6},{3,7},{4,0},{5,1},{6,2},{7,3},{8,12},{9,13},{10,... | collective-permute-start | bytes 3145736 | tf_op jit(solution)/shard_map/ppermute | solution.py:410
  66.4 0.8 copy-start.2
  67.2 25.8 %collective-permute-start.9 = (bf16[4,128,512]{2,1,0:T(8,128)(2,1)}, bf16[4,128,512]{2,1,0:T(8,128)(2,1)S(1)}, u32[]{:S(2)}, u32[]{:S(2)}) collective-permute-start(bf16[4,128,512]{2,1,0:T(8,128)(2,1)} %get-tuple-element.45), channel_id=1, source_target_pairs={{0,16},{1,17},{2,18},{3,19},{4,20},{5,21},{6,22},{7,23},{8,24},{9,... | collective-permute-start | bytes 1572872 | tf_op jit(solution)/shard_map/ppermute | solution.py:427
  68.7 24.9 %collective-permute-start.10 = (bf16[4,128,512]{2,1,0:T(8,128)(2,1)}, bf16[4,128,512]{2,1,0:T(8,128)(2,1)S(1)}, u32[]{:S(2)}, u32[]{:S(2)}) collective-permute-start(bf16[4,128,512]{2,1,0:T(8,128)(2,1)} %get-tuple-element.46), channel_id=1, source_target_pairs={{0,2},{1,3},{2,0},{3,1},{4,6},{5,7},{6,4},{7,5},{8,10},{9,11},{10,... | collective-permute-start | bytes 1572872 | tf_op jit(solution)/shard_map/ppermute | solution.py:427
  69.2 24.4 %collective-permute-start.11 = (bf16[4,128,512]{2,1,0:T(8,128)(2,1)}, bf16[4,128,512]{2,1,0:T(8,128)(2,1)S(1)}, u32[]{:S(2)}, u32[]{:S(2)}) collective-permute-start(bf16[4,128,512]{2,1,0:T(8,128)(2,1)} %get-tuple-element.47), channel_id=1, source_target_pairs={{0,18},{1,19},{2,16},{3,17},{4,22},{5,23},{6,20},{7,21},{8,26},{9,... | collective-permute-start | bytes 1572872 | tf_op jit(solution)/shard_map/ppermute | solution.py:427
  87.9 1.0 copy-start.1
  88.8 1.0 copy-start.3
  93.0 4.2 %collective-permute-start.14 = (bf16[16,128,512]{2,1,0:T(8,128)(2,1)S(1)}, bf16[16,128,512]{2,1,0:T(8,128)(2,1)S(1)}, u32[]{:S(2)}, u32[]{:S(2)}) collective-permute-start(bf16[16,128,512]{2,1,0:T(8,128)(2,1)S(1)} %smooth.6.refs_0_), channel_id=1, source_target_pairs={{0,1},{1,0},{2,3},{3,2},{4,5},{5,4},{6,7},{7,6},{8,9},{9,8},{10,11... | collective-permute-start | bytes 6291464 | tf_op jit(solution)/shard_map/ppermute | solution.py:419
  100.3 17.6 %copy-start.10 = (bf16[512,512]{1,0:T(8,128)(2,1)S(1)}, bf16[512,512]{1,0:T(8,128)(2,1)}, u32[]{:S(2)}) copy-start(bf16[512,512]{1,0:T(8,128)(2,1)} %phonon_ref.3) | copy-start | bytes 1572868
  101.3 16.6 %copy-start.4 = (bf16[4,128,512]{2,1,0:T(8,128)(2,1)S(1)}, bf16[4,128,512]{2,1,0:T(8,128)(2,1)}, u32[]{:S(2)}) copy-start(bf16[4,128,512]{2,1,0:T(8,128)(2,1)} %copy-done.2) | copy-start | bytes 1572868
  101.3 9.4 %collective-permute-start.18 = (bf16[2,128,512]{2,1,0:T(8,128)(2,1)}, bf16[2,128,512]{2,1,0:T(8,128)(2,1)S(1)}, u32[]{:S(2)}, u32[]{:S(2)}) collective-permute-start(bf16[2,128,512]{2,1,0:T(8,128)(2,1)} %get-tuple-element.54), channel_id=1, source_target_pairs={{0,16},{1,17},{2,18},{3,19},{4,20},{5,21},{6,22},{7,23},{8,24},{9,... | collective-permute-start | bytes 786440 | tf_op jit(solution)/shard_map/ppermute | solution.py:427
  102.9 15.0 %collective-permute-start.19 = (bf16[2,128,512]{2,1,0:T(8,128)(2,1)}, bf16[2,128,512]{2,1,0:T(8,128)(2,1)S(1)}, u32[]{:S(2)}, u32[]{:S(2)}) collective-permute-start(bf16[2,128,512]{2,1,0:T(8,128)(2,1)} %get-tuple-element.55), channel_id=1, source_target_pairs={{0,2},{1,3},{2,0},{3,1},{4,6},{5,7},{6,4},{7,5},{8,10},{9,11},{10,... | collective-permute-start | bytes 786440 | tf_op jit(solution)/shard_map/ppermute | solution.py:427
  103.4 14.5 %collective-permute-start.20 = (bf16[2,128,512]{2,1,0:T(8,128)(2,1)}, bf16[2,128,512]{2,1,0:T(8,128)(2,1)S(1)}, u32[]{:S(2)}, u32[]{:S(2)}) collective-permute-start(bf16[2,128,512]{2,1,0:T(8,128)(2,1)} %get-tuple-element.56), channel_id=1, source_target_pairs={{0,18},{1,19},{2,16},{3,17},{4,22},{5,23},{6,20},{7,21},{8,26},{9,... | collective-permute-start | bytes 786440 | tf_op jit(solution)/shard_map/ppermute | solution.py:427
  105.0 0.9 copy-start.5
  105.9 12.0 %copy-start.6 = (bf16[2,128,512]{2,1,0:T(8,128)(2,1)S(1)}, bf16[2,128,512]{2,1,0:T(8,128)(2,1)}, u32[]{:S(2)}) copy-start(bf16[2,128,512]{2,1,0:T(8,128)(2,1)} %get-tuple-element.49.refs_0_.refs_4_) | copy-start | bytes 786436
  107.0 21.3 %collective-permute-start.15 = (bf16[2,128,512]{2,1,0:T(8,128)(2,1)}, bf16[2,128,512]{2,1,0:T(8,128)(2,1)S(1)}, u32[]{:S(2)}, u32[]{:S(2)}) collective-permute-start(bf16[2,128,512]{2,1,0:T(8,128)(2,1)} %get-tuple-element.51), channel_id=1, source_target_pairs={{0,16},{1,17},{2,18},{3,19},{4,20},{5,21},{6,22},{7,23},{8,24},{9,... | collective-permute-start | bytes 786440 | tf_op jit(solution)/shard_map/ppermute | solution.py:427
  108.5 19.8 %collective-permute-start.16 = (bf16[2,128,512]{2,1,0:T(8,128)(2,1)}, bf16[2,128,512]{2,1,0:T(8,128)(2,1)S(1)}, u32[]{:S(2)}, u32[]{:S(2)}) collective-permute-start(bf16[2,128,512]{2,1,0:T(8,128)(2,1)} %get-tuple-element.52), channel_id=1, source_target_pairs={{0,2},{1,3},{2,0},{3,1},{4,6},{5,7},{6,4},{7,5},{8,10},{9,11},{10,... | collective-permute-start | bytes 786440 | tf_op jit(solution)/shard_map/ppermute | solution.py:427
  110.8 17.6 %copy-start.12 = (bf16[2,128,512]{2,1,0:T(8,128)(2,1)S(1)}, bf16[2,128,512]{2,1,0:T(8,128)(2,1)}, u32[]{:S(2)}) copy-start(bf16[2,128,512]{2,1,0:T(8,128)(2,1)} %get-tuple-element.50.refs_4_) | copy-start | bytes 786436
  110.8 17.6 %collective-permute-start.17 = (bf16[2,128,512]{2,1,0:T(8,128)(2,1)}, bf16[2,128,512]{2,1,0:T(8,128)(2,1)S(1)}, u32[]{:S(2)}, u32[]{:S(2)}) collective-permute-start(bf16[2,128,512]{2,1,0:T(8,128)(2,1)} %get-tuple-element.53), channel_id=1, source_target_pairs={{0,18},{1,19},{2,16},{3,17},{4,22},{5,23},{6,20},{7,21},{8,26},{9,... | collective-permute-start | bytes 786440 | tf_op jit(solution)/shard_map/ppermute | solution.py:427

commit v4 on v3

--- a/solution.py
+++ b/solution.py
@@ -277,12 +277,35 @@
     )(mix, *inputs, *addends, *after)
 
 
-def part_kernel(local, group, sums_ref, *refs):
-    outs, sems = refs[-1 - sums_ref.shape[0] // local : -1], refs[-1]
-    first, last = group
+def add_kernel(n_add, slots, lead, *refs):
+    terms, local = refs[: 1 + n_add], refs[0].shape[0] // slots
+    outs, rest = refs[-slots:], refs[-1 - slots]
+    for k in range(slots):
+        energies = slice(k * local, (k + 1) * local)
+        total = sum(r[energies].astype(jnp.float32) for r in terms).astype(jnp.bfloat16)
+        outs[k][...] = total[:lead]
+        if lead < local:
+            rest[k * (local - lead) : (k + 1) * (local - lead)] = total[lead:]
+
+
+def add_call(place, terms, lead, after):
+    slots, tail = len(place.shifts), terms[0].shape[1:]
+    counts = [slots * (place.local - lead)] * (lead < place.local) + [lead] * slots
+    return pl.pallas_call(
+        functools.partial(add_kernel, len(terms) - 1, slots, lead),
+        out_shape=[jax.ShapeDtypeStruct((count,) + tail, jnp.bfloat16) for count in counts],
+        in_specs=[in_vmem()] * len(terms) + anywhere(after),
+        out_specs=[in_vmem()] * len(counts),
+        compiler_params=pltpu.CompilerParams(vmem_limit_bytes=SMALL_VMEM),
+        cost_estimate=pl.CostEstimate(flops=0, bytes_accessed=0, transcendentals=0),
+        name="add",
+    )(*terms, *after)
+
+
+def part_kernel(count, sums_ref, *refs):
+    outs, sems = refs[-1 - sums_ref.shape[0] // count : -1], refs[-1]
     copies = [
-        pltpu.make_async_copy(sums_ref.at[pl.ds(k * local + first, last - first)], out, sems.at[k])
-        for k, out in enumerate(outs)
+        pltpu.make_async_copy(sums_ref.at[pl.ds(k * count, count)], out, sems.at[k]) for k, out in enumerate(outs)
     ]
     for copy in copies:
         copy.start()
@@ -290,11 +313,12 @@
         copy.wait()
 
 
-def part_call(place, sums, group, after):
+def part_call(place, sums, after):
     slots = len(place.shifts)
-    return pl.pallas_call(
-        functools.partial(part_kernel, place.local, group),
-        out_shape=[pltpu.HBM((group[1] - group[0],) + sums.shape[1:], jnp.bfloat16)] * slots,
+    count = sums.shape[0] // slots
+    return pl.pallas_call(
+        functools.partial(part_kernel, count),
+        out_shape=[pltpu.HBM((count,) + sums.shape[1:], jnp.bfloat16)] * slots,
         in_specs=[in_vmem()] + anywhere(after),
         out_specs=anywhere(place.shifts),
         scratch_shapes=[pltpu.SemaphoreType.DMA((slots,))],
@@ -440,15 +464,14 @@
     sent = []
     for part, mine in zip(parts, inputs, strict=True):
         addends = partial_sums(mine)
-        if sent:
-            last_made[:] = [gate_call(GATE, last_made + sent)]
+        (own,) = smooth_call(mix[0], mine, [], 1, last_made)
         if part != parts[-1]:
-            sent = send_back(part, smooth_call(mix[0], mine, addends, len(place.shifts), last_made), None)
+            sent = send_back(part, add_call(place, [own, *addends], local, [own]), None)
             continue
-        (sums,) = smooth_call(mix[0], mine, addends, 1, last_made)
-        last_made[:] = [sums]
-        for g, group in enumerate(groups):
-            send_back(part, part_call(place, sums, group, last_made), g)
+        last_made[:] = [gate_call(GATE, [own, *sent])]
+        rest, *lead = add_call(place, [own, *addends], groups[0][1], last_made)
+        send_back(part, lead, 0)
+        send_back(part, part_call(place, rest, last_made), 1)
     out = None
     for (first, last), arrived in zip(groups, back, strict=True):
         out = dyson_call(place, green0, phonon_me, arrived, first, last, out)

time: 139 us -> 136 us (0.978)
  local copies, waits for them, and re-layouts: 4.64 us -> 0.91 us
  Pallas kernels: 43.1 us -> 44.8 us
  waiting for transfers between devices: 59.3 us -> 57.8 us
    unnamed x26 -> x16, local copies, waits for them, and re-layouts: 4.56 us -> 0.82 us
    ppermute x2, waiting for transfers between devices: 3.55 us -> 0.37 us  [partial_sums(): addends.append(lax.ppermute(sums, AXES, place.swap_perm(dq)))]
    ppermute x4, waiting for transfers between devices: 19 us -> 20.6 us  [send_halos(): lax.ppermute(x, AXES, place.plane_perm(odd))]
    pallas_call x2 -> x3, Pallas kernels: 2.02 us -> 2.99 us  [the longest x2 1.98 us: add_call(): pl.pallas_call(functools.partial(add_kernel, len(terms) - 1, slots, lead)...]
  transfers between devices with their start and end apart: 21 -> 21, of which waited for: 10 -> 10; matrix products, arithmetic and copies ran while one was open for 0% -> 0% of each run, Pallas kernels for 17% -> 21%
where the time goes in v4:
time: 136 us; the launch traced here: 135 us
  waiting for transfers between devices  57.8 us (42%)
  Pallas kernels  44.8 us (33%)
  starting transfers between devices  31.1 us (23%)
    ppermute x6, waiting for transfers between devices, cut_and_send(): lax.ppermute(piece, AXES, place.shift_perm(shift))  27.5 us
    pallas_call x2, Pallas kernels, dyson_call(): pl.pallas_call(functools.partial(dyson_kernel, [part[1] for part, _, _, _...  21 us
    ppermute x4, waiting for transfers between devices, send_halos(): lax.ppermute(x, AXES, place.plane_perm(odd))  20.6 us
    ppermute x6, starting transfers between devices, cut_and_send(): lax.ppermute(piece, AXES, place.shift_perm(shift))  11 us
    pallas_call x4, Pallas kernels, smooth_call(): pl.pallas_call(functools.partial(smooth_kernel, len(inputs), len(addends)...  10.5 us
    ppermute x9, starting transfers between devices, send_back(): piece = lax.ppermute(piece, AXES, place.shift_perm(shift))  10.4 us
    ppermute x4, starting transfers between devices, send_halos(): lax.ppermute(x, AXES, place.plane_perm(odd))  9.55 us
    ppermute x9, waiting for transfers between devices, send_back(): piece = lax.ppermute(piece, AXES, place.shift_perm(shift))  9.31 us
  transfers between devices with their start and end apart: 21, of which 10 were waited for; matrix products, arithmetic and copies ran while one was open for 0% of the time, Pallas kernels for 21%

profile of v4, /device:TPU:0, one launch (start us, length us, event | category | flops | bytes accessed | tf_op | source)
XLA Modules:
  0.0 135.2 jit_solution(7037056973500811262)
XLA Ops:
  0.0 0.1 pad_add_fusion.3.at_ref
  0.1 3.2 %cut.2 = (bf16[4,128,512]{2,1,0:T(8,128)(2,1)S(1)}, bf16[4,128,512]{2,1,0:T(8,128)(2,1)}, bf16[4,128,512]{2,1,0:T(8,128)(2,1)}, bf16[4,128,512]{2,1,0:T(8,128)(2,1)}) custom-call(s32[4]{0:T(128)S(1)} %pad_add_fusion.3.at_ref, bf16[1,4,1024,512]{3,2,1,0:T(8,128)(2,1)} %bitcast.18), custom_call_target="tpu_custom_call" | custom-call | tf_op jit(solution)/shard_map/cut/pallas_call | solution.py:189
  3.3 3.0 %collective-permute-start = (bf16[4,128,512]{2,1,0:T(8,128)(2,1)}, bf16[4,128,512]{2,1,0:T(8,128)(2,1)S(1)}, u32[]{:S(2)}, u32[]{:S(2)}) collective-permute-start(bf16[4,128,512]{2,1,0:T(8,128)(2,1)} %get-tuple-element.35), channel_id=1, source_target_pairs={{0,16},{1,17},{2,18},{3,19},{4,20},{5,21},{6,22},{7,23},{8,24},{9,... | collective-permute-start | bytes 1572872 | tf_op jit(solution)/shard_map/ppermute | solution.py:427
  6.3 1.5 %collective-permute-start.1 = (bf16[4,128,512]{2,1,0:T(8,128)(2,1)}, bf16[4,128,512]{2,1,0:T(8,128)(2,1)}, u32[]{:S(2)}, u32[]{:S(2)}) collective-permute-start(bf16[4,128,512]{2,1,0:T(8,128)(2,1)} %get-tuple-element.36), channel_id=1, source_target_pairs={{0,2},{1,3},{2,0},{3,1},{4,6},{5,7},{6,4},{7,5},{8,10},{9,11},{10,... | collective-permute-start | bytes 1572872 | tf_op jit(solution)/shard_map/ppermute | solution.py:427
  7.9 0.1 pad_add_fusion.2.at_ref
  8.0 3.1 %cut.3 = (bf16[4,128,512]{2,1,0:T(8,128)(2,1)S(1)}, bf16[4,128,512]{2,1,0:T(8,128)(2,1)}, bf16[4,128,512]{2,1,0:T(8,128)(2,1)}, bf16[4,128,512]{2,1,0:T(8,128)(2,1)S(1)}) custom-call(s32[4]{0:T(128)S(1)} %pad_add_fusion.2.at_ref, bf16[1,4,1024,512]{3,2,1,0:T(8,128)(2,1)} %bitcast.19, bf16[4,128,512]{2,1,0:T(8,128)(2,1)S(1)} %get-tuple-element.32.refs_0_), custom_call_target="tpu_custom_call" | custom-call | tf_op jit(solution)/shard_map/cut/pallas_call | solution.py:189
  11.0 0.8 copy-done.6
  11.8 1.9 %collective-permute-start.5 = (bf16[4,128,512]{2,1,0:T(8,128)(2,1)}, bf16[4,128,512]{2,1,0:T(8,128)(2,1)S(1)}, u32[]{:S(2)}, u32[]{:S(2)}) collective-permute-start(bf16[4,128,512]{2,1,0:T(8,128)(2,1)} %get-tuple-element.41), channel_id=1, source_target_pairs={{0,16},{1,17},{2,18},{3,19},{4,20},{5,21},{6,22},{7,23},{8,24},{9,... | collective-permute-start | bytes 1572872 | tf_op jit(solution)/shard_map/ppermute | solution.py:427
  13.8 1.5 %collective-permute-start.6 = (bf16[4,128,512]{2,1,0:T(8,128)(2,1)}, bf16[4,128,512]{2,1,0:T(8,128)(2,1)S(1)}, u32[]{:S(2)}, u32[]{:S(2)}) collective-permute-start(bf16[4,128,512]{2,1,0:T(8,128)(2,1)} %get-tuple-element.42), channel_id=1, source_target_pairs={{0,2},{1,3},{2,0},{3,1},{4,6},{5,7},{6,4},{7,5},{8,10},{9,11},{10,... | collective-permute-start | bytes 1572872 | tf_op jit(solution)/shard_map/ppermute | solution.py:427
  15.3 4.0 %collective-permute-done.refs_1_ = bf16[4,128,512]{2,1,0:T(8,128)(2,1)S(1)} collective-permute-done((bf16[4,128,512]{2,1,0:T(8,128)(2,1)}, bf16[4,128,512]{2,1,0:T(8,128)(2,1)S(1)}, u32[]{:S(2)}, u32[]{:S(2)}) %collective-permute-start) | collective-permute-done | bytes 524320 | tf_op jit(solution)/shard_map/ppermute | solution.py:427
  19.3 3.0 %collective-permute-start.7 = (bf16[4,128,512]{2,1,0:T(8,128)(2,1)}, bf16[4,128,512]{2,1,0:T(8,128)(2,1)S(1)}, u32[]{:S(2)}, u32[]{:S(2)}) collective-permute-start(bf16[4,128,512]{2,1,0:T(8,128)(2,1)} %copy-done.6), channel_id=1, source_target_pairs={{0,18},{1,19},{2,16},{3,17},{4,22},{5,23},{6,20},{7,21},{8,26},{9,... | collective-permute-start | bytes 1572872 | tf_op jit(solution)/shard_map/ppermute | solution.py:427
  22.3 0.1 pad_add_fusion.1.here_ref
  22.4 1.3 mixing.1
  23.7 9.0 %collective-permute-done.1.refs_2_ = bf16[4,128,512]{2,1,0:T(8,128)(2,1)} collective-permute-done((bf16[4,128,512]{2,1,0:T(8,128)(2,1)}, bf16[4,128,512]{2,1,0:T(8,128)(2,1)}, u32[]{:S(2)}, u32[]{:S(2)}) %collective-permute-start.1) | collective-permute-done | bytes 524320 | tf_op jit(solution)/shard_map/ppermute | solution.py:427
  32.7 1.2 halo.2
  34.0 0.7 collective-permute-start.4
  34.7 4.4 %collective-permute-start.3 = (bf16[8,128,512]{2,1,0:T(8,128)(2,1)S(1)}, bf16[8,128,512]{2,1,0:T(8,128)(2,1)S(1)}, u32[]{:S(2)}, u32[]{:S(2)}) collective-permute-start(bf16[8,128,512]{2,1,0:T(8,128)(2,1)S(1)} %get-tuple-element.38.refs_4_), channel_id=1, source_target_pairs={{0,4},{1,5},{2,6},{3,7},{4,0},{5,1},{6,2},{7,3},{8,12},{9,13},{10,... | collective-permute-start | bytes 3145736 | tf_op jit(solution)/shard_map/ppermute | solution.py:434
  39.1 2.7 %collective-permute-done.5.refs_1_ = bf16[4,128,512]{2,1,0:T(8,128)(2,1)S(1)} collective-permute-done((bf16[4,128,512]{2,1,0:T(8,128)(2,1)}, bf16[4,128,512]{2,1,0:T(8,128)(2,1)S(1)}, u32[]{:S(2)}, u32[]{:S(2)}) %collective-permute-start.5) | collective-permute-done | bytes 524320 | tf_op jit(solution)/shard_map/ppermute | solution.py:427
  41.8 11.8 %collective-permute-done.6.refs_2_ = bf16[4,128,512]{2,1,0:T(8,128)(2,1)S(1)} collective-permute-done((bf16[4,128,512]{2,1,0:T(8,128)(2,1)}, bf16[4,128,512]{2,1,0:T(8,128)(2,1)S(1)}, u32[]{:S(2)}, u32[]{:S(2)}) %collective-permute-start.6) | collective-permute-done | bytes 524320 | tf_op jit(solution)/shard_map/ppermute | solution.py:427
  53.6 1.5 %halo.3 = (bf16[8,128,512]{2,1,0:T(8,128)(2,1)}, bf16[8,128,512]{2,1,0:T(8,128)(2,1)}) custom-call(s32[1]{0:T(128)} %bitcast.17.which_ref, bf16[4,128,512]{2,1,0:T(8,128)(2,1)S(1)} %get-tuple-element.33.refs_0_, bf16[4,128,512]{2,1,0:T(8,128)(2,1)S(1)} %collective-permute-done.5.refs_1_, bf16[4,128,512]{2,1,0:T(8,128)(2,1)S(1)} %collective-permute-done.6.refs_2_, ...), custom_call_target="tpu_custom_call" | custom-call | tf_op jit(solution)/shard_map/halo/pallas_call | solution.py:223
  55.2 4.3 %collective-permute-done.3.refs_4_ = bf16[8,128,512]{2,1,0:T(8,128)(2,1)S(1)} collective-permute-done((bf16[8,128,512]{2,1,0:T(8,128)(2,1)S(1)}, bf16[8,128,512]{2,1,0:T(8,128)(2,1)S(1)}, u32[]{:S(2)}, u32[]{:S(2)}) %collective-permute-start.3) | collective-permute-done | bytes 1048608 | tf_op jit(solution)/shard_map/ppermute | solution.py:434
  59.4 2.4 %smooth.4.refs_6_ = bf16[16,128,512]{2,1,0:T(8,128)(2,1)S(1)} custom-call(bf16[256,512]{1,0:T(8,128)(2,1)S(1)} %get-tuple-element.40.mix_ref, bf16[4,128,512]{2,1,0:T(8,128)(2,1)S(1)} %get-tuple-element.32.refs_0_, bf16[4,128,512]{2,1,0:T(8,128)(2,1)S(1)} %collective-permute-done.refs_1_, bf16[4,128,512]{2,1,0:T(8,128)(2,1)} %collective-permute-done.1.refs_2_, ...), custom_call_target="tpu_custom_call" | custom-call | tf_op jit(solution)/shard_map/smooth/pallas_call | solution.py:269
  62.0 1.7 %collective-permute-start.13 = (bf16[8,128,512]{2,1,0:T(8,128)(2,1)}, bf16[8,128,512]{2,1,0:T(8,128)(2,1)}, u32[]{:S(2)}, u32[]{:S(2)}) collective-permute-start(bf16[8,128,512]{2,1,0:T(8,128)(2,1)} %get-tuple-element.49), channel_id=1, source_target_pairs={{4,8},{5,9},{6,10},{7,11},{8,4},{9,5},{10,6},{11,7},{20,24},{21,25... | collective-permute-start | bytes 3145736 | tf_op jit(solution)/shard_map/ppermute | solution.py:434
  63.7 2.8 %collective-permute-start.12 = (bf16[8,128,512]{2,1,0:T(8,128)(2,1)}, bf16[8,128,512]{2,1,0:T(8,128)(2,1)}, u32[]{:S(2)}, u32[]{:S(2)}) collective-permute-start(bf16[8,128,512]{2,1,0:T(8,128)(2,1)} %get-tuple-element.44.refs_0_), channel_id=1, source_target_pairs={{0,4},{1,5},{2,6},{3,7},{4,0},{5,1},{6,2},{7,3},{8,12},{9,13},{10,... | collective-permute-start | bytes 3145736 | tf_op jit(solution)/shard_map/ppermute | solution.py:434
  66.4 2.4 %smooth.5.refs_0_.refs_2_ = bf16[16,128,512]{2,1,0:T(8,128)(2,1)S(1)} custom-call(bf16[256,512]{1,0:T(8,128)(2,1)S(1)} %get-tuple-element.34.refs_4_.mix_ref, bf16[4,128,512]{2,1,0:T(8,128)(2,1)S(1)} %get-tuple-element.32.refs_0_, bf16[4,128,512]{2,1,0:T(8,128)(2,1)S(1)} %collective-permute-done.refs_1_, ...), custom_call_target="tpu_custom_call" | custom-call | tf_op jit(solution)/shard_map/smooth/pallas_call | solution.py:269
  68.9 1.5 %add.213 = (bf16[4,128,512]{2,1,0:T(8,128)(2,1)S(1)}, bf16[4,128,512]{2,1,0:T(8,128)(2,1)}, bf16[4,128,512]{2,1,0:T(8,128)(2,1)}, bf16[4,128,512]{2,1,0:T(8,128)(2,1)}) custom-call(bf16[16,128,512]{2,1,0:T(8,128)(2,1)S(1)} %smooth.5.refs_0_.refs_2_, bf16[16,128,512]{2,1,0:T(8,128)(2,1)S(1)} %collective-permute-done.8.refs_1_, ...), custom_call_target="tpu_custom_call" | custom-call | tf_op jit(solution)/shard_map/add/pallas_call | solution.py:294
  70.4 1.5 %collective-permute-start.9 = (bf16[4,128,512]{2,1,0:T(8,128)(2,1)}, bf16[4,128,512]{2,1,0:T(8,128)(2,1)}, u32[]{:S(2)}, u32[]{:S(2)}) collective-permute-start(bf16[4,128,512]{2,1,0:T(8,128)(2,1)} %get-tuple-element.46), channel_id=1, source_target_pairs={{0,16},{1,17},{2,18},{3,19},{4,20},{5,21},{6,22},{7,23},{8,24},{9,... | collective-permute-start | bytes 1572872 | tf_op jit(solution)/shard_map/ppermute | solution.py:451
  71.9 0.4 collective-permute-start.10
  72.3 1.6 %collective-permute-start.11 = (bf16[4,128,512]{2,1,0:T(8,128)(2,1)}, bf16[4,128,512]{2,1,0:T(8,128)(2,1)}, u32[]{:S(2)}, u32[]{:S(2)}) collective-permute-start(bf16[4,128,512]{2,1,0:T(8,128)(2,1)} %get-tuple-element.48), channel_id=1, source_target_pairs={{0,18},{1,19},{2,16},{3,17},{4,22},{5,23},{6,20},{7,21},{8,26},{9,... | collective-permute-start | bytes 1572872 | tf_op jit(solution)/shard_map/ppermute | solution.py:451
  73.9 0.1 stack.81
  74.0 16.3 %collective-permute-done.12.refs_4_ = bf16[8,128,512]{2,1,0:T(8,128)(2,1)} collective-permute-done((bf16[8,128,512]{2,1,0:T(8,128)(2,1)}, bf16[8,128,512]{2,1,0:T(8,128)(2,1)}, u32[]{:S(2)}, u32[]{:S(2)}) %collective-permute-start.12) | collective-permute-done | bytes 1048608 | tf_op jit(solution)/shard_map/ppermute | solution.py:434
  90.3 2.8 %smooth.6.refs_6_ = bf16[16,128,512]{2,1,0:T(8,128)(2,1)S(1)} custom-call(bf16[256,512]{1,0:T(8,128)(2,1)S(1)} %copy-done.1, bf16[4,128,512]{2,1,0:T(8,128)(2,1)S(1)} %get-tuple-element.33.refs_0_, bf16[4,128,512]{2,1,0:T(8,128)(2,1)S(1)} %collective-permute-done.5.refs_1_, bf16[4,128,512]{2,1,0:T(8,128)(2,1)S(1)} %collective-permute-done.6.refs_2_, ...), custom_call_target="tpu_custom_call" | custom-call | tf_op jit(solution)/shard_map/smooth/pallas_call | solution.py:269
  93.1 2.8 %smooth.7.refs_0_ = bf16[16,128,512]{2,1,0:T(8,128)(2,1)S(1)} custom-call(bf16[256,512]{1,0:T(8,128)(2,1)S(1)} %get-tuple-element.34.refs_4_.mix_ref, bf16[4,128,512]{2,1,0:T(8,128)(2,1)S(1)} %get-tuple-element.33.refs_0_, bf16[4,128,512]{2,1,0:T(8,128)(2,1)S(1)} %collective-permute-done.5.refs_1_, bf16[4,128,512]{2,1,0:T(8,128)(2,1)S(1)} %collective-permute-done.6.refs_2_, ...), custom_call_target="tpu_custom_call" | custom-call | tf_op jit(solution)/shard_map/smooth/pallas_call | solution.py:269
  95.9 1.0 collective-permute-done.10.refs_2_
  96.9 0.4 collective-permute-done.14.refs_1_
  97.3 0.5 add.214
  97.8 1.6 %collective-permute-start.18 = (bf16[2,128,512]{2,1,0:T(8,128)(2,1)S(1)}, bf16[2,128,512]{2,1,0:T(8,128)(2,1)S(1)}, u32[]{:S(2)}, u32[]{:S(2)}) collective-permute-start(bf16[2,128,512]{2,1,0:T(8,128)(2,1)S(1)} %get-tuple-element.56), channel_id=1, source_target_pairs={{0,16},{1,17},{2,18},{3,19},{4,20},{5,21},{6,22},{7,23},{8,24},{9,... | collective-permute-start | bytes 786440 | tf_op jit(solution)/shard_map/ppermute | solution.py:451
  99.3 0.4 collective-permute-start.19
  99.8 1.6 %collective-permute-start.20 = (bf16[2,128,512]{2,1,0:T(8,128)(2,1)S(1)}, bf16[2,128,512]{2,1,0:T(8,128)(2,1)S(1)}, u32[]{:S(2)}, u32[]{:S(2)}) collective-permute-start(bf16[2,128,512]{2,1,0:T(8,128)(2,1)S(1)} %get-tuple-element.58), channel_id=1, source_target_pairs={{0,18},{1,19},{2,16},{3,17},{4,22},{5,23},{6,20},{7,21},{8,26},{9,... | collective-permute-start | bytes 786440 | tf_op jit(solution)/shard_map/ppermute | solution.py:451
  101.3 0.1 pad_add_fusion.row_ref
  101.4 1.0 part.1
  102.4 1.6 %collective-permute-start.15 = (bf16[2,128,512]{2,1,0:T(8,128)(2,1)}, bf16[2,128,512]{2,1,0:T(8,128)(2,1)S(1)}, u32[]{:S(2)}, u32[]{:S(2)}) collective-permute-start(bf16[2,128,512]{2,1,0:T(8,128)(2,1)} %get-tuple-element.53), channel_id=1, source_target_pairs={{0,16},{1,17},{2,18},{3,19},{4,20},{5,21},{6,22},{7,23},{8,24},{9,... | collective-permute-start | bytes 786440 | tf_op jit(solution)/shard_map/ppermute | solution.py:451
  104.0 0.4 collective-permute-start.16
  104.4 2.6 %collective-permute-done.18.refs_5_ = bf16[2,128,512]{2,1,0:T(8,128)(2,1)S(1)} collective-permute-done((bf16[2,128,512]{2,1,0:T(8,128)(2,1)S(1)}, bf16[2,128,512]{2,1,0:T(8,128)(2,1)S(1)}, u32[]{:S(2)}, u32[]{:S(2)}) %collective-permute-start.18) | collective-permute-done | bytes 262176 | tf_op jit(solution)/shard_map/ppermute | solution.py:451
  107.0 1.4 %collective-permute-start.17 = (bf16[2,128,512]{2,1,0:T(8,128)(2,1)}, bf16[2,128,512]{2,1,0:T(8,128)(2,1)S(1)}, u32[]{:S(2)}, u32[]{:S(2)}) collective-permute-start(bf16[2,128,512]{2,1,0:T(8,128)(2,1)} %get-tuple-element.55), channel_id=1, source_target_pairs={{0,18},{1,19},{2,16},{3,17},{4,22},{5,23},{6,20},{7,21},{8,26},{9,... | collective-permute-start | bytes 786440 | tf_op jit(solution)/shard_map/ppermute | solution.py:451
  108.3 5.8 %collective-permute-done.19.refs_6_ = bf16[2,128,512]{2,1,0:T(8,128)(2,1)S(1)} collective-permute-done((bf16[2,128,512]{2,1,0:T(8,128)(2,1)S(1)}, bf16[2,128,512]{2,1,0:T(8,128)(2,1)S(1)}, u32[]{:S(2)}, u32[]{:S(2)}) %collective-permute-start.19) | collective-permute-done | bytes 262176 | tf_op jit(solution)/shard_map/ppermute | solution.py:451
  114.1 10.5 %dyson.2.refs_8_ = bf16[1,4,2,512,512]{4,3,2,1,0:T(8,128)(2,1)} custom-call(s32[16]{0:T(128)S(1)} %pad_add_fusion.row_ref, bf16[1,4,2,512,512]{4,3,2,1,0:T(8,128)(2,1)} %green_ref.3, bf16[512,512]{1,0:T(8,128)(2,1)S(1)} %copy-done.5, bf16[4,128,512]{2,1,0:T(8,128)(2,1)S(1)} %get-tuple-element.45.refs_6_.refs_0_, ...), custom_call_target="tpu_custom_call" | custom-call | flops 8589934592 | bytes 6815744 | tf_op jit(solution)/shard_map/dyson/pallas_call | solution.py:395
  124.7 10.5 %dyson.3 = bf16[1,4,2,512,512]{4,3,2,1,0:T(8,128)(2,1)} custom-call(s32[16]{0:T(128)S(1)} %pad_add_fusion.row_ref, bf16[1,4,2,512,512]{4,3,2,1,0:T(8,128)(2,1)} %green_ref.3, bf16[512,512]{1,0:T(8,128)(2,1)S(1)} %copy-done.5, bf16[4,128,512]{2,1,0:T(8,128)(2,1)S(1)} %get-tuple-element.45.refs_6_.refs_0_, ...), custom_call_target="tpu_custom_call", output_to_operand_aliasing={{}: (11, {})} | custom-call | flops 8589934592 | bytes 6815744 | tf_op jit(solution)/shard_map/dyson/pallas_call | solution.py:395
  (32 shorter events, 0.2 us)
Async XLA Ops:
  3.3 16.0 %collective-permute-start = (bf16[4,128,512]{2,1,0:T(8,128)(2,1)}, bf16[4,128,512]{2,1,0:T(8,128)(2,1)S(1)}, u32[]{:S(2)}, u32[]{:S(2)}) collective-permute-start(bf16[4,128,512]{2,1,0:T(8,128)(2,1)} %get-tuple-element.35), channel_id=1, source_target_pairs={{0,16},{1,17},{2,18},{3,19},{4,20},{5,21},{6,22},{7,23},{8,24},{9,... | collective-permute-start | bytes 1572872 | tf_op jit(solution)/shard_map/ppermute | solution.py:427
  6.3 26.4 %collective-permute-start.1 = (bf16[4,128,512]{2,1,0:T(8,128)(2,1)}, bf16[4,128,512]{2,1,0:T(8,128)(2,1)}, u32[]{:S(2)}, u32[]{:S(2)}) collective-permute-start(bf16[4,128,512]{2,1,0:T(8,128)(2,1)} %get-tuple-element.36), channel_id=1, source_target_pairs={{0,2},{1,3},{2,0},{3,1},{4,6},{5,7},{6,4},{7,5},{8,10},{9,11},{10,... | collective-permute-start | bytes 1572872 | tf_op jit(solution)/shard_map/ppermute | solution.py:427
  7.9 24.9 %collective-permute-start.2 = (bf16[4,128,512]{2,1,0:T(8,128)(2,1)}, bf16[4,128,512]{2,1,0:T(8,128)(2,1)}, u32[]{:S(2)}, u32[]{:S(2)}) collective-permute-start(bf16[4,128,512]{2,1,0:T(8,128)(2,1)} %get-tuple-element.37), channel_id=1, source_target_pairs={{0,18},{1,19},{2,16},{3,17},{4,22},{5,23},{6,20},{7,21},{8,26},{9,... | collective-permute-start | bytes 1572872 | tf_op jit(solution)/shard_map/ppermute | solution.py:427
  8.0 14.4 %copy-start.2 = (f32[2,2,16]{2,1,0:T(2,128)S(1)}, f32[2,2,16]{2,1,0:T(2,128)}, u32[]{:S(2)}) copy-start(f32[2,2,16]{2,1,0:T(2,128)} %coupling_ref.1) | copy-start | bytes 772
  8.0 14.4 %copy-start.3 = (s32[2,16]{1,0:T(2,128)S(1)}, s32[2,16]{1,0:T(2,128)}, u32[]{:S(2)}) copy-start(s32[2,16]{1,0:T(2,128)} %shift_ref.1) | copy-start | bytes 388
  8.0 14.4 %copy-start.4 = (s32[16]{0:T(128)S(1)}, s32[16]{0:T(128)}, u32[]{:S(2)}) copy-start(s32[16]{0:T(128)} %offset_ref.1) | copy-start | bytes 196
  11.0 0.8 copy-start.6
  11.8 30.0 %collective-permute-start.5 = (bf16[4,128,512]{2,1,0:T(8,128)(2,1)}, bf16[4,128,512]{2,1,0:T(8,128)(2,1)S(1)}, u32[]{:S(2)}, u32[]{:S(2)}) collective-permute-start(bf16[4,128,512]{2,1,0:T(8,128)(2,1)} %get-tuple-element.41), channel_id=1, source_target_pairs={{0,16},{1,17},{2,18},{3,19},{4,20},{5,21},{6,22},{7,23},{8,24},{9,... | collective-permute-start | bytes 1572872 | tf_op jit(solution)/shard_map/ppermute | solution.py:427
  13.8 39.9 %collective-permute-start.6 = (bf16[4,128,512]{2,1,0:T(8,128)(2,1)}, bf16[4,128,512]{2,1,0:T(8,128)(2,1)S(1)}, u32[]{:S(2)}, u32[]{:S(2)}) collective-permute-start(bf16[4,128,512]{2,1,0:T(8,128)(2,1)} %get-tuple-element.42), channel_id=1, source_target_pairs={{0,2},{1,3},{2,0},{3,1},{4,6},{5,7},{6,4},{7,5},{8,10},{9,11},{10,... | collective-permute-start | bytes 1572872 | tf_op jit(solution)/shard_map/ppermute | solution.py:427
  19.3 34.3 %collective-permute-start.7 = (bf16[4,128,512]{2,1,0:T(8,128)(2,1)}, bf16[4,128,512]{2,1,0:T(8,128)(2,1)S(1)}, u32[]{:S(2)}, u32[]{:S(2)}) collective-permute-start(bf16[4,128,512]{2,1,0:T(8,128)(2,1)} %copy-done.6), channel_id=1, source_target_pairs={{0,18},{1,19},{2,16},{3,17},{4,22},{5,23},{6,20},{7,21},{8,26},{9,... | collective-permute-start | bytes 1572872 | tf_op jit(solution)/shard_map/ppermute | solution.py:427
  23.7 35.7 %copy-start = (bf16[256,512]{1,0:T(8,128)(2,1)}, bf16[256,512]{1,0:T(8,128)(2,1)S(1)}, u32[]{:S(2)}) copy-start(bf16[256,512]{1,0:T(8,128)(2,1)S(1)} %get-tuple-element.40.mix_ref) | copy-start | bytes 786436
  34.0 21.2 %collective-permute-start.4 = (bf16[8,128,512]{2,1,0:T(8,128)(2,1)S(1)}, bf16[8,128,512]{2,1,0:T(8,128)(2,1)S(1)}, u32[]{:S(2)}, u32[]{:S(2)}) collective-permute-start(bf16[8,128,512]{2,1,0:T(8,128)(2,1)S(1)} %get-tuple-element.39), channel_id=1, source_target_pairs={{4,8},{5,9},{6,10},{7,11},{8,4},{9,5},{10,6},{11,7},{20,24},{21,25... | collective-permute-start | bytes 3145736 | tf_op jit(solution)/shard_map/ppermute | solution.py:434
  34.7 24.7 %collective-permute-start.3 = (bf16[8,128,512]{2,1,0:T(8,128)(2,1)S(1)}, bf16[8,128,512]{2,1,0:T(8,128)(2,1)S(1)}, u32[]{:S(2)}, u32[]{:S(2)}) collective-permute-start(bf16[8,128,512]{2,1,0:T(8,128)(2,1)S(1)} %get-tuple-element.38.refs_4_), channel_id=1, source_target_pairs={{0,4},{1,5},{2,6},{3,7},{4,0},{5,1},{6,2},{7,3},{8,12},{9,13},{10,... | collective-permute-start | bytes 3145736 | tf_op jit(solution)/shard_map/ppermute | solution.py:434
  61.9 7.0 %collective-permute-start.8 = (bf16[16,128,512]{2,1,0:T(8,128)(2,1)S(1)}, bf16[16,128,512]{2,1,0:T(8,128)(2,1)S(1)}, u32[]{:S(2)}, u32[]{:S(2)}) collective-permute-start(bf16[16,128,512]{2,1,0:T(8,128)(2,1)S(1)} %smooth.4.refs_6_), channel_id=1, source_target_pairs={{0,1},{1,0},{2,3},{3,2},{4,5},{5,4},{6,7},{7,6},{8,9},{9,8},{10,11... | collective-permute-start | bytes 6291464 | tf_op jit(solution)/shard_map/ppermute | solution.py:443
  62.0 12.0 %collective-permute-start.13 = (bf16[8,128,512]{2,1,0:T(8,128)(2,1)}, bf16[8,128,512]{2,1,0:T(8,128)(2,1)}, u32[]{:S(2)}, u32[]{:S(2)}) collective-permute-start(bf16[8,128,512]{2,1,0:T(8,128)(2,1)} %get-tuple-element.49), channel_id=1, source_target_pairs={{4,8},{5,9},{6,10},{7,11},{8,4},{9,5},{10,6},{11,7},{20,24},{21,25... | collective-permute-start | bytes 3145736 | tf_op jit(solution)/shard_map/ppermute | solution.py:434
  63.7 26.6 %collective-permute-start.12 = (bf16[8,128,512]{2,1,0:T(8,128)(2,1)}, bf16[8,128,512]{2,1,0:T(8,128)(2,1)}, u32[]{:S(2)}, u32[]{:S(2)}) collective-permute-start(bf16[8,128,512]{2,1,0:T(8,128)(2,1)} %get-tuple-element.44.refs_0_), channel_id=1, source_target_pairs={{0,4},{1,5},{2,6},{3,7},{4,0},{5,1},{6,2},{7,3},{8,12},{9,13},{10,... | collective-permute-start | bytes 3145736 | tf_op jit(solution)/shard_map/ppermute | solution.py:434
  68.9 21.4 %copy-start.1 = (bf16[256,512]{1,0:T(8,128)(2,1)S(1)}, bf16[256,512]{1,0:T(8,128)(2,1)}, u32[]{:S(2)}) copy-start(bf16[256,512]{1,0:T(8,128)(2,1)} %copy-done) | copy-start | bytes 786436
  70.4 25.5 %collective-permute-start.9 = (bf16[4,128,512]{2,1,0:T(8,128)(2,1)}, bf16[4,128,512]{2,1,0:T(8,128)(2,1)}, u32[]{:S(2)}, u32[]{:S(2)}) collective-permute-start(bf16[4,128,512]{2,1,0:T(8,128)(2,1)} %get-tuple-element.46), channel_id=1, source_target_pairs={{0,16},{1,17},{2,18},{3,19},{4,20},{5,21},{6,22},{7,23},{8,24},{9,... | collective-permute-start | bytes 1572872 | tf_op jit(solution)/shard_map/ppermute | solution.py:451
  71.9 25.0 %collective-permute-start.10 = (bf16[4,128,512]{2,1,0:T(8,128)(2,1)}, bf16[4,128,512]{2,1,0:T(8,128)(2,1)}, u32[]{:S(2)}, u32[]{:S(2)}) collective-permute-start(bf16[4,128,512]{2,1,0:T(8,128)(2,1)} %get-tuple-element.47), channel_id=1, source_target_pairs={{0,2},{1,3},{2,0},{3,1},{4,6},{5,7},{6,4},{7,5},{8,10},{9,11},{10,... | collective-permute-start | bytes 1572872 | tf_op jit(solution)/shard_map/ppermute | solution.py:451
  72.3 24.6 %collective-permute-start.11 = (bf16[4,128,512]{2,1,0:T(8,128)(2,1)}, bf16[4,128,512]{2,1,0:T(8,128)(2,1)}, u32[]{:S(2)}, u32[]{:S(2)}) collective-permute-start(bf16[4,128,512]{2,1,0:T(8,128)(2,1)} %get-tuple-element.48), channel_id=1, source_target_pairs={{0,18},{1,19},{2,16},{3,17},{4,22},{5,23},{6,20},{7,21},{8,26},{9,... | collective-permute-start | bytes 1572872 | tf_op jit(solution)/shard_map/ppermute | solution.py:451
  93.1 4.2 %collective-permute-start.14 = (bf16[16,128,512]{2,1,0:T(8,128)(2,1)S(1)}, bf16[16,128,512]{2,1,0:T(8,128)(2,1)S(1)}, u32[]{:S(2)}, u32[]{:S(2)}) collective-permute-start(bf16[16,128,512]{2,1,0:T(8,128)(2,1)S(1)} %smooth.6.refs_6_), channel_id=1, source_target_pairs={{0,1},{1,0},{2,3},{3,2},{4,5},{5,4},{6,7},{7,6},{8,9},{9,8},{10,11... | collective-permute-start | bytes 6291464 | tf_op jit(solution)/shard_map/ppermute | solution.py:443
  96.9 17.2 %copy-start.5 = (bf16[512,512]{1,0:T(8,128)(2,1)S(1)}, bf16[512,512]{1,0:T(8,128)(2,1)}, u32[]{:S(2)}) copy-start(bf16[512,512]{1,0:T(8,128)(2,1)} %phonon_ref.3) | copy-start | bytes 1572868
  97.8 9.2 %collective-permute-start.18 = (bf16[2,128,512]{2,1,0:T(8,128)(2,1)S(1)}, bf16[2,128,512]{2,1,0:T(8,128)(2,1)S(1)}, u32[]{:S(2)}, u32[]{:S(2)}) collective-permute-start(bf16[2,128,512]{2,1,0:T(8,128)(2,1)S(1)} %get-tuple-element.56), channel_id=1, source_target_pairs={{0,16},{1,17},{2,18},{3,19},{4,20},{5,21},{6,22},{7,23},{8,24},{9,... | collective-permute-start | bytes 786440 | tf_op jit(solution)/shard_map/ppermute | solution.py:451
  99.3 14.8 %collective-permute-start.19 = (bf16[2,128,512]{2,1,0:T(8,128)(2,1)S(1)}, bf16[2,128,512]{2,1,0:T(8,128)(2,1)S(1)}, u32[]{:S(2)}, u32[]{:S(2)}) collective-permute-start(bf16[2,128,512]{2,1,0:T(8,128)(2,1)S(1)} %get-tuple-element.57), channel_id=1, source_target_pairs={{0,2},{1,3},{2,0},{3,1},{4,6},{5,7},{6,4},{7,5},{8,10},{9,11},{10,... | collective-permute-start | bytes 786440 | tf_op jit(solution)/shard_map/ppermute | solution.py:451
  99.8 14.4 %collective-permute-start.20 = (bf16[2,128,512]{2,1,0:T(8,128)(2,1)S(1)}, bf16[2,128,512]{2,1,0:T(8,128)(2,1)S(1)}, u32[]{:S(2)}, u32[]{:S(2)}) collective-permute-start(bf16[2,128,512]{2,1,0:T(8,128)(2,1)S(1)} %get-tuple-element.58), channel_id=1, source_target_pairs={{0,18},{1,19},{2,16},{3,17},{4,22},{5,23},{6,20},{7,21},{8,26},{9,... | collective-permute-start | bytes 786440 | tf_op jit(solution)/shard_map/ppermute | solution.py:451
  102.4 22.2 %collective-permute-start.15 = (bf16[2,128,512]{2,1,0:T(8,128)(2,1)}, bf16[2,128,512]{2,1,0:T(8,128)(2,1)S(1)}, u32[]{:S(2)}, u32[]{:S(2)}) collective-permute-start(bf16[2,128,512]{2,1,0:T(8,128)(2,1)} %get-tuple-element.53), channel_id=1, source_target_pairs={{0,16},{1,17},{2,18},{3,19},{4,20},{5,21},{6,22},{7,23},{8,24},{9,... | collective-permute-start | bytes 786440 | tf_op jit(solution)/shard_map/ppermute | solution.py:451
  104.0 20.7 %collective-permute-start.16 = (bf16[2,128,512]{2,1,0:T(8,128)(2,1)}, bf16[2,128,512]{2,1,0:T(8,128)(2,1)S(1)}, u32[]{:S(2)}, u32[]{:S(2)}) collective-permute-start(bf16[2,128,512]{2,1,0:T(8,128)(2,1)} %get-tuple-element.54), channel_id=1, source_target_pairs={{0,2},{1,3},{2,0},{3,1},{4,6},{5,7},{6,4},{7,5},{8,10},{9,11},{10,... | collective-permute-start | bytes 786440 | tf_op jit(solution)/shard_map/ppermute | solution.py:451
  107.0 17.7 %copy-start.7 = (bf16[2,128,512]{2,1,0:T(8,128)(2,1)S(1)}, bf16[2,128,512]{2,1,0:T(8,128)(2,1)}, u32[]{:S(2)}) copy-start(bf16[2,128,512]{2,1,0:T(8,128)(2,1)} %get-tuple-element.52.refs_4_) | copy-start | bytes 786436
  107.0 17.7 %collective-permute-start.17 = (bf16[2,128,512]{2,1,0:T(8,128)(2,1)}, bf16[2,128,512]{2,1,0:T(8,128)(2,1)S(1)}, u32[]{:S(2)}, u32[]{:S(2)}) collective-permute-start(bf16[2,128,512]{2,1,0:T(8,128)(2,1)} %get-tuple-element.55), channel_id=1, source_target_pairs={{0,18},{1,19},{2,16},{3,17},{4,22},{5,23},{6,20},{7,21},{8,26},{9,... | collective-permute-start | bytes 786440 | tf_op jit(solution)/shard_map/ppermute | solution.py:451
